TPU v7x, 128 devices: a whole 4x4x4 slice. The times are simulated.
128 devices in a mesh: layer: 4 (over x_lo, core), fsdp: 32 (over x_hi, y, z).
Axes of the slice: x: 4 (x_hi: 2, x_lo: 2; x = x_hi * 2 + x_lo), y: 4, z: 4, core: 2. Of those that a mesh axis runs over, the one named last changes fastest.
Arguments:
- gradient: bfloat16 [4, 1536, 4608], P(None, ('layer', 'fsdp')), may hold values from -6 to 6
- eigenbasis: float32 [4, 4608, 4608], P('layer', 'fsdp'), may hold values from -0.09375 to 0.09375
- gram_sum: float32 [4, 4608, 4608], P('layer', 'fsdp'), may hold values from -6 to 6
- first_moment: float32 [4, 1536, 4608], P('layer', None, 'fsdp'), may hold values from -3 to 3
- second_moment: float32 [4, 1536, 4608], P('layer', None, 'fsdp'), may hold values from 0.1 to 4
Outputs:
- update: bfloat16 [4, 1536, 4608], P(None, ('layer', 'fsdp'))
- new_gram: float32 [4, 4608, 4608], P('layer', 'fsdp')
- new_first: float32 [4, 1536, 4608], P('layer', None, 'fsdp')
- new_second: float32 [4, 1536, 4608], P('layer', None, 'fsdp')
All inputs are finite; a program needn't handle non-finite values.
Results may differ from a plain program's by a relative error of at most 0.0058.
Values may be sent and summed in bfloat16 or wider, within the bound.
No kernel may reach another device: no remote copies, remote signals or barrier semaphores. Data moves between devices by JAX's collectives and lax.ppermute only.
A program may use at most 192 MiB of HBM per device.

v0:
```python
import jax
import jax.numpy as jnp
from jax import lax
from jax.sharding import PartitionSpec as P

bias_fix = 1.0 - 0.95**10


def body(gradient, eigenbasis, gram_sum, first_moment, second_moment):
    layer_count = lax.axis_size("layer")
    fsdp_count = lax.axis_size("fsdp")
    row_block = gradient.shape[1]
    model_width = gradient.shape[2]
    span_size = eigenbasis.shape[1]
    first_col = lax.axis_index("fsdp") * span_size
    basis_half = eigenbasis[0].astype(jnp.bfloat16)
    owned = lax.all_to_all(gradient, "layer", split_axis=0, concat_axis=0, tiled=True)
    gathered = lax.all_gather(owned, "fsdp", axis=1, tiled=True)
    flat_rows = gathered.reshape(-1, model_width)
    rotated = lax.dot_general(
        flat_rows, basis_half, (((1,), (1,)), ((), ())), preferred_element_type=jnp.float32
    )
    own_cols = lax.dynamic_slice_in_dim(flat_rows, first_col, span_size, 1)
    product = lax.dot_general(
        own_cols, flat_rows, (((0,), (0,)), ((), ())), preferred_element_type=jnp.float32
    )
    new_gram = (0.95 * gram_sum[0] + 0.05 * product)[None]
    new_first = 0.95 * first_moment[0] + 0.05 * rotated
    new_second = 0.95 * second_moment[0] + 0.05 * rotated * rotated
    direction = (new_first / bias_fix / (jnp.sqrt(new_second / bias_fix) + 1e-08)).astype(
        jnp.bfloat16
    )
    reordered = direction.reshape(layer_count, fsdp_count, row_block, span_size)
    reordered = reordered.transpose(1, 0, 2, 3).reshape(-1, span_size)
    summed = lax.psum_scatter(
        jnp.dot(reordered, basis_half, preferred_element_type=jnp.float32),
        "fsdp",
        scatter_dimension=0,
        tiled=True,
    )
    update_rows = summed.astype(jnp.bfloat16).reshape(layer_count, row_block, model_width)
    update = lax.all_to_all(update_rows, "layer", split_axis=0, concat_axis=0, tiled=True)
    return (update, new_gram, new_first[None], new_second[None])


def solution(mesh):
    return jax.shard_map(
        body,
        mesh=mesh,
        in_specs=(
            P(None, ("layer", "fsdp"), None),
            P("layer", "fsdp", None),
            P("layer", "fsdp", None),
            P("layer", None, "fsdp"),
            P("layer", None, "fsdp"),
        ),
        out_specs=(
            P(None, ("layer", "fsdp"), None),
            P("layer", "fsdp", None),
            P("layer", None, "fsdp"),
            P("layer", None, "fsdp"),
        ),
        check_vma=False,
    )
```

profile of v0, /device:TPU:1, one launch (start us, length us, event | category | flops | bytes accessed | tf_op | source)
XLA Modules:
  0.0 536.3 jit_solution(17488483789820508786)
XLA Ops:
  7.2 0.0 all-gather.2.cloned.1.call-start
  7.2 1.1 copy.18
  8.3 12.9 %all_to_all.10 = bf16[4,12,4608]{2,1,0:T(8,128)(2,1)S(1)} all-to-all(bf16[4,12,4608]{2,1,0:T(8,128)(2,1)S(1)} %copy.18), channel_id=1, replica_groups=mesh['layer'=4,'fsdp'=32] {'layer'}, dimensions={0} | all-to-all | bytes 884736 | tf_op jit(solution)/shard_map/all_to_all | solution.py:17
  21.2 1.1 copy.19
  22.3 0.0 all-gather.2.cloned.1.call-update
  22.3 0.0 copy-start.2
  22.3 0.0 reduce-scatter.2.cloned.1.call-start
  22.4 142.2 %all-gather.2.cloned.1.call-done = bf16[4,384,4608]{2,0,1:T(4,128)(2,1)} async-done(((bf16[4,12,4608]{2,0,1:T(4,128)(2,1)}), bf16[4,384,4608]{2,0,1:T(4,128)(2,1)}) %all-gather.2.cloned.1.call-update) | async-done | bytes 14155792 | tf_op jit(solution)/shard_map/all_gather | solution.py:18
  164.5 9.5 %copy.20 = bf16[4,384,4608]{2,1,0:T(8,128)(2,1)S(1)} copy(bf16[4,384,4608]{2,0,1:T(4,128)(2,1)} %all-gather.2.cloned.1.call-done) | data formatting | bytes 28311552 | tf_op jit(solution)/shard_map/all_gather | solution.py:18
  174.1 0.0 copy-start
  174.1 0.0 copy-done.2
  174.1 9.0 %fusion.11 = (f32[1,1536,144]{1,2,0:T(8,128)}, bf16[1536,144]{0,1:T(8,128)(2,1)S(1)}, f32[1,1536,144]{1,2,0:T(8,128)}) fusion(f32[1,1536,144]{1,2,0:T(8,128)} %param.9, f32[1,1536,144]{1,2,0:T(8,128)} %param.8, bf16[1536,4608]{1,0:T(8,128)(2,1)S(1)} %bitcast.32, f32[1,144,4608]{2,1,0:T(8,128)S(1)} %copy-done.2), kind=kOutput, calls=%fused_computation.15 | convolution fusion | flops 2041528320 | bytes 20791296 | tf_op jit(solution)/shard_map/dot_general | solution.py:20
  183.1 0.0 copy-done
  183.1 0.3 copy.21
  183.4 0.2 reshape.29
  183.6 0.1 copy.22
  183.8 0.4 reshape.30
  184.2 13.1 %fusion.2 = f32[1536,4608]{1,0:T(8,128)} fusion(bf16[1536,144]{1,0:T(8,128)(2,1)S(1)} %reshape.30, f32[1,144,4608]{2,1,0:T(8,128)} %param.6), kind=kOutput, calls=%fused_computation.3 | convolution fusion | flops 2039095296 | bytes 31408128 | tf_op jit(solution)/shard_map/dot_general | solution.py:36
  197.3 0.0 reduce-scatter.2.cloned.1.call-update
  197.3 0.0 copy-start.1
  197.4 313.7 %reduce-scatter.2.cloned.1.call-done = f32[48,4608]{1,0:T(8,128)} async-done(((f32[1536,4608]{1,0:T(8,128)}), f32[48,4608]{1,0:T(8,128)}) %reduce-scatter.2.cloned.1.call-update) | async-done | bytes 884752 | tf_op jit(solution)/shard_map/reduce_scatter | solution.py:35
  511.1 1.2 convert_element_type.16
  512.3 0.9 reshape.31
  513.2 5.7 %all-to-all-start.1 = ((bf16[4,12,4608]{2,1,0:T(8,128)(2,1)}), bf16[4,12,4608]{2,1,0:T(8,128)(2,1)S(1)}, u32[]{:S(2)}, u32[]{:S(2)}) async-start(bf16[4,12,4608]{2,1,0:T(8,128)(2,1)} %reshape.31), calls=%async_computation.2 | async-start | bytes 1179648 | tf_op jit(solution)/shard_map/all_to_all | solution.py:42
  518.9 0.0 copy-done.1
  518.9 9.4 %fusion.1 = f32[1,144,4608]{2,1,0:T(8,128)} fusion(bf16[1536,4608]{1,0:T(8,128)(2,1)} %bitcast.33, f32[1,144,4608]{2,1,0:T(8,128)S(1)} %copy-done.1, s32[]{:T(128)S(6)} %select_n.3), kind=kOutput, calls=%fused_computation.2 | convolution fusion | flops 2040422400 | bytes 20250628 | tf_op jit(solution)/shard_map/dot_general | solution.py:24
  528.4 0.0 all-to-all-done.1
  528.4 1.1 copy.23
Async XLA Ops:
  7.2 157.4 %all-gather.2.cloned.1.call-start = ((), (), s32[]{:S(2)}) async-start(), calls=%async_computation.3 | async-start | bytes 14598144 | tf_op jit(solution)/shard_map/all_gather | solution.py:18
  22.3 151.8 %copy-start.2 = (f32[1,144,4608]{2,1,0:T(8,128)S(1)}, f32[1,144,4608]{2,1,0:T(8,128)}, u32[]{:S(2)}) copy-start(f32[1,144,4608]{2,1,0:T(8,128)} %param.6) | copy-start | bytes 7962628
  22.3 488.7 %reduce-scatter.2.cloned.1.call-start = ((), (), s32[]{:S(2)}) async-start(), calls=%async_computation.4 | async-start | bytes 29196288 | tf_op jit(solution)/shard_map/reduce_scatter | solution.py:35
  174.1 9.1 %copy-start = (bf16[4,384,4608]{2,1,0:T(8,128)(2,1)}, bf16[4,384,4608]{2,1,0:T(8,128)(2,1)S(1)}, u32[]{:S(2)}) copy-start(bf16[4,384,4608]{2,1,0:T(8,128)(2,1)S(1)} %copy.20) | copy-start | bytes 42467332
  197.3 321.6 %copy-start.1 = (f32[1,144,4608]{2,1,0:T(8,128)S(1)}, f32[1,144,4608]{2,1,0:T(8,128)}, u32[]{:S(2)}) copy-start(f32[1,144,4608]{2,1,0:T(8,128)} %param.7) | copy-start | bytes 7962628
  513.2 15.2 %all-to-all-start.1 = ((bf16[4,12,4608]{2,1,0:T(8,128)(2,1)}), bf16[4,12,4608]{2,1,0:T(8,128)(2,1)S(1)}, u32[]{:S(2)}, u32[]{:S(2)}) async-start(bf16[4,12,4608]{2,1,0:T(8,128)(2,1)} %reshape.31), calls=%async_computation.2 | async-start | bytes 1179648 | tf_op jit(solution)/shard_map/all_to_all | solution.py:42
Sparse Core Ops, SparseCore 0:
  22.4 142.0 all-gather.1
  197.5 313.5 reduce-scatter.1
where the time goes:
time: 537 us; the launch traced here: 536 us
  waiting for transfers between devices  456 us (85%)
  matrix products  31.6 us (6%)
  local copies, waits for them, and re-layouts  14.8 us (3%)
  between operations  14.1 us (3%)
  blocking collectives  12.9 us (2%)
  starting transfers between devices  5.8 us (1%)
    reduce_scatter x1, waiting for transfers between devices, body(): lax.psum_scatter(jnp.dot(reordered, basis_half, preferred_element_type=jn...  314 us
    all_gather x1, waiting for transfers between devices, body(): gathered = lax.all_gather(owned, 'fsdp', axis=1, tiled=True)  142 us
    dot_general x1, matrix products, body(): jnp.dot(reordered, basis_half, preferred_element_type=jnp.float32)  13.1 us
    all_to_all x1, blocking collectives, body(): lax.all_to_all(gradient, 'layer', split_axis=0, concat_axis=0, tiled=True)  12.9 us
  transfers between devices with their start and end apart: 3, of which 2 were waited for; matrix products, arithmetic and copies ran while one was open for 2% of the time, Pallas kernels for 0%

commit v1 on v0

v1 whole, which is shorter than its diff:
```python
import jax
import jax.numpy as jnp
from jax import lax
from jax.sharding import Mesh, PartitionSpec as P

bias_fix = 1.0 - 0.95**10
half = jnp.bfloat16
AXES = ("xl", "core", "xh", "y", "z")
OFFSETS = (0, -1, 1, 2)


def shift(value, axis, step):
    size = lax.axis_size(axis)
    return lax.ppermute(value, axis, [(i, (i + step) % size) for i in range(size)])


def shift_x(value, step):
    place = [(x % 2) * 2 + x // 2 for x in range(4)]
    return lax.ppermute(value, ("xl", "xh"), [(place[x], place[(x + step) % 4]) for x in range(4)])


def ring_gather(value, axis):
    cut = value.shape[0] // 2
    before = shift(value, axis, 1)
    after = shift(value, axis, -1)
    far_top = shift(before[:cut], axis, 1)
    far_low = shift(after[cut:], axis, -1)
    return jnp.concatenate([value, before, after, far_top, far_low], 0)


def ring_sum(blocks, axis):
    mine, to_before, to_after, far = blocks
    cut = mine.shape[0] // 2
    far = far.astype(half)
    top = shift(far[:cut], axis, 1)
    low = shift(far[cut:], axis, -1)
    up = jnp.concatenate([to_after[:cut] + top.astype(jnp.float32), to_after[cut:]], 0)
    down = jnp.concatenate([to_before[:cut], to_before[cut:] + low.astype(jnp.float32)], 0)
    up = shift(up.astype(half), axis, 1)
    down = shift(down.astype(half), axis, -1)
    return mine + up.astype(jnp.float32) + down.astype(jnp.float32)


def body(gradient, eigenbasis, gram_sum, first_moment, second_moment):
    rows = gradient.shape[1]
    width = gradient.shape[2]
    span = eigenbasis.shape[1]
    total = first_moment.shape[1]
    xl, core, xh, y, z = (lax.axis_index(a) for a in AXES)

    def pick(pair, index):
        return jnp.where(index == 0, pair[0], pair[1])

    pairs = gradient.reshape(2, 2, rows, width)
    keep = pick((pairs[:, 0], pairs[:, 1]), core)
    other = shift(pick((pairs[:, 1], pairs[:, 0]), core), "core", 1)
    chip = jnp.concatenate([keep, other], 1)
    own_layer = pick((chip[0], chip[1]), xl)
    next_layer = pick((chip[1], chip[0]), xl)
    line = jnp.concatenate(
        [own_layer, shift_x(next_layer, 1), shift_x(next_layer, -1), shift(own_layer, "xh", 1)], 0
    )
    grads = ring_gather(line, "y")
    count = grads.shape[0]

    basis = ring_gather(eigenbasis[0].astype(half), "z")

    at = lax.broadcasted_iota(jnp.int32, (1, 4 * count), 1)

    def offset(index):
        return jnp.where(index == 0, 0, jnp.where(index == 1, -1, index - 1))

    row = at % rows
    core_of = (core + at // rows) % 2
    x_of = (2 * xh + xl + offset(at // (2 * rows) % 4) + 4) % 4
    y_of = (y + offset(at // (8 * rows) % 4) + 4) % 4
    z_of = (z + offset(at // (32 * rows)) + 4) % 4
    number = ((((x_of % 2 * 2 + core_of) * 2 + x_of // 2) * 4 + y_of) * 4 + z_of) * rows + row
    order = (lax.broadcasted_iota(jnp.int32, (total, 4 * count), 0) == number).astype(half)

    first = first_moment[0].T
    second = second_moment[0].T
    first_high = first.astype(half)
    first_low = (first - first_high.astype(jnp.float32)).astype(half)
    moments = jnp.concatenate([first_high, first_low, second.astype(half)], 0)
    moments = jnp.dot(moments, order, preferred_element_type=jnp.float32).astype(half)
    moments = moments.reshape(3, span, 4, count)
    moved = [moments[:, :, 0]]
    for k, step in ((1, 1), (2, -1), (3, 2)):
        moved.append(shift(moments[:, :, (0, 2, 1, 3)[k]], "z", step))
    moved = jnp.concatenate(moved, 1).astype(jnp.float32)

    rotated = lax.dot_general(
        basis, grads, (((1,), (1,)), ((), ())), preferred_element_type=jnp.float32
    )
    new_first = 0.95 * (moved[0] + moved[1]) + 0.05 * rotated
    new_second = 0.95 * moved[2] + 0.05 * rotated * rotated
    direction = (new_first / bias_fix / (jnp.sqrt(new_second / bias_fix) + 1e-08)).astype(half)

    step_rows = count // 4
    terms = [
        lax.dot_general(
            direction[:, k * step_rows : (k + 1) * step_rows],
            basis,
            (((0,), (0,)), ((), ())),
            preferred_element_type=jnp.float32,
        )
        for k in range(4)
    ]
    summed = ring_sum(terms, "y").reshape(4, 2 * rows, width)
    sent = summed.astype(half)
    far = shift(sent[3], "xh", 1)
    left = shift_x(sent[1], -1)
    right = shift_x(sent[2], 1)
    own_update = (summed[0] + far.astype(jnp.float32)).astype(half)
    next_update = (left.astype(jnp.float32) + right.astype(jnp.float32)).astype(half)
    update = jnp.stack([pick((own_update, next_update), xl), pick((next_update, own_update), xl)])
    given = shift(update[:, rows:], "core", 1)
    update = update[:, :rows]
    update = jnp.stack([pick((update, given), core), pick((given, update), core)], 1)
    update = update.reshape(4, rows, width)

    terms = []
    for k in range(4):
        column = ((xh * 4 + y) * 4 + (z + OFFSETS[k] + 4) % 4) * span
        columns = lax.dynamic_slice_in_dim(grads, column, span, 1)
        terms.append(
            lax.dot_general(
                columns, grads, (((0,), (0,)), ((), ())), preferred_element_type=jnp.float32
            )
        )
    new_gram = 0.95 * gram_sum[0] + 0.05 * ring_sum(terms, "z")

    blocks = rotated.astype(half).reshape(4, span, count)
    owned = [blocks[0]]
    for k, step in ((1, 1), (2, -1), (3, 2)):
        owned.append(shift(blocks[(0, 2, 1, 3)[k]], "z", step))
    owned = lax.dot_general(
        jnp.concatenate(owned, 1), order, (((1,), (1,)), ((), ())), preferred_element_type=jnp.float32
    )
    out_first = 0.95 * first + 0.05 * owned
    out_second = 0.95 * second + 0.05 * owned * owned
    return (update, new_gram[None], out_first.T[None], out_second.T[None])


def solution(mesh):
    fine = Mesh(mesh.devices.reshape(2, 2, 2, 4, 4), AXES)
    layer, fsdp = ("xl", "core"), ("xh", "y", "z")
    return jax.shard_map(
        body,
        mesh=fine,
        in_specs=(
            P(None, AXES, None),
            P(layer, fsdp, None),
            P(layer, fsdp, None),
            P(layer, None, fsdp),
            P(layer, None, fsdp),
        ),
        out_specs=(
            P(None, AXES, None),
            P(layer, fsdp, None),
            P(layer, None, fsdp),
            P(layer, None, fsdp),
        ),
        check_vma=False,
    )
```

time: 537 us -> 168 us (0.31)
  the two profiles are of different devices: /device:TPU:1 before, /device:TPU:16 now
where the time goes in v1:
time: 168 us
  waiting for transfers between devices  75.7 us (45%)
  starting transfers between devices  43.8 us (26%)
  matrix products  19.8 us (12%)
  local copies, waits for them, and re-layouts  16.4 us (10%)
  other arithmetic  11.1 us (7%)
    ppermute x26, waiting for transfers between devices, shift(): lax.ppermute(value, axis, [(i, (i + step) % size) for i in range(size)])  74.1 us
    ppermute x26, starting transfers between devices, shift(): lax.ppermute(value, axis, [(i, (i + step) % size) for i in range(size)])  36.8 us
    unnamed x31, local copies, waits for them, and re-layouts  10 us
    ppermute x4, starting transfers between devices, shift_x(): lax.ppermute(value, ('xl', 'xh'), [(place[x], place[(x + step) % 4]) for...  6.99 us
    dot_general x4, matrix products, body(): lax.dot_general(columns, grads, (((0,), (0,)), ((), ())), preferred_eleme...  5.82 us
    dot_general x4, matrix products, body(): lax.dot_general(direction[:, k * step_rows:(k + 1) * step_rows], basis, (...  4.93 us
    select_n x3, other arithmetic, pick(): return jnp.where(index == 0, pair[0], pair[1])  3.51 us
    unnamed x1, other arithmetic  3.45 us
  transfers between devices with their start and end apart: 30, of which 12 were waited for; matrix products, arithmetic and copies ran while one was open for 25% of the time, Pallas kernels for 0%

profile of v1, /device:TPU:16, one launch (start us, length us, event | category | flops | bytes accessed | tf_op | source)
XLA Modules:
  0.0 167.9 jit_solution(3450391740991462046)
XLA Ops:
  0.7 1.3 reshape.357
  2.0 1.8 %broadcast_select_fusion.1 = (bf16[2,1,12,4608]{3,1,0,2:T(2,128)(2,1)}, bf16[2,1,12,4608]{3,1,0,2:T(2,128)(2,1)S(1)}) fusion(pred[]{:T(512)S(6)} %eq.82, bf16[2,2,12,4608]{3,1,0,2:T(2,128)(2,1)S(1)} %reshape.357), kind=kLoop, calls=%fused_computation.63 | loop fusion | flops 221184 | bytes 884737 | tf_op jit(solution)/shard_map/jit(_where)/select_n | solution.py:52
  4.9 2.3 %fusion.9 = bf16[432,1536]{1,0:T(8,128)(2,1)S(1)} fusion(s32[1536]{0:T(1024)S(1)} %fusion.70, bf16[144,1536]{1,0:T(8,128)(2,1)S(1)} %convert_bitcast_fusion.1, bf16[144,1536]{1,0:T(8,128)(2,1)S(1)} %get-tuple-element.4, bf16[144,1536]{1,0:T(8,128)(2,1)S(1)} %get-tuple-element.5), kind=kOutput, calls=%fused_computation.14 | convolution fusion | flops 2045435904 | bytes 2660352 | tf_op jit(solution)/shard_map/dot_general | solution.py:86
  7.6 2.7 %fusion.93 = (bf16[3,144,1,384]{3,2,1,0:T(2,128)(2,1)}, bf16[3,144,1,384]{3,2,1,0:T(2,128)(2,1)S(1)}, bf16[3,144,1,384]{3,2,1,0:T(2,128)(2,1)S(1)}, bf16[3,144,1,384]{3,2,1,0:T(2,128)(2,1)S(1)}) fusion(bf16[3,144,4,384]{3,2,1,0:T(4,128)(2,1)S(1)} %reshape.356), kind=kLoop, calls=%fused_computation.198 | loop fusion | bytes 2654208 | tf_op jit(solution)/shard_map/slice | solution.py:88
  11.0 3.9 %collective-permute-start.2 = (bf16[3,144,384]{2,1,0:T(8,128)(2,1)}, bf16[3,144,384]{2,1,0:T(8,128)(2,1)}, u32[]{:S(2)}, u32[]{:S(2)}) collective-permute-start(bf16[3,144,384]{2,1,0:T(8,128)(2,1)} %bitcast.79), channel_id=1, source_target_pairs={{0,2},{1,3},{2,0},{3,1},{4,6},{5,7},{6,4},{7,5},{8,10},{9,11},{10,... | collective-permute-start | bytes 995336 | tf_op jit(solution)/shard_map/ppermute | solution.py:14
  17.1 1.3 collective-permute-start
  20.3 1.5 collective-permute-start.8
  21.8 1.7 %collective-permute-start.9 = (bf16[24,4608]{1,0:T(8,128)(2,1)}, bf16[24,4608]{1,0:T(8,128)(2,1)}, u32[]{:S(2)}, u32[]{:S(2)}) collective-permute-start(bf16[24,4608]{1,0:T(8,128)(2,1)} %bitcast.83), channel_id=1, source_target_pairs={{0,80},{64,0},{16,64},{80,16},{1,81},{65,1},{17,65},{81,17},{2,82}... | collective-permute-start | bytes 663560 | tf_op jit(solution)/shard_map/ppermute | solution.py:19
  25.1 1.8 %collective-permute-start.10 = (bf16[24,4608]{1,0:T(8,128)(2,1)}, bf16[24,4608]{1,0:T(8,128)(2,1)}, u32[]{:S(2)}, u32[]{:S(2)}) collective-permute-start(bf16[24,4608]{1,0:T(8,128)(2,1)} %get-tuple-element.9), channel_id=1, source_target_pairs={{0,16},{16,0},{1,17},{17,1},{2,18},{18,2},{3,19},{19,3},{4,20},{20... | collective-permute-start | bytes 663560 | tf_op jit(solution)/shard_map/ppermute | solution.py:14
  26.9 3.5 %constant_dynamic-update-slice_fusion.4 = (bf16[576,4608]{1,0:T(8,128)(2,1)}, bf16[144,4608]{1,0:T(8,128)(2,1)}) fusion(f32[1,144,4608]{2,1,0:T(8,128)} %param.6), kind=kLoop, calls=%fused_computation.112 | loop fusion | flops 663551 | bytes 5308416
  30.4 1.9 %copy.56 = bf16[3,144,1,384]{3,1,0,2:T(8,128)(2,1)} copy(bf16[3,144,1,384]{3,2,1,0:T(2,128)(2,1)} %get-tuple-element.16) | data formatting | bytes 663552
  32.2 1.5 collective-permute-start.3
  33.7 2.2 %collective-permute-start.4 = (bf16[144,4608]{1,0:T(8,128)(2,1)}, bf16[144,4608]{1,0:T(8,128)(2,1)S(1)}, u32[]{:S(2)}, u32[]{:S(2)}) collective-permute-start(bf16[144,4608]{1,0:T(8,128)(2,1)} %get-tuple-element.11), channel_id=1, source_target_pairs={{0,3},{1,0},{2,1},{3,2},{4,7},{5,4},{6,5},{7,6},{8,11},{9,8},{10,9... | collective-permute-start | bytes 3981320 | tf_op jit(solution)/shard_map/ppermute | solution.py:14
  35.9 1.4 maximum_convert_fusion
  37.4 1.5 pad_maximum_fusion.2
  38.9 1.4 collective-permute-start.11
  41.0 0.9 constant_dynamic-update-slice_fusion.11
  41.9 1.0 constant_dynamic-update-slice_fusion.10
  42.9 1.0 constant_dynamic-update-slice_fusion.9
  43.8 20.6 %collective-permute-done.3 = bf16[144,4608]{1,0:T(8,128)(2,1)S(1)} collective-permute-done((bf16[144,4608]{1,0:T(8,128)(2,1)}, bf16[144,4608]{1,0:T(8,128)(2,1)S(1)}, u32[]{:S(2)}, u32[]{:S(2)}) %collective-permute-start.3) | collective-permute-done | bytes 1327136 | tf_op jit(solution)/shard_map/ppermute | solution.py:14
  64.8 3.3 %collective-permute-start.6 = (bf16[72,4608]{1,0:T(8,128)(2,1)S(1)}, bf16[72,4608]{1,0:T(8,128)(2,1)S(1)}, u32[]{:S(2)}, u32[]{:S(2)}) collective-permute-start(bf16[72,4608]{1,0:T(8,128)(2,1)S(1)} %slice.187), channel_id=1, source_target_pairs={{0,3},{1,0},{2,1},{3,2},{4,7},{5,4},{6,5},{7,6},{8,11},{9,8},{10,9... | collective-permute-start | bytes 1990664 | tf_op jit(solution)/shard_map/ppermute | solution.py:14
  68.3 1.4 collective-permute-start.13
  70.6 7.7 %collective-permute-done.13 = bf16[48,4608]{1,0:T(8,128)(2,1)S(1)} collective-permute-done((bf16[48,4608]{1,0:T(8,128)(2,1)S(1)}, bf16[48,4608]{1,0:T(8,128)(2,1)S(1)}, u32[]{:S(2)}, u32[]{:S(2)}) %collective-permute-start.13) | collective-permute-done | bytes 442400 | tf_op jit(solution)/shard_map/ppermute | solution.py:14
  78.4 1.1 collective-permute-done.14
  79.5 1.0 convolution_convert_fusion
  80.9 1.0 fusion.42
  81.9 1.0 fusion.45
  83.5 3.4 %fusion.94 = (bf16[576,384]{1,0:T(8,128)(2,1)S(1)}, bf16[576,384]{1,0:T(8,128)(2,1)S(1)}) fusion(f32[3,576,384]{2,1,0:T(8,128)S(1)} %maximum_convert_fusion, bf16[576,4608]{1,0:T(8,128)(2,1)S(1)} %constant_dynamic-update-slice_fusion, bf16[384,4608]{1,0:T(8,128)(2,1)S(1)} %constant_dynamic-update-slice_fusion.5), kind=kOutput, calls=%fused_computation.199 | convolution fusion | flops 2041307136 | bytes 12386304 | tf_op jit(solution)/shard_map/dot_general | solution.py:93
  86.9 1.2 fusion.48
  88.1 1.2 convolution_convert_fusion.1
  89.9 2.0 %collective-permute-start.29 = (bf16[144,384]{1,0:T(8,128)(2,1)S(1)}, bf16[144,384]{1,0:T(8,128)(2,1)S(1)}, u32[]{:S(2)}, u32[]{:S(2)}) collective-permute-start(bf16[144,384]{1,0:T(8,128)(2,1)S(1)} %get-tuple-element.32), channel_id=1, source_target_pairs={{0,2},{1,3},{2,0},{3,1},{4,6},{5,7},{6,4},{7,5},{8,10},{9,11},{10,... | collective-permute-start | bytes 331784 | tf_op jit(solution)/shard_map/ppermute | solution.py:14
  92.0 2.4 %collective-permute-start.28 = (bf16[144,384]{1,0:T(8,128)(2,1)S(1)}, bf16[144,384]{1,0:T(8,128)(2,1)S(1)}, u32[]{:S(2)}, u32[]{:S(2)}) collective-permute-start(bf16[144,384]{1,0:T(8,128)(2,1)S(1)} %get-tuple-element.33), channel_id=1, source_target_pairs={{0,3},{1,0},{2,1},{3,2},{4,7},{5,4},{6,5},{7,6},{8,11},{9,8},{10,9... | collective-permute-start | bytes 331784 | tf_op jit(solution)/shard_map/ppermute | solution.py:14
  94.4 1.2 fusion.51
  96.3 3.8 %collective-permute-start.23 = (bf16[72,4608]{1,0:T(8,128)(2,1)S(1)}, bf16[72,4608]{1,0:T(8,128)(2,1)S(1)}, u32[]{:S(2)}, u32[]{:S(2)}) collective-permute-start(bf16[72,4608]{1,0:T(8,128)(2,1)S(1)} %get-tuple-element.14), channel_id=1, source_target_pairs={{0,1},{1,2},{2,3},{3,0},{4,5},{5,6},{6,7},{7,4},{8,9},{9,10},{10,1... | collective-permute-start | bytes 1990664 | tf_op jit(solution)/shard_map/ppermute | solution.py:14
  100.1 1.3 collective-permute-start.15
  101.6 3.4 %fusion.25 = (f32[1,1536,144]{1,2,0:T(8,128)}, f32[1,1536,144]{1,2,0:T(8,128)}) fusion(f32[1,1536,144]{1,2,0:T(8,128)S(1)} %copy-done.6, f32[1,1536,144]{1,2,0:T(8,128)S(1)} %copy-done.4, bf16[144,384]{1,0:T(8,128)(2,1)S(1)} %collective-permute-done.29, bf16[144,384]{1,0:T(8,128)(2,1)S(1)} %collective-permute-done.28, ...), kind=kOutput, calls=%fused_computation.42 | convolution fusion | flops 684933120 | bytes 3987456 | tf_op jit(solution)/shard_map/dot_general | solution.py:138
  105.8 5.1 %collective-permute-done.15 = bf16[48,4608]{1,0:T(8,128)(2,1)S(1)} collective-permute-done((bf16[48,4608]{1,0:T(8,128)(2,1)S(1)}, bf16[48,4608]{1,0:T(8,128)(2,1)S(1)}, u32[]{:S(2)}, u32[]{:S(2)}) %collective-permute-start.15) | collective-permute-done | bytes 442400 | tf_op jit(solution)/shard_map/ppermute | solution.py:14
  112.1 3.0 %collective-permute-start.26 = (bf16[144,4608]{1,0:T(8,128)(2,1)S(1)}, bf16[144,4608]{1,0:T(8,128)(2,1)S(1)}, u32[]{:S(2)}, u32[]{:S(2)}) collective-permute-start(bf16[144,4608]{1,0:T(8,128)(2,1)S(1)} %pad_maximum_fusion.1), channel_id=1, source_target_pairs={{0,3},{1,0},{2,1},{3,2},{4,7},{5,4},{6,5},{7,6},{8,11},{9,8},{10,9... | collective-permute-start | bytes 3981320 | tf_op jit(solution)/shard_map/ppermute | solution.py:14
  115.3 7.0 %collective-permute-done.18 = bf16[96,4608]{1,0:T(8,128)(2,1)S(1)} collective-permute-done((bf16[96,4608]{1,0:T(8,128)(2,1)S(1)}, bf16[96,4608]{1,0:T(8,128)(2,1)S(1)}, u32[]{:S(2)}, u32[]{:S(2)}) %collective-permute-start.18) | collective-permute-done | bytes 884768 | tf_op jit(solution)/shard_map/ppermute | solution.py:14
  122.3 5.1 %collective-permute-done.16 = bf16[96,4608]{1,0:T(8,128)(2,1)S(1)} collective-permute-done((bf16[96,4608]{1,0:T(8,128)(2,1)S(1)}, bf16[96,4608]{1,0:T(8,128)(2,1)S(1)}, u32[]{:S(2)}, u32[]{:S(2)}) %collective-permute-start.16) | collective-permute-done | bytes 884768 | tf_op jit(solution)/shard_map/ppermute | solution.py:14
  127.3 1.3 fusion.98
  128.7 1.0 collective-permute-start.21
  129.7 2.8 %collective-permute-start.20 = (bf16[24,4608]{1,0:T(8,128)(2,1)S(1)}, bf16[24,4608]{1,0:T(8,128)(2,1)S(1)}, u32[]{:S(2)}, u32[]{:S(2)}) collective-permute-start(bf16[24,4608]{1,0:T(8,128)(2,1)S(1)} %get-tuple-element.26), channel_id=1, source_target_pairs={{0,80},{64,0},{16,64},{80,16},{1,81},{65,1},{17,65},{81,17},{2,82}... | collective-permute-start | bytes 663560 | tf_op jit(solution)/shard_map/ppermute | solution.py:19
  132.4 1.9 %collective-permute-start.19 = (bf16[24,4608]{1,0:T(8,128)(2,1)S(1)}, bf16[24,4608]{1,0:T(8,128)(2,1)S(1)}, u32[]{:S(2)}, u32[]{:S(2)}) collective-permute-start(bf16[24,4608]{1,0:T(8,128)(2,1)S(1)} %get-tuple-element.24), channel_id=1, source_target_pairs={{0,16},{16,0},{1,17},{17,1},{2,18},{18,2},{3,19},{19,3},{4,20},{20... | collective-permute-start | bytes 663560 | tf_op jit(solution)/shard_map/ppermute | solution.py:14
  135.1 1.6 collective-permute-done.21
  136.7 3.4 %collective-permute-done.19 = bf16[24,4608]{1,0:T(8,128)(2,1)S(1)} collective-permute-done((bf16[24,4608]{1,0:T(8,128)(2,1)S(1)}, bf16[24,4608]{1,0:T(8,128)(2,1)S(1)}, u32[]{:S(2)}, u32[]{:S(2)}) %collective-permute-start.19) | collective-permute-done | bytes 221216 | tf_op jit(solution)/shard_map/ppermute | solution.py:14
  140.4 23.0 %collective-permute-done.24 = bf16[144,4608]{1,0:T(8,128)(2,1)S(1)} collective-permute-done((bf16[144,4608]{1,0:T(8,128)(2,1)S(1)}, bf16[144,4608]{1,0:T(8,128)(2,1)S(1)}, u32[]{:S(2)}, u32[]{:S(2)}) %collective-permute-start.24) | collective-permute-done | bytes 1327136 | tf_op jit(solution)/shard_map/ppermute | solution.py:14
  163.4 2.9 %fusion.5 = f32[1,144,4608]{2,1,0:T(8,128)} fusion(bf16[384,4608]{1,0:T(8,128)(2,1)S(1)} %constant_dynamic-update-slice_fusion.5, bf16[144,4608]{1,0:T(8,128)(2,1)S(1)} %collective-permute-done.26, bf16[144,4608]{1,0:T(8,128)(2,1)S(1)} %collective-permute-done.24, f32[1,144,4608]{2,1,0:T(8,128)S(1)} %copy-done.1, s32[]{:T(128)S(6)} %select_n.288), kind=kOutput, calls=%fused_computation.7 | convolution fusion | flops 514252800 | bytes 11698180 | tf_op jit(solution)/shard_map/dot_general | solution.py:128
  (94 shorter events, 17.5 us)
Async XLA Ops:
  0.6 4.1 %copy-start.5 = (f32[1,1536,144]{1,2,0:T(8,128)S(1)}, f32[1,1536,144]{1,2,0:T(8,128)}, u32[]{:S(2)}) copy-start(f32[1,1536,144]{1,2,0:T(8,128)} %param.9) | copy-start | bytes 2654212
  0.6 4.1 %copy-start.3 = (f32[1,1536,144]{1,2,0:T(8,128)S(1)}, f32[1,1536,144]{1,2,0:T(8,128)}, u32[]{:S(2)}) copy-start(f32[1,1536,144]{1,2,0:T(8,128)} %param.8) | copy-start | bytes 2654212
  4.7 14.0 %collective-permute-start.7 = (bf16[2,12,4608]{2,0,1:T(2,128)(2,1)}, bf16[2,12,4608]{2,0,1:T(2,128)(2,1)S(1)}, u32[]{:S(2)}, u32[]{:S(2)}) collective-permute-start(bf16[2,12,4608]{2,0,1:T(2,128)(2,1)} %bitcast.84), channel_id=1, source_target_pairs={{0,32},{32,0},{1,33},{33,1},{2,34},{34,2},{3,35},{35,3},{4,36},{36... | collective-permute-start | bytes 663560 | tf_op jit(solution)/shard_map/ppermute | solution.py:14
  10.2 8.2 %copy-start.2 = (bf16[2,1,12,4608]{3,1,0,2:T(2,128)(2,1)S(1)}, bf16[2,1,12,4608]{3,1,0,2:T(2,128)(2,1)}, u32[]{:S(2)}) copy-start(bf16[2,1,12,4608]{3,1,0,2:T(2,128)(2,1)} %get-tuple-element.35) | copy-start | bytes 663556
  11.0 14.1 %collective-permute-start.2 = (bf16[3,144,384]{2,1,0:T(8,128)(2,1)}, bf16[3,144,384]{2,1,0:T(8,128)(2,1)}, u32[]{:S(2)}, u32[]{:S(2)}) collective-permute-start(bf16[3,144,384]{2,1,0:T(8,128)(2,1)} %bitcast.79), channel_id=1, source_target_pairs={{0,2},{1,3},{2,0},{3,1},{4,6},{5,7},{6,4},{7,5},{8,10},{9,11},{10,... | collective-permute-start | bytes 995336 | tf_op jit(solution)/shard_map/ppermute | solution.py:14
  15.6 16.6 %collective-permute-start.1 = (bf16[3,144,384]{2,1,0:T(8,128)(2,1)}, bf16[3,144,384]{2,1,0:T(8,128)(2,1)}, u32[]{:S(2)}, u32[]{:S(2)}) collective-permute-start(bf16[3,144,384]{2,1,0:T(8,128)(2,1)} %bitcast.80), channel_id=1, source_target_pairs={{0,3},{1,0},{2,1},{3,2},{4,7},{5,4},{6,5},{7,6},{8,11},{9,8},{10,9... | collective-permute-start | bytes 995336 | tf_op jit(solution)/shard_map/ppermute | solution.py:14
  17.1 16.6 %collective-permute-start = (bf16[3,144,384]{2,1,0:T(8,128)(2,1)}, bf16[3,144,384]{2,1,0:T(8,128)(2,1)}, u32[]{:S(2)}, u32[]{:S(2)}) collective-permute-start(bf16[3,144,384]{2,1,0:T(8,128)(2,1)} %bitcast.81), channel_id=1, source_target_pairs={{0,1},{1,2},{2,3},{3,0},{4,5},{5,6},{6,7},{7,4},{8,9},{9,10},{10,1... | collective-permute-start | bytes 995336 | tf_op jit(solution)/shard_map/ppermute | solution.py:14
  20.3 17.0 %collective-permute-start.8 = (bf16[24,4608]{1,0:T(8,128)(2,1)}, bf16[24,4608]{1,0:T(8,128)(2,1)}, u32[]{:S(2)}, u32[]{:S(2)}) collective-permute-start(bf16[24,4608]{1,0:T(8,128)(2,1)} %bitcast.83), channel_id=1, source_target_pairs={{0,64},{64,16},{16,80},{80,0},{1,65},{65,17},{17,81},{81,1},{2,66}... | collective-permute-start | bytes 663560 | tf_op jit(solution)/shard_map/ppermute | solution.py:19
  21.8 15.5 %collective-permute-start.9 = (bf16[24,4608]{1,0:T(8,128)(2,1)}, bf16[24,4608]{1,0:T(8,128)(2,1)}, u32[]{:S(2)}, u32[]{:S(2)}) collective-permute-start(bf16[24,4608]{1,0:T(8,128)(2,1)} %bitcast.83), channel_id=1, source_target_pairs={{0,80},{64,0},{16,64},{80,16},{1,81},{65,1},{17,65},{81,17},{2,82}... | collective-permute-start | bytes 663560 | tf_op jit(solution)/shard_map/ppermute | solution.py:19
  25.1 12.3 %collective-permute-start.10 = (bf16[24,4608]{1,0:T(8,128)(2,1)}, bf16[24,4608]{1,0:T(8,128)(2,1)}, u32[]{:S(2)}, u32[]{:S(2)}) collective-permute-start(bf16[24,4608]{1,0:T(8,128)(2,1)} %get-tuple-element.9), channel_id=1, source_target_pairs={{0,16},{16,0},{1,17},{17,1},{2,18},{18,2},{3,19},{19,3},{4,20},{20... | collective-permute-start | bytes 663560 | tf_op jit(solution)/shard_map/ppermute | solution.py:14
  32.2 32.2 %collective-permute-start.3 = (bf16[144,4608]{1,0:T(8,128)(2,1)}, bf16[144,4608]{1,0:T(8,128)(2,1)S(1)}, u32[]{:S(2)}, u32[]{:S(2)}) collective-permute-start(bf16[144,4608]{1,0:T(8,128)(2,1)} %get-tuple-element.11), channel_id=1, source_target_pairs={{0,1},{1,2},{2,3},{3,0},{4,5},{5,6},{6,7},{7,4},{8,9},{9,10},{10,1... | collective-permute-start | bytes 3981320 | tf_op jit(solution)/shard_map/ppermute | solution.py:14
  33.7 31.0 %collective-permute-start.4 = (bf16[144,4608]{1,0:T(8,128)(2,1)}, bf16[144,4608]{1,0:T(8,128)(2,1)S(1)}, u32[]{:S(2)}, u32[]{:S(2)}) collective-permute-start(bf16[144,4608]{1,0:T(8,128)(2,1)} %get-tuple-element.11), channel_id=1, source_target_pairs={{0,3},{1,0},{2,1},{3,2},{4,7},{5,4},{6,5},{7,6},{8,11},{9,8},{10,9... | collective-permute-start | bytes 3981320 | tf_op jit(solution)/shard_map/ppermute | solution.py:14
  37.4 30.7 %copy-start = (bf16[576,4608]{1,0:T(8,128)(2,1)S(1)}, bf16[576,4608]{1,0:T(8,128)(2,1)}, u32[]{:S(2)}) copy-start(bf16[576,4608]{1,0:T(8,128)(2,1)} %get-tuple-element.10) | copy-start | bytes 15925252
  38.9 29.4 %collective-permute-start.11 = (bf16[96,4608]{1,0:T(8,128)(2,1)S(1)}, bf16[96,4608]{1,0:T(8,128)(2,1)S(1)}, u32[]{:S(2)}, u32[]{:S(2)}) collective-permute-start(bf16[96,4608]{1,0:T(8,128)(2,1)S(1)} %pad_maximum_fusion.2), channel_id=1, source_target_pairs={{0,4},{4,8},{8,12},{12,0},{1,5},{5,9},{9,13},{13,1},{2,6},{6,10},{... | collective-permute-start | bytes 2654216 | tf_op jit(solution)/shard_map/ppermute | solution.py:14
  40.2 29.5 %collective-permute-start.12 = (bf16[96,4608]{1,0:T(8,128)(2,1)S(1)}, bf16[96,4608]{1,0:T(8,128)(2,1)S(1)}, u32[]{:S(2)}, u32[]{:S(2)}) collective-permute-start(bf16[96,4608]{1,0:T(8,128)(2,1)S(1)} %pad_maximum_fusion.2), channel_id=1, source_target_pairs={{0,12},{4,0},{8,4},{12,8},{1,13},{5,1},{9,5},{13,9},{2,14},{6,2},{... | collective-permute-start | bytes 2654216 | tf_op jit(solution)/shard_map/ppermute | solution.py:14
  64.5 18.6 %collective-permute-start.5 = (bf16[72,4608]{1,0:T(8,128)(2,1)S(1)}, bf16[72,4608]{1,0:T(8,128)(2,1)S(1)}, u32[]{:S(2)}, u32[]{:S(2)}) collective-permute-start(bf16[72,4608]{1,0:T(8,128)(2,1)S(1)} %slice.186), channel_id=1, source_target_pairs={{0,1},{1,2},{2,3},{3,0},{4,5},{5,6},{6,7},{7,4},{8,9},{9,10},{10,1... | collective-permute-start | bytes 1990664 | tf_op jit(solution)/shard_map/ppermute | solution.py:14
  64.8 18.6 %collective-permute-start.6 = (bf16[72,4608]{1,0:T(8,128)(2,1)S(1)}, bf16[72,4608]{1,0:T(8,128)(2,1)S(1)}, u32[]{:S(2)}, u32[]{:S(2)}) collective-permute-start(bf16[72,4608]{1,0:T(8,128)(2,1)S(1)} %slice.187), channel_id=1, source_target_pairs={{0,3},{1,0},{2,1},{3,2},{4,7},{5,4},{6,5},{7,6},{8,11},{9,8},{10,9... | collective-permute-start | bytes 1990664 | tf_op jit(solution)/shard_map/ppermute | solution.py:14
  68.3 10.0 %collective-permute-start.13 = (bf16[48,4608]{1,0:T(8,128)(2,1)S(1)}, bf16[48,4608]{1,0:T(8,128)(2,1)S(1)}, u32[]{:S(2)}, u32[]{:S(2)}) collective-permute-start(bf16[48,4608]{1,0:T(8,128)(2,1)S(1)} %slice.192), channel_id=1, source_target_pairs={{0,4},{4,8},{8,12},{12,0},{1,5},{5,9},{9,13},{13,1},{2,6},{6,10},{... | collective-permute-start | bytes 1327112 | tf_op jit(solution)/shard_map/ppermute | solution.py:14
  69.7 9.8 %collective-permute-start.14 = (bf16[48,4608]{1,0:T(8,128)(2,1)S(1)}, bf16[48,4608]{1,0:T(8,128)(2,1)S(1)}, u32[]{:S(2)}, u32[]{:S(2)}) collective-permute-start(bf16[48,4608]{1,0:T(8,128)(2,1)S(1)} %slice.193), channel_id=1, source_target_pairs={{0,12},{4,0},{8,4},{12,8},{1,13},{5,1},{9,5},{13,9},{2,14},{6,2},{... | collective-permute-start | bytes 1327112 | tf_op jit(solution)/shard_map/ppermute | solution.py:14
  80.6 31.3 %collective-permute-start.25 = (bf16[72,4608]{1,0:T(8,128)(2,1)S(1)}, bf16[72,4608]{1,0:T(8,128)(2,1)S(1)}, u32[]{:S(2)}, u32[]{:S(2)}) collective-permute-start(bf16[72,4608]{1,0:T(8,128)(2,1)S(1)} %get-tuple-element.15), channel_id=1, source_target_pairs={{0,3},{1,0},{2,1},{3,2},{4,7},{5,4},{6,5},{7,6},{8,11},{9,8},{10,9... | collective-permute-start | bytes 1990664 | tf_op jit(solution)/shard_map/ppermute | solution.py:14
  89.4 15.6 %collective-permute-start.17 = (bf16[48,4608]{1,0:T(8,128)(2,1)S(1)}, bf16[48,4608]{1,0:T(8,128)(2,1)S(1)}, u32[]{:S(2)}, u32[]{:S(2)}) collective-permute-start(bf16[48,4608]{1,0:T(8,128)(2,1)S(1)} %get-tuple-element.28), channel_id=1, source_target_pairs={{0,12},{4,0},{8,4},{12,8},{1,13},{5,1},{9,5},{13,9},{2,14},{6,2},{... | collective-permute-start | bytes 1327112 | tf_op jit(solution)/shard_map/ppermute | solution.py:14
  89.9 6.4 %collective-permute-start.29 = (bf16[144,384]{1,0:T(8,128)(2,1)S(1)}, bf16[144,384]{1,0:T(8,128)(2,1)S(1)}, u32[]{:S(2)}, u32[]{:S(2)}) collective-permute-start(bf16[144,384]{1,0:T(8,128)(2,1)S(1)} %get-tuple-element.32), channel_id=1, source_target_pairs={{0,2},{1,3},{2,0},{3,1},{4,6},{5,7},{6,4},{7,5},{8,10},{9,11},{10,... | collective-permute-start | bytes 331784 | tf_op jit(solution)/shard_map/ppermute | solution.py:14
  92.0 8.1 %collective-permute-start.28 = (bf16[144,384]{1,0:T(8,128)(2,1)S(1)}, bf16[144,384]{1,0:T(8,128)(2,1)S(1)}, u32[]{:S(2)}, u32[]{:S(2)}) collective-permute-start(bf16[144,384]{1,0:T(8,128)(2,1)S(1)} %get-tuple-element.33), channel_id=1, source_target_pairs={{0,3},{1,0},{2,1},{3,2},{4,7},{5,4},{6,5},{7,6},{8,11},{9,8},{10,9... | collective-permute-start | bytes 331784 | tf_op jit(solution)/shard_map/ppermute | solution.py:14
  94.4 7.2 %copy-start.4 = (f32[1,1536,144]{1,2,0:T(8,128)S(1)}, f32[1,1536,144]{1,2,0:T(8,128)}, u32[]{:S(2)}) copy-start(f32[1,1536,144]{1,2,0:T(8,128)} %param.8) | copy-start | bytes 2654212
  94.4 7.2 %copy-start.6 = (f32[1,1536,144]{1,2,0:T(8,128)S(1)}, f32[1,1536,144]{1,2,0:T(8,128)}, u32[]{:S(2)}) copy-start(f32[1,1536,144]{1,2,0:T(8,128)} %param.9) | copy-start | bytes 2654212
  94.4 7.2 %collective-permute-start.27 = (bf16[144,384]{1,0:T(8,128)(2,1)S(1)}, bf16[144,384]{1,0:T(8,128)(2,1)S(1)}, u32[]{:S(2)}, u32[]{:S(2)}) collective-permute-start(bf16[144,384]{1,0:T(8,128)(2,1)S(1)} %get-tuple-element.34), channel_id=1, source_target_pairs={{0,1},{1,2},{2,3},{3,0},{4,5},{5,6},{6,7},{7,4},{8,9},{9,10},{10,1... | collective-permute-start | bytes 331784 | tf_op jit(solution)/shard_map/ppermute | solution.py:14
  96.3 18.9 %collective-permute-start.23 = (bf16[72,4608]{1,0:T(8,128)(2,1)S(1)}, bf16[72,4608]{1,0:T(8,128)(2,1)S(1)}, u32[]{:S(2)}, u32[]{:S(2)}) collective-permute-start(bf16[72,4608]{1,0:T(8,128)(2,1)S(1)} %get-tuple-element.14), channel_id=1, source_target_pairs={{0,1},{1,2},{2,3},{3,0},{4,5},{5,6},{6,7},{7,4},{8,9},{9,10},{10,1... | collective-permute-start | bytes 1990664 | tf_op jit(solution)/shard_map/ppermute | solution.py:14
  100.1 10.7 %collective-permute-start.15 = (bf16[48,4608]{1,0:T(8,128)(2,1)S(1)}, bf16[48,4608]{1,0:T(8,128)(2,1)S(1)}, u32[]{:S(2)}, u32[]{:S(2)}) collective-permute-start(bf16[48,4608]{1,0:T(8,128)(2,1)S(1)} %get-tuple-element.27), channel_id=1, source_target_pairs={{0,4},{4,8},{8,12},{12,0},{1,5},{5,9},{9,13},{13,1},{2,6},{6,10},{... | collective-permute-start | bytes 1327112 | tf_op jit(solution)/shard_map/ppermute | solution.py:14
  105.2 17.1 %collective-permute-start.18 = (bf16[96,4608]{1,0:T(8,128)(2,1)S(1)}, bf16[96,4608]{1,0:T(8,128)(2,1)S(1)}, u32[]{:S(2)}, u32[]{:S(2)}) collective-permute-start(bf16[96,4608]{1,0:T(8,128)(2,1)S(1)} %pad_maximum_fusion.4), channel_id=1, source_target_pairs={{0,12},{4,0},{8,4},{12,8},{1,13},{5,1},{9,5},{13,9},{2,14},{6,2},{... | collective-permute-start | bytes 2654216 | tf_op jit(solution)/shard_map/ppermute | solution.py:14
  111.0 16.4 %collective-permute-start.16 = (bf16[96,4608]{1,0:T(8,128)(2,1)S(1)}, bf16[96,4608]{1,0:T(8,128)(2,1)S(1)}, u32[]{:S(2)}, u32[]{:S(2)}) collective-permute-start(bf16[96,4608]{1,0:T(8,128)(2,1)S(1)} %pad_maximum_fusion.3), channel_id=1, source_target_pairs={{0,4},{4,8},{8,12},{12,0},{1,5},{5,9},{9,13},{13,1},{2,6},{6,10},{... | collective-permute-start | bytes 2654216 | tf_op jit(solution)/shard_map/ppermute | solution.py:14
  112.1 28.3 %collective-permute-start.26 = (bf16[144,4608]{1,0:T(8,128)(2,1)S(1)}, bf16[144,4608]{1,0:T(8,128)(2,1)S(1)}, u32[]{:S(2)}, u32[]{:S(2)}) collective-permute-start(bf16[144,4608]{1,0:T(8,128)(2,1)S(1)} %pad_maximum_fusion.1), channel_id=1, source_target_pairs={{0,3},{1,0},{2,1},{3,2},{4,7},{5,4},{6,5},{7,6},{8,11},{9,8},{10,9... | collective-permute-start | bytes 3981320 | tf_op jit(solution)/shard_map/ppermute | solution.py:14
  128.7 34.8 %copy-start.1 = (f32[1,144,4608]{2,1,0:T(8,128)S(1)}, f32[1,144,4608]{2,1,0:T(8,128)}, u32[]{:S(2)}) copy-start(f32[1,144,4608]{2,1,0:T(8,128)} %param.7) | copy-start | bytes 7962628
  128.7 8.0 %collective-permute-start.21 = (bf16[24,4608]{1,0:T(8,128)(2,1)S(1)}, bf16[24,4608]{1,0:T(8,128)(2,1)S(1)}, u32[]{:S(2)}, u32[]{:S(2)}) collective-permute-start(bf16[24,4608]{1,0:T(8,128)(2,1)S(1)} %get-tuple-element.25), channel_id=1, source_target_pairs={{0,64},{64,16},{16,80},{80,0},{1,65},{65,17},{17,81},{81,1},{2,66}... | collective-permute-start | bytes 663560 | tf_op jit(solution)/shard_map/ppermute | solution.py:19
  129.7 7.0 %collective-permute-start.20 = (bf16[24,4608]{1,0:T(8,128)(2,1)S(1)}, bf16[24,4608]{1,0:T(8,128)(2,1)S(1)}, u32[]{:S(2)}, u32[]{:S(2)}) collective-permute-start(bf16[24,4608]{1,0:T(8,128)(2,1)S(1)} %get-tuple-element.26), channel_id=1, source_target_pairs={{0,80},{64,0},{16,64},{80,16},{1,81},{65,1},{17,65},{81,17},{2,82}... | collective-permute-start | bytes 663560 | tf_op jit(solution)/shard_map/ppermute | solution.py:19
  132.4 7.7 %collective-permute-start.19 = (bf16[24,4608]{1,0:T(8,128)(2,1)S(1)}, bf16[24,4608]{1,0:T(8,128)(2,1)S(1)}, u32[]{:S(2)}, u32[]{:S(2)}) collective-permute-start(bf16[24,4608]{1,0:T(8,128)(2,1)S(1)} %get-tuple-element.24), channel_id=1, source_target_pairs={{0,16},{16,0},{1,17},{17,1},{2,18},{18,2},{3,19},{19,3},{4,20},{20... | collective-permute-start | bytes 663560 | tf_op jit(solution)/shard_map/ppermute | solution.py:14
  134.4 29.0 %collective-permute-start.24 = (bf16[144,4608]{1,0:T(8,128)(2,1)S(1)}, bf16[144,4608]{1,0:T(8,128)(2,1)S(1)}, u32[]{:S(2)}, u32[]{:S(2)}) collective-permute-start(bf16[144,4608]{1,0:T(8,128)(2,1)S(1)} %pad_maximum_fusion), channel_id=1, source_target_pairs={{0,1},{1,2},{2,3},{3,0},{4,5},{5,6},{6,7},{7,4},{8,9},{9,10},{10,1... | collective-permute-start | bytes 3981320 | tf_op jit(solution)/shard_map/ppermute | solution.py:14
  140.3 26.0 %collective-permute-start.22 = (bf16[2,12,4608]{2,1,0:T(8,128)(2,1)S(1)}, bf16[2,12,4608]{2,1,0:T(8,128)(2,1)S(1)}, u32[]{:S(2)}, u32[]{:S(2)}) collective-permute-start(bf16[2,12,4608]{2,1,0:T(8,128)(2,1)S(1)} %pad_maximum_fusion.7), channel_id=1, source_target_pairs={{0,32},{32,0},{1,33},{33,1},{2,34},{34,2},{3,35},{35,3},{4,36},{36... | collective-permute-start | bytes 663560 | tf_op jit(solution)/shard_map/ppermute | solution.py:14

commit v2 on v1

v2 whole, which is shorter than its diff:
```python
import jax
import jax.numpy as jnp
from jax import lax
from jax.sharding import Mesh, PartitionSpec as P

bias_fix = 1.0 - 0.95**10
half = jnp.bfloat16
AXES = ("xl", "core", "xh", "y", "z")
OFFSETS = (-1, 1, 2, 0)


def route(value, target):
    sizes = (2, 2, 2, 4, 4)
    pairs = []
    for source in range(128):
        at, rest = [], source
        for size in reversed(sizes):
            at.append(rest % size)
            rest //= size
        place = 0
        for to, size in zip(target(*reversed(at)), sizes):
            place = place * size + to % size
        pairs.append((source, place))
    return lax.ppermute(value, AXES, pairs)


def shift_core(value):
    return route(value, lambda xl, c, xh, y, z: (xl, 1 - c, xh, y, z))


def shift_x(value, step):
    return route(
        value,
        lambda xl, c, xh, y, z: ((xl + step) % 2, c, (2 * xh + xl + step) % 4 // 2, y, z),
    )


def shift_own(value, step):
    return route(
        value, lambda xl, c, xh, y, z: (xl, c, xh, y + step * c, z + step * (1 - c))
    )


def shift_row(value, step):
    return route(
        value, lambda xl, c, xh, y, z: (xl, c, xh, y + step * (1 - c), z + step * c)
    )


def ring_near(own, shift):
    cut = own.shape[0] // 2
    before, after = shift(own, 1), shift(own, -1)
    return before, after, before[:cut], after[cut:]


def ring_far(own, near, shift):
    before, after, top, low = near
    return jnp.concatenate([before, after, shift(top, 1), shift(low, -1), own], 0)


def ring_sum(term, size, shift, wait=None):
    cut = size // 2
    top = shift(term(2, 0, cut).astype(half), 1)
    low = shift(term(2, cut, size - cut).astype(half), -1)
    if wait is not None:
        top, low, wait = lax.optimization_barrier((top, low, wait))
    up = term(1, 0, size) + jnp.pad(top.astype(jnp.float32), ((0, size - cut), (0, 0)))
    down = term(0, 0, size) + jnp.pad(low.astype(jnp.float32), ((cut, 0), (0, 0)))
    up = shift(up.astype(half), 1)
    down = shift(down.astype(half), -1)
    return up, down, wait


def body(gradient, eigenbasis, gram_sum, first_moment, second_moment):
    rows = gradient.shape[1]
    width = gradient.shape[2]
    span = eigenbasis.shape[1]
    total = first_moment.shape[1]
    xl, core, xh, y, z = (lax.axis_index(a) for a in AXES)

    def pick(pair, index):
        return jnp.where(index == 0, pair[0], pair[1])

    pairs = gradient.reshape(2, 2, rows, width)
    keep = pick((pairs[:, 0], pairs[:, 1]), core)
    other = shift_core(pick((pairs[:, 1], pairs[:, 0]), core))
    chip = jnp.concatenate([keep, other], 1)
    own_layer = pick((chip[0], chip[1]), xl)
    next_layer = pick((chip[1], chip[0]), xl)
    line = jnp.concatenate(
        [shift_x(next_layer, 1), shift_x(next_layer, -1), shift_x(own_layer, 2), own_layer], 0
    )
    count = 4 * line.shape[0]

    own_basis = eigenbasis[0].astype(half)
    near = ring_near(own_basis, shift_own)
    line_near = ring_near(line, shift_row)

    at = lax.broadcasted_iota(jnp.int32, (1, 4 * count), 1)

    def offset(index):
        return jnp.where(index == 0, -1, jnp.where(index == 3, 0, index))

    row = at % rows
    core_of = (core + at // rows) % 2
    x_of = (2 * xh + xl + offset(at // (2 * rows) % 4) + 4) % 4
    along_row = offset(at // (8 * rows) % 4) + 4
    along_own = offset(at // (32 * rows)) + 4
    y_of = (y + jnp.where(core == 0, along_row, along_own)) % 4
    z_of = (z + jnp.where(core == 0, along_own, along_row)) % 4
    number = ((((x_of % 2 * 2 + core_of) * 2 + x_of // 2) * 4 + y_of) * 4 + z_of) * rows + row
    order = (lax.broadcasted_iota(jnp.int32, (total, 4 * count), 0) == number).astype(half)

    first = first_moment[0].T
    second = second_moment[0].T
    first_high = first.astype(half)
    first_low = (first - first_high.astype(jnp.float32)).astype(half)
    moments = jnp.concatenate([first_high, first_low, second.astype(half)], 0)
    moments = jnp.dot(moments, order, preferred_element_type=jnp.float32).astype(half)
    moments, *tied = lax.optimization_barrier((moments, *near[2:]))
    near = (*near[:2], *tied)
    moments = [moments[:, k * count : (k + 1) * count] for k in range(4)]
    moved = [
        shift_own(moments[1], 1),
        shift_own(moments[0], -1),
        shift_own(moments[2], 2),
        moments[3],
    ]
    moved = [value.reshape(3, span, count) for value in moved]
    moved = jnp.concatenate(moved, 1).astype(jnp.float32)

    basis = ring_far(own_basis, near, shift_own)
    grads = ring_far(line, line_near, shift_row)
    rotated = lax.dot_general(
        basis, grads, (((1,), (1,)), ((), ())), preferred_element_type=jnp.float32
    )
    new_first = 0.95 * (moved[0] + moved[1]) + 0.05 * rotated
    new_second = 0.95 * moved[2] + 0.05 * rotated * rotated
    direction = (new_first / bias_fix / (jnp.sqrt(new_second / bias_fix) + 1e-08)).astype(half)

    def update_term(place, start, size):
        at = place * 8 * rows + start
        return lax.dot_general(
            direction[:, at : at + size],
            basis,
            (((0,), (0,)), ((), ())),
            preferred_element_type=jnp.float32,
        )

    up, down, _ = ring_sum(update_term, 8 * rows, shift_row)
    summed = update_term(3, 0, 8 * rows) + up.astype(jnp.float32) + down.astype(jnp.float32)
    summed = summed.reshape(4, 2 * rows, width)
    sent = summed.astype(half)
    far = shift_x(sent[2], 2)
    left = shift_x(sent[0], -1)
    right = shift_x(sent[1], 1)
    own_update = (summed[3] + far.astype(jnp.float32)).astype(half)
    next_update = (left.astype(jnp.float32) + right.astype(jnp.float32)).astype(half)
    update = jnp.stack([pick((own_update, next_update), xl), pick((next_update, own_update), xl)])
    def gram_term(place, start, size):
        y_at = (y + OFFSETS[place] * core + 4) % 4
        z_at = (z + OFFSETS[place] * (1 - core) + 4) % 4
        column = ((xh * 4 + y_at) * 4 + z_at) * span + start
        columns = lax.dynamic_slice_in_dim(grads, column, size, 1)
        return lax.dot_general(
            columns, grads, (((0,), (0,)), ((), ())), preferred_element_type=jnp.float32
        )

    blocks = rotated.astype(half).reshape(4, span, count)
    up, down, blocks = ring_sum(gram_term, span, shift_own, blocks)
    update, up, down = lax.optimization_barrier((update, up, down))
    product = gram_term(3, 0, span) + up.astype(jnp.float32) + down.astype(jnp.float32)
    new_gram = 0.95 * gram_sum[0] + 0.05 * product

    given = shift_core(update[:, rows:])
    update = update[:, :rows]
    update = jnp.stack([pick((update, given), core), pick((given, update), core)], 1)
    update = update.reshape(4, rows, width)

    owned = [
        shift_own(blocks[1], 1),
        shift_own(blocks[0], -1),
        shift_own(blocks[2], 2),
        blocks[3],
    ]
    owned = lax.dot_general(
        jnp.concatenate(owned, 1), order, (((1,), (1,)), ((), ())), preferred_element_type=jnp.float32
    )
    out_first = 0.95 * first + 0.05 * owned
    out_second = 0.95 * second + 0.05 * owned * owned
    return (update, new_gram[None], out_first.T[None], out_second.T[None])


def solution(mesh):
    fine = Mesh(mesh.devices.reshape(2, 2, 2, 4, 4), AXES)
    layer, fsdp = ("xl", "core"), ("xh", "y", "z")
    return jax.shard_map(
        body,
        mesh=fine,
        in_specs=(
            P(None, AXES, None),
            P(layer, fsdp, None),
            P(layer, fsdp, None),
            P(layer, None, fsdp),
            P(layer, None, fsdp),
        ),
        out_specs=(
            P(None, AXES, None),
            P(layer, fsdp, None),
            P(layer, None, fsdp),
            P(layer, None, fsdp),
        ),
        check_vma=False,
    )
```

time: 168 us -> 143 us (0.85)
  the two profiles are of different devices: /device:TPU:16 before, /device:TPU:1 now
where the time goes in v2:
time: 143 us
  waiting for transfers between devices  63.2 us (44%)
  starting transfers between devices  40.2 us (28%)
  matrix products  22.7 us (16%)
  other arithmetic  10.1 us (7%)
  local copies, waits for them, and re-layouts  5.5 us (4%)
    ppermute x30, waiting for transfers between devices, route(): return lax.ppermute(value, AXES, pairs)  63.2 us
    ppermute x30, starting transfers between devices, route(): return lax.ppermute(value, AXES, pairs)  40.2 us
    dot_general x5, matrix products, gram_term(): lax.dot_general(columns, grads, (((0,), (0,)), ((), ())), preferred_eleme...  6.49 us
    dot_general x5, matrix products, update_term(): lax.dot_general(direction[:, at:at + size], basis, (((0,), (0,)), ((), ()...  6.04 us
    select_n x3, other arithmetic, pick(): return jnp.where(index == 0, pair[0], pair[1])  3.51 us
    unnamed x39, local copies, waits for them, and re-layouts  3.48 us
    dot_general x1, matrix products, body(): lax.dot_general(jnp.concatenate(owned, 1), order, (((1,), (1,)), ((), ())...  3.42 us
    dot_general x1, matrix products, body(): jnp.dot(moments, order, preferred_element_type=jnp.float32).astype(half)  3.41 us
  transfers between devices with their start and end apart: 30, of which 13 were waited for; matrix products, arithmetic and copies ran while one was open for 24% of the time, Pallas kernels for 0%

profile of v2, /device:TPU:1, one launch (start us, length us, event | category | flops | bytes accessed | tf_op | source)
XLA Modules:
  0.0 142.9 jit_solution(5868183241805605469)
XLA Ops:
  0.6 3.0 %convert_bitcast_fusion = bf16[144,4608]{1,0:T(8,128)(2,1)} fusion(f32[1,144,4608]{2,1,0:T(8,128)} %param.6), kind=kLoop, calls=%fused_computation.31 | loop fusion | flops 663552 | bytes 3981312 | tf_op jit(solution)/shard_map/convert_element_type | solution.py:95
  3.6 2.1 %collective-permute-start = (bf16[144,4608]{1,0:T(8,128)(2,1)}, bf16[144,4608]{1,0:T(8,128)(2,1)S(1)}, u32[]{:S(2)}, u32[]{:S(2)}) collective-permute-start(bf16[144,4608]{1,0:T(8,128)(2,1)} %convert_bitcast_fusion), channel_id=1, source_target_pairs={{0,1},{1,2},{2,3},{3,0},{4,5},{5,6},{6,7},{7,4},{8,9},{9,10},{10,1... | collective-permute-start | bytes 3981320 | tf_op jit(solution)/shard_map/ppermute | solution.py:24
  5.8 1.4 %collective-permute-start.1 = (bf16[144,4608]{1,0:T(8,128)(2,1)}, bf16[144,4608]{1,0:T(8,128)(2,1)S(1)}, u32[]{:S(2)}, u32[]{:S(2)}) collective-permute-start(bf16[144,4608]{1,0:T(8,128)(2,1)} %convert_bitcast_fusion), channel_id=1, source_target_pairs={{0,3},{1,0},{2,1},{3,2},{4,7},{5,4},{6,5},{7,6},{8,11},{9,8},{10,9... | collective-permute-start | bytes 3981320 | tf_op jit(solution)/shard_map/ppermute | solution.py:24
  7.4 1.0 broadcast_select_fusion.1
  8.7 2.1 %collective-permute-start.7 = (bf16[2,12,4608]{2,0,1:T(2,128)(2,1)S(1)}, bf16[2,12,4608]{2,0,1:T(2,128)(2,1)S(1)}, u32[]{:S(2)}, u32[]{:S(2)}) collective-permute-start(bf16[2,12,4608]{2,0,1:T(2,128)(2,1)S(1)} %bitcast.99), channel_id=1, source_target_pairs={{0,32},{1,33},{2,34},{3,35},{4,36},{5,37},{6,38},{7,39},{8,40},{9,... | collective-permute-start | bytes 663560 | tf_op jit(solution)/shard_map/ppermute | solution.py:24
  10.7 1.0 fusion.31
  12.8 0.9 broadcast_select_fusion.3
  14.5 2.5 %collective-permute-start.9 = (bf16[24,4608]{1,0:T(8,128)(2,1)}, bf16[24,4608]{1,0:T(8,128)(2,1)S(1)}, u32[]{:S(2)}, u32[]{:S(2)}) collective-permute-start(bf16[24,4608]{1,0:T(8,128)(2,1)} %bitcast.89), channel_id=1, source_target_pairs={{0,80},{1,81},{2,82},{3,83},{4,84},{5,85},{6,86},{7,87},{8,88},{9,... | collective-permute-start | bytes 663560 | tf_op jit(solution)/shard_map/ppermute | solution.py:24
  17.0 1.6 %broadcast_select_fusion.2 = bf16[1,24,4608]{2,0,1:T(2,128)(2,1)S(1)} fusion(bf16[1,24,4608]{2,0,1:T(2,128)(2,1)S(1)} %get-tuple-element.23, pred[]{:T(512)S(6)} %eq.99, bf16[2,12,4608]{2,0,1:T(2,128)(2,1)} %copy-done.5, bf16[2,12,4608]{2,0,1:T(2,128)(2,1)S(1)} %bitcast.93), kind=kLoop, calls=%fused_computation.58 | loop fusion | flops 552960 | bytes 884737 | tf_op jit(solution)/shard_map/jit(_where)/select_n | solution.py:82
  19.3 1.7 %collective-permute-start.10 = (bf16[24,4608]{1,0:T(8,128)(2,1)}, bf16[24,4608]{1,0:T(8,128)(2,1)}, u32[]{:S(2)}, u32[]{:S(2)}) collective-permute-start(bf16[24,4608]{1,0:T(8,128)(2,1)} %bitcast.88), channel_id=1, source_target_pairs={{0,16},{1,17},{2,18},{3,19},{4,20},{5,21},{6,22},{7,23},{8,24},{9,... | collective-permute-start | bytes 663560 | tf_op jit(solution)/shard_map/ppermute | solution.py:24
  21.0 3.4 %fusion.13 = bf16[432,1536]{1,0:T(8,128)(2,1)} fusion(s32[1536]{0:T(1024)S(1)} %fusion.67, bf16[144,1536]{1,0:T(8,128)(2,1)S(1)} %copy-done.11, bf16[144,1536]{1,0:T(8,128)(2,1)S(1)} %copy-done.8, bf16[144,1536]{1,0:T(8,128)(2,1)S(1)} %copy-done.9), kind=kOutput, calls=%fused_computation.24 | convolution fusion | flops 2045435904 | bytes 2660352 | tf_op jit(solution)/shard_map/dot_general | solution.py:119
  24.4 4.6 %collective-permute-done.10 = bf16[24,4608]{1,0:T(8,128)(2,1)} collective-permute-done((bf16[24,4608]{1,0:T(8,128)(2,1)}, bf16[24,4608]{1,0:T(8,128)(2,1)}, u32[]{:S(2)}, u32[]{:S(2)}) %collective-permute-start.10) | collective-permute-done | bytes 221216 | tf_op jit(solution)/shard_map/ppermute | solution.py:24
  29.9 1.1 pad_maximum_fusion
  31.1 2.7 %collective-permute-start.12 = (bf16[96,4608]{1,0:T(8,128)(2,1)S(1)}, bf16[96,4608]{1,0:T(8,128)(2,1)S(1)}, u32[]{:S(2)}, u32[]{:S(2)}) collective-permute-start(bf16[96,4608]{1,0:T(8,128)(2,1)S(1)} %pad_maximum_fusion), channel_id=1, source_target_pairs={{0,12},{1,13},{2,14},{3,15},{4,0},{5,1},{6,2},{7,3},{8,4},{9,5},{1... | collective-permute-start | bytes 2654216 | tf_op jit(solution)/shard_map/ppermute | solution.py:24
  33.8 1.4 collective-permute-start.5
  35.3 2.7 %collective-permute-start.4 = (bf16[432,384]{1,0:T(8,128)(2,1)S(1)}, bf16[432,384]{1,0:T(8,128)(2,1)S(1)}, u32[]{:S(2)}, u32[]{:S(2)}) collective-permute-start(bf16[432,384]{1,0:T(8,128)(2,1)S(1)} %get-tuple-element.30), channel_id=1, source_target_pairs={{0,2},{1,3},{2,0},{3,1},{4,6},{5,7},{6,4},{7,5},{8,10},{9,11},{10,... | collective-permute-start | bytes 995336 | tf_op jit(solution)/shard_map/ppermute | solution.py:24
  38.0 1.1 collective-permute-start.3
  39.3 9.6 %collective-permute-done.11 = bf16[96,4608]{1,0:T(8,128)(2,1)S(1)} collective-permute-done((bf16[96,4608]{1,0:T(8,128)(2,1)S(1)}, bf16[96,4608]{1,0:T(8,128)(2,1)S(1)}, u32[]{:S(2)}, u32[]{:S(2)}) %collective-permute-start.11) | collective-permute-done | bytes 884768 | tf_op jit(solution)/shard_map/ppermute | solution.py:24
  48.9 2.5 %collective-permute-start.2 = (bf16[432,384]{1,0:T(8,128)(2,1)S(1)}, bf16[432,384]{1,0:T(8,128)(2,1)S(1)}, u32[]{:S(2)}, u32[]{:S(2)}) collective-permute-start(bf16[432,384]{1,0:T(8,128)(2,1)S(1)} %get-tuple-element.28), channel_id=1, source_target_pairs={{0,1},{1,2},{2,3},{3,0},{4,5},{5,6},{6,7},{7,4},{8,9},{9,10},{10,1... | collective-permute-start | bytes 995336 | tf_op jit(solution)/shard_map/ppermute | solution.py:24
  51.7 6.1 %collective-permute-done.4 = bf16[432,384]{1,0:T(8,128)(2,1)S(1)} collective-permute-done((bf16[432,384]{1,0:T(8,128)(2,1)S(1)}, bf16[432,384]{1,0:T(8,128)(2,1)S(1)}, u32[]{:S(2)}, u32[]{:S(2)}) %collective-permute-start.4) | collective-permute-done | bytes 331808 | tf_op jit(solution)/shard_map/ppermute | solution.py:24
  57.8 1.7 %collective-permute-start.14 = (bf16[48,4608]{1,0:T(8,128)(2,1)S(1)}, bf16[48,4608]{1,0:T(8,128)(2,1)S(1)}, u32[]{:S(2)}, u32[]{:S(2)}) collective-permute-start(bf16[48,4608]{1,0:T(8,128)(2,1)S(1)} %slice.137), channel_id=1, source_target_pairs={{0,12},{1,13},{2,14},{3,15},{4,0},{5,1},{6,2},{7,3},{8,4},{9,5},{1... | collective-permute-start | bytes 1327112 | tf_op jit(solution)/shard_map/ppermute | solution.py:24
  59.5 3.0 %collective-permute-done.2 = bf16[432,384]{1,0:T(8,128)(2,1)S(1)} collective-permute-done((bf16[432,384]{1,0:T(8,128)(2,1)S(1)}, bf16[432,384]{1,0:T(8,128)(2,1)S(1)}, u32[]{:S(2)}, u32[]{:S(2)}) %collective-permute-start.2) | collective-permute-done | bytes 331808 | tf_op jit(solution)/shard_map/ppermute | solution.py:24
  62.7 6.5 %collective-permute-done.14 = bf16[48,4608]{1,0:T(8,128)(2,1)S(1)} collective-permute-done((bf16[48,4608]{1,0:T(8,128)(2,1)S(1)}, bf16[48,4608]{1,0:T(8,128)(2,1)S(1)}, u32[]{:S(2)}, u32[]{:S(2)}) %collective-permute-start.14) | collective-permute-done | bytes 442400 | tf_op jit(solution)/shard_map/ppermute | solution.py:24
  69.3 1.0 constant_dynamic-update-slice_fusion.6
  72.2 3.4 %fusion.98 = (bf16[576,384]{1,0:T(8,128)(2,1)S(1)}, bf16[576,384]{1,0:T(8,128)(2,1)S(1)}) fusion(f32[3,576,384]{2,1,0:T(8,128)S(1)} %maximum_convert_fusion, bf16[576,4608]{1,0:T(8,128)(2,1)S(1)} %constant_dynamic-update-slice_fusion, bf16[384,4608]{1,0:T(8,128)(2,1)S(1)} %constant_dynamic-update-slice_fusion.5), kind=kOutput, calls=%fused_computation.198 | convolution fusion | flops 2041307136 | bytes 12386304 | tf_op jit(solution)/shard_map/dot_general | solution.py:134
  75.6 1.2 convolution_convert_fusion.2
  76.7 2.8 %collective-permute-start.17 = (bf16[48,4608]{1,0:T(8,128)(2,1)S(1)}, bf16[48,4608]{1,0:T(8,128)(2,1)S(1)}, u32[]{:S(2)}, u32[]{:S(2)}) collective-permute-start(bf16[48,4608]{1,0:T(8,128)(2,1)S(1)} %convolution_convert_fusion.2), channel_id=1, source_target_pairs={{0,12},{1,13},{2,14},{3,15},{4,0},{5,1},{6,2},{7,3},{8,4},{9,5},{1... | collective-permute-start | bytes 1327112 | tf_op jit(solution)/shard_map/ppermute | solution.py:24
  79.5 1.2 convolution_convert_fusion.3
  81.6 2.0 %collective-permute-start.23 = (bf16[72,4608]{1,0:T(8,128)(2,1)S(1)}, bf16[72,4608]{1,0:T(8,128)(2,1)S(1)}, u32[]{:S(2)}, u32[]{:S(2)}) collective-permute-start(bf16[72,4608]{1,0:T(8,128)(2,1)S(1)} %convolution_convert_fusion), channel_id=1, source_target_pairs={{0,3},{1,0},{2,1},{3,2},{4,7},{5,4},{6,5},{7,6},{8,11},{9,8},{10,9... | collective-permute-start | bytes 1990664 | tf_op jit(solution)/shard_map/ppermute | solution.py:24
  83.6 1.2 collective-permute-done.17
  84.8 1.2 fusion.10
  85.9 3.2 %collective-permute-start.18 = (bf16[96,4608]{1,0:T(8,128)(2,1)S(1)}, bf16[96,4608]{1,0:T(8,128)(2,1)S(1)}, u32[]{:S(2)}, u32[]{:S(2)}) collective-permute-start(bf16[96,4608]{1,0:T(8,128)(2,1)S(1)} %fusion.10), channel_id=1, source_target_pairs={{0,12},{1,13},{2,14},{3,15},{4,0},{5,1},{6,2},{7,3},{8,4},{9,5},{1... | collective-permute-start | bytes 2654216 | tf_op jit(solution)/shard_map/ppermute | solution.py:24
  89.1 1.8 %collective-permute-done.15 = bf16[48,4608]{1,0:T(8,128)(2,1)S(1)} collective-permute-done((bf16[48,4608]{1,0:T(8,128)(2,1)S(1)}, bf16[48,4608]{1,0:T(8,128)(2,1)S(1)}, u32[]{:S(2)}, u32[]{:S(2)}) %collective-permute-start.15) | collective-permute-done | bytes 442400 | tf_op jit(solution)/shard_map/ppermute | solution.py:24
  90.9 1.2 fusion.9
  92.2 3.0 %collective-permute-done.23 = bf16[72,4608]{1,0:T(8,128)(2,1)S(1)} collective-permute-done((bf16[72,4608]{1,0:T(8,128)(2,1)S(1)}, bf16[72,4608]{1,0:T(8,128)(2,1)S(1)}, u32[]{:S(2)}, u32[]{:S(2)}) %collective-permute-start.23) | collective-permute-done | bytes 663584 | tf_op jit(solution)/shard_map/ppermute | solution.py:24
  95.3 1.0 fusion.6
  96.3 1.0 fusion.7
  97.3 2.7 %collective-permute-start.25 = (bf16[144,4608]{1,0:T(8,128)(2,1)S(1)}, bf16[144,4608]{1,0:T(8,128)(2,1)S(1)}, u32[]{:S(2)}, u32[]{:S(2)}) collective-permute-start(bf16[144,4608]{1,0:T(8,128)(2,1)S(1)} %fusion.7), channel_id=1, source_target_pairs={{0,3},{1,0},{2,1},{3,2},{4,7},{5,4},{6,5},{7,6},{8,11},{9,8},{10,9... | collective-permute-start | bytes 3981320 | tf_op jit(solution)/shard_map/ppermute | solution.py:24
  100.8 3.4 %collective-permute-done.18 = bf16[96,4608]{1,0:T(8,128)(2,1)S(1)} collective-permute-done((bf16[96,4608]{1,0:T(8,128)(2,1)S(1)}, bf16[96,4608]{1,0:T(8,128)(2,1)S(1)}, u32[]{:S(2)}, u32[]{:S(2)}) %collective-permute-start.18) | collective-permute-done | bytes 884768 | tf_op jit(solution)/shard_map/ppermute | solution.py:24
  104.2 2.4 %collective-permute-start.28 = (bf16[144,384]{1,0:T(8,128)(2,1)S(1)}, bf16[144,384]{1,0:T(8,128)(2,1)S(1)}, u32[]{:S(2)}, u32[]{:S(2)}) collective-permute-start(bf16[144,384]{1,0:T(8,128)(2,1)S(1)} %get-tuple-element.44), channel_id=1, source_target_pairs={{0,3},{1,0},{2,1},{3,2},{4,7},{5,4},{6,5},{7,6},{8,11},{9,8},{10,9... | collective-permute-start | bytes 331784 | tf_op jit(solution)/shard_map/ppermute | solution.py:24
  106.7 1.3 fusion.100
  108.1 16.0 %collective-permute-done.29 = bf16[144,384]{1,0:T(8,128)(2,1)S(1)} collective-permute-done((bf16[144,384]{1,0:T(8,128)(2,1)S(1)}, bf16[144,384]{1,0:T(8,128)(2,1)S(1)}, u32[]{:S(2)}, u32[]{:S(2)}) %collective-permute-start.29) | collective-permute-done | bytes 110624 | tf_op jit(solution)/shard_map/ppermute | solution.py:24
  124.1 2.7 %collective-permute-start.20 = (bf16[24,4608]{1,0:T(8,128)(2,1)S(1)}, bf16[24,4608]{1,0:T(8,128)(2,1)S(1)}, u32[]{:S(2)}, u32[]{:S(2)}) collective-permute-start(bf16[24,4608]{1,0:T(8,128)(2,1)S(1)} %get-tuple-element.38), channel_id=1, source_target_pairs={{0,80},{1,81},{2,82},{3,83},{4,84},{5,85},{6,86},{7,87},{8,88},{9,... | collective-permute-start | bytes 663560 | tf_op jit(solution)/shard_map/ppermute | solution.py:24
  127.0 3.4 %fusion.27 = (f32[1,1536,144]{1,2,0:T(8,128)}, f32[1,1536,144]{1,2,0:T(8,128)}) fusion(f32[1,1536,144]{1,2,0:T(8,128)S(1)} %copy-done.7, f32[1,1536,144]{1,2,0:T(8,128)S(1)} %copy-done.4, bf16[144,384]{1,0:T(8,128)(2,1)S(1)} %get-tuple-element.42, bf16[144,384]{1,0:T(8,128)(2,1)S(1)} %collective-permute-done.29, ...), kind=kOutput, calls=%fused_computation.44 | convolution fusion | flops 684933120 | bytes 3987456 | tf_op jit(solution)/shard_map/dot_general | solution.py:186
  130.5 1.1 collective-permute-done.21
  131.6 6.1 %collective-permute-done.19 = bf16[24,4608]{1,0:T(8,128)(2,1)S(1)} collective-permute-done((bf16[24,4608]{1,0:T(8,128)(2,1)S(1)}, bf16[24,4608]{1,0:T(8,128)(2,1)S(1)}, u32[]{:S(2)}, u32[]{:S(2)}) %collective-permute-start.19) | collective-permute-done | bytes 221216 | tf_op jit(solution)/shard_map/ppermute | solution.py:24
  138.4 2.9 %fusion.5 = f32[1,144,4608]{2,1,0:T(8,128)} fusion(bf16[384,4608]{1,0:T(8,128)(2,1)S(1)} %constant_dynamic-update-slice_fusion.5, bf16[144,4608]{1,0:T(8,128)(2,1)S(1)} %collective-permute-done.25, bf16[144,4608]{1,0:T(8,128)(2,1)S(1)} %collective-permute-done.24, f32[1,144,4608]{2,1,0:T(8,128)S(1)} %copy-done.1, s32[]{:T(128)S(6)} %select_n.361), kind=kOutput, calls=%fused_computation.9 | convolution fusion | flops 514252800 | bytes 11698180 | tf_op jit(solution)/shard_map/dot_general | solution.py:165
  141.9 0.9 reshape.363
  (90 shorter events, 10.1 us)
Async XLA Ops:
  0.6 6.6 %copy-start.10 = (bf16[4,12,4608]{2,0,1:T(4,128)(2,1)S(1)}, bf16[4,12,4608]{2,0,1:T(4,128)(2,1)}, u32[]{:S(2)}) copy-start(bf16[4,12,4608]{2,0,1:T(4,128)(2,1)} %param.5) | copy-start | bytes 1327108
  3.6 30.1 %collective-permute-start = (bf16[144,4608]{1,0:T(8,128)(2,1)}, bf16[144,4608]{1,0:T(8,128)(2,1)S(1)}, u32[]{:S(2)}, u32[]{:S(2)}) collective-permute-start(bf16[144,4608]{1,0:T(8,128)(2,1)} %convert_bitcast_fusion), channel_id=1, source_target_pairs={{0,1},{1,2},{2,3},{3,0},{4,5},{5,6},{6,7},{7,4},{8,9},{9,10},{10,1... | collective-permute-start | bytes 3981320 | tf_op jit(solution)/shard_map/ppermute | solution.py:24
  5.8 28.0 %collective-permute-start.1 = (bf16[144,4608]{1,0:T(8,128)(2,1)}, bf16[144,4608]{1,0:T(8,128)(2,1)S(1)}, u32[]{:S(2)}, u32[]{:S(2)}) collective-permute-start(bf16[144,4608]{1,0:T(8,128)(2,1)} %convert_bitcast_fusion), channel_id=1, source_target_pairs={{0,3},{1,0},{2,1},{3,2},{4,7},{5,4},{6,5},{7,6},{8,11},{9,8},{10,9... | collective-permute-start | bytes 3981320 | tf_op jit(solution)/shard_map/ppermute | solution.py:24
  7.4 3.4 %copy-start.3 = (f32[1,1536,144]{1,2,0:T(8,128)S(1)}, f32[1,1536,144]{1,2,0:T(8,128)}, u32[]{:S(2)}) copy-start(f32[1,1536,144]{1,2,0:T(8,128)} %param.8) | copy-start | bytes 2654212
  7.4 4.3 %copy-start.6 = (f32[1,1536,144]{1,2,0:T(8,128)S(1)}, f32[1,1536,144]{1,2,0:T(8,128)}, u32[]{:S(2)}) copy-start(f32[1,1536,144]{1,2,0:T(8,128)} %param.9) | copy-start | bytes 2654212
  8.7 4.2 %collective-permute-start.7 = (bf16[2,12,4608]{2,0,1:T(2,128)(2,1)S(1)}, bf16[2,12,4608]{2,0,1:T(2,128)(2,1)S(1)}, u32[]{:S(2)}, u32[]{:S(2)}) collective-permute-start(bf16[2,12,4608]{2,0,1:T(2,128)(2,1)S(1)} %bitcast.99), channel_id=1, source_target_pairs={{0,32},{1,33},{2,34},{3,35},{4,36},{5,37},{6,38},{7,39},{8,40},{9,... | collective-permute-start | bytes 663560 | tf_op jit(solution)/shard_map/ppermute | solution.py:24
  12.5 8.5 %copy-start.8 = (bf16[144,1536]{1,0:T(8,128)(2,1)S(1)}, bf16[144,1536]{1,0:T(8,128)(2,1)}, u32[]{:S(2)}) copy-start(bf16[144,1536]{1,0:T(8,128)(2,1)} %get-tuple-element.24) | copy-start | bytes 1327108
  12.5 8.5 %copy-start.9 = (bf16[144,1536]{1,0:T(8,128)(2,1)S(1)}, bf16[144,1536]{1,0:T(8,128)(2,1)}, u32[]{:S(2)}) copy-start(bf16[144,1536]{1,0:T(8,128)(2,1)} %get-tuple-element.25) | copy-start | bytes 1327108
  12.5 8.5 %copy-start.11 = (bf16[144,1536]{1,0:T(8,128)(2,1)S(1)}, bf16[144,1536]{1,0:T(8,128)(2,1)}, u32[]{:S(2)}) copy-start(bf16[144,1536]{1,0:T(8,128)(2,1)} %convert_bitcast_fusion.1) | copy-start | bytes 1327108
  12.8 4.1 %copy-start.5 = (bf16[2,12,4608]{2,0,1:T(2,128)(2,1)}, bf16[2,12,4608]{2,0,1:T(2,128)(2,1)S(1)}, u32[]{:S(2)}) copy-start(bf16[2,12,4608]{2,0,1:T(2,128)(2,1)S(1)} %collective-permute-done.7) | copy-start | bytes 663556
  14.5 14.6 %collective-permute-start.9 = (bf16[24,4608]{1,0:T(8,128)(2,1)}, bf16[24,4608]{1,0:T(8,128)(2,1)S(1)}, u32[]{:S(2)}, u32[]{:S(2)}) collective-permute-start(bf16[24,4608]{1,0:T(8,128)(2,1)} %bitcast.89), channel_id=1, source_target_pairs={{0,80},{1,81},{2,82},{3,83},{4,84},{5,85},{6,86},{7,87},{8,88},{9,... | collective-permute-start | bytes 663560 | tf_op jit(solution)/shard_map/ppermute | solution.py:24
  17.0 12.9 %collective-permute-start.8 = (bf16[24,4608]{1,0:T(8,128)(2,1)}, bf16[24,4608]{1,0:T(8,128)(2,1)S(1)}, u32[]{:S(2)}, u32[]{:S(2)}) collective-permute-start(bf16[24,4608]{1,0:T(8,128)(2,1)} %bitcast.89), channel_id=1, source_target_pairs={{0,64},{1,65},{2,66},{3,67},{4,68},{5,69},{6,70},{7,71},{8,72},{9,... | collective-permute-start | bytes 663560 | tf_op jit(solution)/shard_map/ppermute | solution.py:24
  19.3 9.8 %collective-permute-start.10 = (bf16[24,4608]{1,0:T(8,128)(2,1)}, bf16[24,4608]{1,0:T(8,128)(2,1)}, u32[]{:S(2)}, u32[]{:S(2)}) collective-permute-start(bf16[24,4608]{1,0:T(8,128)(2,1)} %bitcast.88), channel_id=1, source_target_pairs={{0,16},{1,17},{2,18},{3,19},{4,20},{5,21},{6,22},{7,23},{8,24},{9,... | collective-permute-start | bytes 663560 | tf_op jit(solution)/shard_map/ppermute | solution.py:24
  24.4 10.8 %copy-start.2 = (bf16[432,1536]{1,0:T(8,128)(2,1)S(1)}, bf16[432,1536]{1,0:T(8,128)(2,1)}, u32[]{:S(2)}) copy-start(bf16[432,1536]{1,0:T(8,128)(2,1)} %fusion.13) | copy-start | bytes 3981316
  31.0 17.9 %collective-permute-start.11 = (bf16[96,4608]{1,0:T(8,128)(2,1)S(1)}, bf16[96,4608]{1,0:T(8,128)(2,1)S(1)}, u32[]{:S(2)}, u32[]{:S(2)}) collective-permute-start(bf16[96,4608]{1,0:T(8,128)(2,1)S(1)} %pad_maximum_fusion), channel_id=1, source_target_pairs={{0,4},{1,5},{2,6},{3,7},{4,8},{5,9},{6,10},{7,11},{8,12},{9,13},{1... | collective-permute-start | bytes 2654216 | tf_op jit(solution)/shard_map/ppermute | solution.py:24
  31.1 20.4 %collective-permute-start.12 = (bf16[96,4608]{1,0:T(8,128)(2,1)S(1)}, bf16[96,4608]{1,0:T(8,128)(2,1)S(1)}, u32[]{:S(2)}, u32[]{:S(2)}) collective-permute-start(bf16[96,4608]{1,0:T(8,128)(2,1)S(1)} %pad_maximum_fusion), channel_id=1, source_target_pairs={{0,12},{1,13},{2,14},{3,15},{4,0},{5,1},{6,2},{7,3},{8,4},{9,5},{1... | collective-permute-start | bytes 2654216 | tf_op jit(solution)/shard_map/ppermute | solution.py:24
  33.8 38.0 %collective-permute-start.5 = (bf16[72,4608]{1,0:T(8,128)(2,1)S(1)}, bf16[72,4608]{1,0:T(8,128)(2,1)S(1)}, u32[]{:S(2)}, u32[]{:S(2)}) collective-permute-start(bf16[72,4608]{1,0:T(8,128)(2,1)S(1)} %slice.128), channel_id=1, source_target_pairs={{0,1},{1,2},{2,3},{3,0},{4,5},{5,6},{6,7},{7,4},{8,9},{9,10},{10,1... | collective-permute-start | bytes 1990664 | tf_op jit(solution)/shard_map/ppermute | solution.py:24
  35.3 22.4 %collective-permute-start.4 = (bf16[432,384]{1,0:T(8,128)(2,1)S(1)}, bf16[432,384]{1,0:T(8,128)(2,1)S(1)}, u32[]{:S(2)}, u32[]{:S(2)}) collective-permute-start(bf16[432,384]{1,0:T(8,128)(2,1)S(1)} %get-tuple-element.30), channel_id=1, source_target_pairs={{0,2},{1,3},{2,0},{3,1},{4,6},{5,7},{6,4},{7,5},{8,10},{9,11},{10,... | collective-permute-start | bytes 995336 | tf_op jit(solution)/shard_map/ppermute | solution.py:24
  38.0 19.7 %collective-permute-start.3 = (bf16[432,384]{1,0:T(8,128)(2,1)S(1)}, bf16[432,384]{1,0:T(8,128)(2,1)S(1)}, u32[]{:S(2)}, u32[]{:S(2)}) collective-permute-start(bf16[432,384]{1,0:T(8,128)(2,1)S(1)} %get-tuple-element.31), channel_id=1, source_target_pairs={{0,3},{1,0},{2,1},{3,2},{4,7},{5,4},{6,5},{7,6},{8,11},{9,8},{10,9... | collective-permute-start | bytes 995336 | tf_op jit(solution)/shard_map/ppermute | solution.py:24
  48.9 13.6 %collective-permute-start.2 = (bf16[432,384]{1,0:T(8,128)(2,1)S(1)}, bf16[432,384]{1,0:T(8,128)(2,1)S(1)}, u32[]{:S(2)}, u32[]{:S(2)}) collective-permute-start(bf16[432,384]{1,0:T(8,128)(2,1)S(1)} %get-tuple-element.28), channel_id=1, source_target_pairs={{0,1},{1,2},{2,3},{3,0},{4,5},{5,6},{6,7},{7,4},{8,9},{9,10},{10,1... | collective-permute-start | bytes 995336 | tf_op jit(solution)/shard_map/ppermute | solution.py:24
  51.5 11.2 %collective-permute-start.13 = (bf16[48,4608]{1,0:T(8,128)(2,1)S(1)}, bf16[48,4608]{1,0:T(8,128)(2,1)S(1)}, u32[]{:S(2)}, u32[]{:S(2)}) collective-permute-start(bf16[48,4608]{1,0:T(8,128)(2,1)S(1)} %slice.136), channel_id=1, source_target_pairs={{0,4},{1,5},{2,6},{3,7},{4,8},{5,9},{6,10},{7,11},{8,12},{9,13},{1... | collective-permute-start | bytes 1327112 | tf_op jit(solution)/shard_map/ppermute | solution.py:24
  57.7 14.2 %collective-permute-start.6 = (bf16[72,4608]{1,0:T(8,128)(2,1)S(1)}, bf16[72,4608]{1,0:T(8,128)(2,1)S(1)}, u32[]{:S(2)}, u32[]{:S(2)}) collective-permute-start(bf16[72,4608]{1,0:T(8,128)(2,1)S(1)} %slice.129), channel_id=1, source_target_pairs={{0,3},{1,0},{2,1},{3,2},{4,7},{5,4},{6,5},{7,6},{8,11},{9,8},{10,9... | collective-permute-start | bytes 1990664 | tf_op jit(solution)/shard_map/ppermute | solution.py:24
  57.8 11.5 %collective-permute-start.14 = (bf16[48,4608]{1,0:T(8,128)(2,1)S(1)}, bf16[48,4608]{1,0:T(8,128)(2,1)S(1)}, u32[]{:S(2)}, u32[]{:S(2)}) collective-permute-start(bf16[48,4608]{1,0:T(8,128)(2,1)S(1)} %slice.137), channel_id=1, source_target_pairs={{0,12},{1,13},{2,14},{3,15},{4,0},{5,1},{6,2},{7,3},{8,4},{9,5},{1... | collective-permute-start | bytes 1327112 | tf_op jit(solution)/shard_map/ppermute | solution.py:24
  70.3 1.8 %copy-start = (f32[1,144,4608]{2,1,0:T(8,128)S(1)}, f32[1,144,4608]{2,1,0:T(8,128)}, u32[]{:S(2)}) copy-start(f32[1,144,4608]{2,1,0:T(8,128)} %param.6) | copy-start | bytes 7962628
  71.2 21.1 %collective-permute-start.22 = (bf16[72,4608]{1,0:T(8,128)(2,1)S(1)}, bf16[72,4608]{1,0:T(8,128)(2,1)S(1)}, u32[]{:S(2)}, u32[]{:S(2)}) collective-permute-start(bf16[72,4608]{1,0:T(8,128)(2,1)S(1)} %convolution_convert_fusion.1), channel_id=1, source_target_pairs={{0,1},{1,2},{2,3},{3,0},{4,5},{5,6},{6,7},{7,4},{8,9},{9,10},{10,1... | collective-permute-start | bytes 1990664 | tf_op jit(solution)/shard_map/ppermute | solution.py:24
  76.7 8.0 %collective-permute-start.17 = (bf16[48,4608]{1,0:T(8,128)(2,1)S(1)}, bf16[48,4608]{1,0:T(8,128)(2,1)S(1)}, u32[]{:S(2)}, u32[]{:S(2)}) collective-permute-start(bf16[48,4608]{1,0:T(8,128)(2,1)S(1)} %convolution_convert_fusion.2), channel_id=1, source_target_pairs={{0,12},{1,13},{2,14},{3,15},{4,0},{5,1},{6,2},{7,3},{8,4},{9,5},{1... | collective-permute-start | bytes 1327112 | tf_op jit(solution)/shard_map/ppermute | solution.py:24
  80.7 10.2 %collective-permute-start.15 = (bf16[48,4608]{1,0:T(8,128)(2,1)S(1)}, bf16[48,4608]{1,0:T(8,128)(2,1)S(1)}, u32[]{:S(2)}, u32[]{:S(2)}) collective-permute-start(bf16[48,4608]{1,0:T(8,128)(2,1)S(1)} %convolution_convert_fusion.3), channel_id=1, source_target_pairs={{0,4},{1,5},{2,6},{3,7},{4,8},{5,9},{6,10},{7,11},{8,12},{9,13},{1... | collective-permute-start | bytes 1327112 | tf_op jit(solution)/shard_map/ppermute | solution.py:24
  81.6 13.7 %collective-permute-start.23 = (bf16[72,4608]{1,0:T(8,128)(2,1)S(1)}, bf16[72,4608]{1,0:T(8,128)(2,1)S(1)}, u32[]{:S(2)}, u32[]{:S(2)}) collective-permute-start(bf16[72,4608]{1,0:T(8,128)(2,1)S(1)} %convolution_convert_fusion), channel_id=1, source_target_pairs={{0,3},{1,0},{2,1},{3,2},{4,7},{5,4},{6,5},{7,6},{8,11},{9,8},{10,9... | collective-permute-start | bytes 1990664 | tf_op jit(solution)/shard_map/ppermute | solution.py:24
  85.9 18.3 %collective-permute-start.18 = (bf16[96,4608]{1,0:T(8,128)(2,1)S(1)}, bf16[96,4608]{1,0:T(8,128)(2,1)S(1)}, u32[]{:S(2)}, u32[]{:S(2)}) collective-permute-start(bf16[96,4608]{1,0:T(8,128)(2,1)S(1)} %fusion.10), channel_id=1, source_target_pairs={{0,12},{1,13},{2,14},{3,15},{4,0},{5,1},{6,2},{7,3},{8,4},{9,5},{1... | collective-permute-start | bytes 2654216 | tf_op jit(solution)/shard_map/ppermute | solution.py:24
  92.1 14.5 %collective-permute-start.16 = (bf16[96,4608]{1,0:T(8,128)(2,1)S(1)}, bf16[96,4608]{1,0:T(8,128)(2,1)S(1)}, u32[]{:S(2)}, u32[]{:S(2)}) collective-permute-start(bf16[96,4608]{1,0:T(8,128)(2,1)S(1)} %fusion.9), channel_id=1, source_target_pairs={{0,4},{1,5},{2,6},{3,7},{4,8},{5,9},{6,10},{7,11},{8,12},{9,13},{1... | collective-permute-start | bytes 2654216 | tf_op jit(solution)/shard_map/ppermute | solution.py:24
  96.2 41.6 %collective-permute-start.24 = (bf16[144,4608]{1,0:T(8,128)(2,1)S(1)}, bf16[144,4608]{1,0:T(8,128)(2,1)S(1)}, u32[]{:S(2)}, u32[]{:S(2)}) collective-permute-start(bf16[144,4608]{1,0:T(8,128)(2,1)S(1)} %fusion.6), channel_id=1, source_target_pairs={{0,1},{1,2},{2,3},{3,0},{4,5},{5,6},{6,7},{7,4},{8,9},{9,10},{10,1... | collective-permute-start | bytes 3981320 | tf_op jit(solution)/shard_map/ppermute | solution.py:24
  97.3 40.5 %collective-permute-start.25 = (bf16[144,4608]{1,0:T(8,128)(2,1)S(1)}, bf16[144,4608]{1,0:T(8,128)(2,1)S(1)}, u32[]{:S(2)}, u32[]{:S(2)}) collective-permute-start(bf16[144,4608]{1,0:T(8,128)(2,1)S(1)} %fusion.7), channel_id=1, source_target_pairs={{0,3},{1,0},{2,1},{3,2},{4,7},{5,4},{6,5},{7,6},{8,11},{9,8},{10,9... | collective-permute-start | bytes 3981320 | tf_op jit(solution)/shard_map/ppermute | solution.py:24
  100.1 24.0 %collective-permute-start.29 = (bf16[144,384]{1,0:T(8,128)(2,1)S(1)}, bf16[144,384]{1,0:T(8,128)(2,1)S(1)}, u32[]{:S(2)}, u32[]{:S(2)}) collective-permute-start(bf16[144,384]{1,0:T(8,128)(2,1)S(1)} %get-tuple-element.43), channel_id=1, source_target_pairs={{0,2},{1,3},{2,0},{3,1},{4,6},{5,7},{6,4},{7,5},{8,10},{9,11},{10,... | collective-permute-start | bytes 331784 | tf_op jit(solution)/shard_map/ppermute | solution.py:24
  104.2 19.9 %collective-permute-start.28 = (bf16[144,384]{1,0:T(8,128)(2,1)S(1)}, bf16[144,384]{1,0:T(8,128)(2,1)S(1)}, u32[]{:S(2)}, u32[]{:S(2)}) collective-permute-start(bf16[144,384]{1,0:T(8,128)(2,1)S(1)} %get-tuple-element.44), channel_id=1, source_target_pairs={{0,3},{1,0},{2,1},{3,2},{4,7},{5,4},{6,5},{7,6},{8,11},{9,8},{10,9... | collective-permute-start | bytes 331784 | tf_op jit(solution)/shard_map/ppermute | solution.py:24
  106.6 20.4 %copy-start.4 = (f32[1,1536,144]{1,2,0:T(8,128)S(1)}, f32[1,1536,144]{1,2,0:T(8,128)}, u32[]{:S(2)}) copy-start(f32[1,1536,144]{1,2,0:T(8,128)} %param.8) | copy-start | bytes 2654212
  106.7 20.4 %copy-start.7 = (f32[1,1536,144]{1,2,0:T(8,128)S(1)}, f32[1,1536,144]{1,2,0:T(8,128)}, u32[]{:S(2)}) copy-start(f32[1,1536,144]{1,2,0:T(8,128)} %param.9) | copy-start | bytes 2654212
  106.7 20.1 %collective-permute-start.27 = (bf16[144,384]{1,0:T(8,128)(2,1)S(1)}, bf16[144,384]{1,0:T(8,128)(2,1)S(1)}, u32[]{:S(2)}, u32[]{:S(2)}) collective-permute-start(bf16[144,384]{1,0:T(8,128)(2,1)S(1)} %get-tuple-element.41), channel_id=1, source_target_pairs={{0,1},{1,2},{2,3},{3,0},{4,5},{5,6},{6,7},{7,4},{8,9},{9,10},{10,1... | collective-permute-start | bytes 331784 | tf_op jit(solution)/shard_map/ppermute | solution.py:24
  124.1 7.4 %collective-permute-start.21 = (bf16[24,4608]{1,0:T(8,128)(2,1)S(1)}, bf16[24,4608]{1,0:T(8,128)(2,1)S(1)}, u32[]{:S(2)}, u32[]{:S(2)}) collective-permute-start(bf16[24,4608]{1,0:T(8,128)(2,1)S(1)} %get-tuple-element.37), channel_id=1, source_target_pairs={{0,64},{1,65},{2,66},{3,67},{4,68},{5,69},{6,70},{7,71},{8,72},{9,... | collective-permute-start | bytes 663560 | tf_op jit(solution)/shard_map/ppermute | solution.py:24
  124.1 7.4 %collective-permute-start.20 = (bf16[24,4608]{1,0:T(8,128)(2,1)S(1)}, bf16[24,4608]{1,0:T(8,128)(2,1)S(1)}, u32[]{:S(2)}, u32[]{:S(2)}) collective-permute-start(bf16[24,4608]{1,0:T(8,128)(2,1)S(1)} %get-tuple-element.38), channel_id=1, source_target_pairs={{0,80},{1,81},{2,82},{3,83},{4,84},{5,85},{6,86},{7,87},{8,88},{9,... | collective-permute-start | bytes 663560 | tf_op jit(solution)/shard_map/ppermute | solution.py:24
  126.8 10.8 %collective-permute-start.19 = (bf16[24,4608]{1,0:T(8,128)(2,1)S(1)}, bf16[24,4608]{1,0:T(8,128)(2,1)S(1)}, u32[]{:S(2)}, u32[]{:S(2)}) collective-permute-start(bf16[24,4608]{1,0:T(8,128)(2,1)S(1)} %get-tuple-element.36), channel_id=1, source_target_pairs={{0,16},{1,17},{2,18},{3,19},{4,20},{5,21},{6,22},{7,23},{8,24},{9,... | collective-permute-start | bytes 663560 | tf_op jit(solution)/shard_map/ppermute | solution.py:24
  130.4 8.0 %copy-start.1 = (f32[1,144,4608]{2,1,0:T(8,128)S(1)}, f32[1,144,4608]{2,1,0:T(8,128)}, u32[]{:S(2)}) copy-start(f32[1,144,4608]{2,1,0:T(8,128)} %param.7) | copy-start | bytes 7962628
  137.9 3.4 %collective-permute-start.26 = (bf16[2,12,4608]{2,1,0:T(8,128)(2,1)S(1)}, bf16[2,12,4608]{2,1,0:T(8,128)(2,1)S(1)}, u32[]{:S(2)}, u32[]{:S(2)}) collective-permute-start(bf16[2,12,4608]{2,1,0:T(8,128)(2,1)S(1)} %slice.123), channel_id=1, source_target_pairs={{0,32},{1,33},{2,34},{3,35},{4,36},{5,37},{6,38},{7,39},{8,40},{9,... | collective-permute-start | bytes 663560 | tf_op jit(solution)/shard_map/ppermute | solution.py:24

commit v3 on v2

--- a/solution.py
+++ b/solution.py
@@ -48,27 +48,35 @@
 
 
 def ring_near(own, shift):
-    cut = own.shape[0] // 2
-    before, after = shift(own, 1), shift(own, -1)
-    return before, after, before[:cut], after[cut:]
-
-
-def ring_far(own, near, shift):
-    before, after, top, low = near
-    return jnp.concatenate([before, after, shift(top, 1), shift(low, -1), own], 0)
-
-
-def ring_sum(term, size, shift, wait=None):
-    cut = size // 2
-    top = shift(term(2, 0, cut).astype(half), 1)
-    low = shift(term(2, cut, size - cut).astype(half), -1)
-    if wait is not None:
-        top, low, wait = lax.optimization_barrier((top, low, wait))
-    up = term(1, 0, size) + jnp.pad(top.astype(jnp.float32), ((0, size - cut), (0, 0)))
-    down = term(0, 0, size) + jnp.pad(low.astype(jnp.float32), ((cut, 0), (0, 0)))
+    return shift(own, 1), shift(own, -1)
+
+
+def ring_far(near, shift, riders=None):
+    cut = near[0].shape[1] // 2
+    up, down = near[0][:, :cut], near[1][:, cut:]
+    if riders is None:
+        return shift(up, 1), shift(down, -1)
+    up = shift(jnp.concatenate([up, riders[1]], 1), 1)
+    down = shift(jnp.concatenate([down, riders[0]], 1), -1)
+    return up[:, :cut], down[:, :cut], up[:, cut:], down[:, cut:]
+
+
+def joined(own, near, far):
+    return jnp.concatenate([*near, jnp.concatenate(far, 1), own], 0)
+
+
+def ring_sum(term, width, shift, riders=None):
+    cut = width // 2
+    up, down = term(2, 0, cut).astype(half), term(2, cut, width).astype(half)
+    if riders is not None:
+        up = jnp.concatenate([up, riders[1]], 1)
+        down = jnp.concatenate([down, riders[0]], 1)
+    top, low = shift(up, 1), shift(down, -1)
+    up = term(1, 0, width) + jnp.pad(top[:, :cut].astype(jnp.float32), ((0, 0), (0, cut)))
+    down = term(0, 0, width) + jnp.pad(low[:, :cut].astype(jnp.float32), ((0, 0), (cut, 0)))
     up = shift(up.astype(half), 1)
     down = shift(down.astype(half), -1)
-    return up, down, wait
+    return up, down, (top[:, cut:], low[:, cut:])
 
 
 def body(gradient, eigenbasis, gram_sum, first_moment, second_moment):
@@ -87,6 +95,9 @@
     chip = jnp.concatenate([keep, other], 1)
     own_layer = pick((chip[0], chip[1]), xl)
     next_layer = pick((chip[1], chip[0]), xl)
+    own_layer, next_layer, old_first, old_second = lax.optimization_barrier(
+        (own_layer, next_layer, first_moment[0], second_moment[0])
+    )
     line = jnp.concatenate(
         [shift_x(next_layer, 1), shift_x(next_layer, -1), shift_x(own_layer, 2), own_layer], 0
     )
@@ -113,24 +124,23 @@
 
     first = first_moment[0].T
     second = second_moment[0].T
-    first_high = first.astype(half)
-    first_low = (first - first_high.astype(jnp.float32)).astype(half)
-    moments = jnp.concatenate([first_high, first_low, second.astype(half)], 0)
+    old_first = old_first.T
+    first_high = old_first.astype(half)
+    first_low = (old_first - first_high.astype(jnp.float32)).astype(half)
+    moments = jnp.concatenate([first_high, first_low, old_second.T.astype(half)], 0)
     moments = jnp.dot(moments, order, preferred_element_type=jnp.float32).astype(half)
-    moments, *tied = lax.optimization_barrier((moments, *near[2:]))
-    near = (*near[:2], *tied)
-    moments = [moments[:, k * count : (k + 1) * count] for k in range(4)]
-    moved = [
-        shift_own(moments[1], 1),
-        shift_own(moments[0], -1),
-        shift_own(moments[2], 2),
-        moments[3],
+    moments = moments.reshape(3, span, 4 * count)
+    moments = [
+        jnp.concatenate(list(moments[:, :, k * count : (k + 1) * count]), 1) for k in range(4)
     ]
-    moved = [value.reshape(3, span, count) for value in moved]
-    moved = jnp.concatenate(moved, 1).astype(jnp.float32)
-
-    basis = ring_far(own_basis, near, shift_own)
-    grads = ring_far(line, line_near, shift_row)
+    farthest, *near = lax.optimization_barrier((moments[2], *near))
+    top, low, moved_before, moved_after = ring_far(near, shift_own, moments[:2])
+    moved = [moved_before, moved_after, shift_own(farthest, 2), moments[3]]
+    moved = jnp.concatenate(moved, 0).astype(jnp.float32)
+    moved = [moved[:, k * count : (k + 1) * count] for k in range(3)]
+
+    basis = joined(own_basis, near, (top, low))
+    grads = joined(line, line_near, ring_far(line_near, shift_row))
     rotated = lax.dot_general(
         basis, grads, (((1,), (1,)), ((), ())), preferred_element_type=jnp.float32
     )
@@ -138,17 +148,17 @@
     new_second = 0.95 * moved[2] + 0.05 * rotated * rotated
     direction = (new_first / bias_fix / (jnp.sqrt(new_second / bias_fix) + 1e-08)).astype(half)
 
-    def update_term(place, start, size):
-        at = place * 8 * rows + start
+    def update_term(place, first, last):
+        at = place * 8 * rows
         return lax.dot_general(
-            direction[:, at : at + size],
-            basis,
+            direction[:, at : at + 8 * rows],
+            basis[:, first:last],
             (((0,), (0,)), ((), ())),
             preferred_element_type=jnp.float32,
         )
 
-    up, down, _ = ring_sum(update_term, 8 * rows, shift_row)
-    summed = update_term(3, 0, 8 * rows) + up.astype(jnp.float32) + down.astype(jnp.float32)
+    up, down, _ = ring_sum(update_term, width, shift_row)
+    summed = update_term(3, 0, width) + up.astype(jnp.float32) + down.astype(jnp.float32)
     summed = summed.reshape(4, 2 * rows, width)
     sent = summed.astype(half)
     far = shift_x(sent[2], 2)
@@ -157,19 +167,23 @@
     own_update = (summed[3] + far.astype(jnp.float32)).astype(half)
     next_update = (left.astype(jnp.float32) + right.astype(jnp.float32)).astype(half)
     update = jnp.stack([pick((own_update, next_update), xl), pick((next_update, own_update), xl)])
-    def gram_term(place, start, size):
+    def gram_term(place, first, last):
         y_at = (y + OFFSETS[place] * core + 4) % 4
         z_at = (z + OFFSETS[place] * (1 - core) + 4) % 4
-        column = ((xh * 4 + y_at) * 4 + z_at) * span + start
-        columns = lax.dynamic_slice_in_dim(grads, column, size, 1)
+        column = ((xh * 4 + y_at) * 4 + z_at) * span
+        columns = lax.dynamic_slice_in_dim(grads, column, span, 1)
         return lax.dot_general(
-            columns, grads, (((0,), (0,)), ((), ())), preferred_element_type=jnp.float32
+            columns,
+            grads[:, first:last],
+            (((0,), (0,)), ((), ())),
+            preferred_element_type=jnp.float32,
         )
 
     blocks = rotated.astype(half).reshape(4, span, count)
-    up, down, blocks = ring_sum(gram_term, span, shift_own, blocks)
+    up, down, (from_before, from_after) = ring_sum(gram_term, width, shift_own, blocks[:2])
+    owned = [from_before, from_after, shift_own(blocks[2], 2), blocks[3]]
     update, up, down = lax.optimization_barrier((update, up, down))
-    product = gram_term(3, 0, span) + up.astype(jnp.float32) + down.astype(jnp.float32)
+    product = gram_term(3, 0, width) + up.astype(jnp.float32) + down.astype(jnp.float32)
     new_gram = 0.95 * gram_sum[0] + 0.05 * product
 
     given = shift_core(update[:, rows:])
@@ -177,12 +191,6 @@
     update = jnp.stack([pick((update, given), core), pick((given, update), core)], 1)
     update = update.reshape(4, rows, width)
 
-    owned = [
-        shift_own(blocks[1], 1),
-        shift_own(blocks[0], -1),
-        shift_own(blocks[2], 2),
-        blocks[3],
-    ]
     owned = lax.dot_general(
         jnp.concatenate(owned, 1), order, (((1,), (1,)), ((), ())), preferred_element_type=jnp.float32
     )

time: 143 us -> 127 us (0.89)
  waiting for transfers between devices: 63.2 us -> 46.7 us
  matrix products: 22.7 us -> 20.2 us
  starting transfers between devices: 40.2 us -> 42.5 us
    ppermute x30 -> x26, waiting for transfers between devices: 63.2 us -> 46.7 us  [route(): return lax.ppermute(value, AXES, pairs)]
    concatenate x2 -> x6, other arithmetic: 1.24 us -> 4.17 us  [the longest x1 3.88 us: joined(): return jnp.concatenate([*near, jnp.concatenate(far, 1), own], 0)]
    ppermute x30 -> x26, starting transfers between devices: 40.2 us -> 42.5 us  [route(): return lax.ppermute(value, AXES, pairs)]
    unnamed x39 -> x21, local copies, waits for them, and re-layouts: 3.48 us -> 1.44 us
  transfers between devices with their start and end apart: 30 -> 26, of which waited for: 13 -> 10; matrix products, arithmetic and copies ran while one was open for 24% -> 21% of each run, Pallas kernels for 0% -> 0%
where the time goes in v3:
time: 127 us; the launch traced here: 126 us
  waiting for transfers between devices  46.7 us (37%)
  starting transfers between devices  42.5 us (33%)
  matrix products  20.2 us (16%)
  other arithmetic  9.82 us (8%)
  local copies, waits for them, and re-layouts  5.83 us (5%)
    ppermute x26, waiting for transfers between devices, route(): return lax.ppermute(value, AXES, pairs)  46.7 us
    ppermute x26, starting transfers between devices, route(): return lax.ppermute(value, AXES, pairs)  42.5 us
    dot_general x5, matrix products, gram_term(): lax.dot_general(columns, grads[:, first:last], (((0,), (0,)), ((), ())),...  6.09 us
    dot_general x5, matrix products, update_term(): lax.dot_general(direction[:, at:at + 8 * rows], basis[:, first:last], (((...  5.04 us
    concatenate x1, other arithmetic, joined(): return jnp.concatenate([*near, jnp.concatenate(far, 1), own], 0)  3.88 us
    dot_general x1, matrix products, body(): lax.dot_general(jnp.concatenate(owned, 1), order, (((1,), (1,)), ((), ())...  3.42 us
    dot_general x1, matrix products, body(): lax.dot_general(basis, grads, (((1,), (1,)), ((), ())), preferred_element...  3.36 us
    select_n x3, other arithmetic, pick(): return jnp.where(index == 0, pair[0], pair[1])  2.74 us
  transfers between devices with their start and end apart: 26, of which 10 were waited for; matrix products, arithmetic and copies ran while one was open for 21% of the time, Pallas kernels for 0%

profile of v3, /device:TPU:1, one launch (start us, length us, event | category | flops | bytes accessed | tf_op | source)
XLA Modules:
  0.0 126.3 jit_solution(3232647306968127063)
XLA Ops:
  0.6 1.2 reshape.347
  1.8 1.0 broadcast_select_fusion.1
  2.9 0.9 copy.28
  3.8 1.4 %collective-permute-start = (bf16[2,12,4608]{2,0,1:T(2,128)(2,1)}, bf16[2,12,4608]{2,0,1:T(2,128)(2,1)S(1)}, u32[]{:S(2)}, u32[]{:S(2)}) collective-permute-start(bf16[2,12,4608]{2,0,1:T(2,128)(2,1)} %bitcast.75), channel_id=1, source_target_pairs={{0,32},{1,33},{2,34},{3,35},{4,36},{5,37},{6,38},{7,39},{8,40},{9,... | collective-permute-start | bytes 663560 | tf_op jit(solution)/shard_map/ppermute | solution.py:24
  5.2 1.9 %convert_bitcast_fusion = bf16[144,4608]{1,0:T(8,128)(2,1)S(1)} fusion(f32[1,144,4608]{2,1,0:T(8,128)} %param.6), kind=kLoop, calls=%fused_computation.33 | loop fusion | flops 663552 | bytes 3981312 | tf_op jit(solution)/shard_map/convert_element_type | solution.py:106
  7.1 1.4 %collective-permute-start.1 = (bf16[144,4608]{1,0:T(8,128)(2,1)S(1)}, bf16[144,4608]{1,0:T(8,128)(2,1)S(1)}, u32[]{:S(2)}, u32[]{:S(2)}) collective-permute-start(bf16[144,4608]{1,0:T(8,128)(2,1)S(1)} %convert_bitcast_fusion), channel_id=1, source_target_pairs={{0,1},{1,2},{2,3},{3,0},{4,5},{5,6},{6,7},{7,4},{8,9},{9,10},{10,1... | collective-permute-start | bytes 3981320 | tf_op jit(solution)/shard_map/ppermute | solution.py:24
  8.5 1.5 %collective-permute-start.2 = (bf16[144,4608]{1,0:T(8,128)(2,1)S(1)}, bf16[144,4608]{1,0:T(8,128)(2,1)}, u32[]{:S(2)}, u32[]{:S(2)}) collective-permute-start(bf16[144,4608]{1,0:T(8,128)(2,1)S(1)} %convert_bitcast_fusion), channel_id=1, source_target_pairs={{0,3},{1,0},{2,1},{3,2},{4,7},{5,4},{6,5},{7,6},{8,11},{9,8},{10,9... | collective-permute-start | bytes 3981320 | tf_op jit(solution)/shard_map/ppermute | solution.py:24
  10.4 0.9 broadcast_select_fusion.2
  11.3 0.8 broadcast_select_fusion.3
  12.2 1.3 %collective-permute-start.6 = (bf16[24,4608]{1,0:T(8,128)(2,1)S(1)}, bf16[24,4608]{1,0:T(8,128)(2,1)S(1)}, u32[]{:S(2)}, u32[]{:S(2)}) collective-permute-start(bf16[24,4608]{1,0:T(8,128)(2,1)S(1)} %get-tuple-element.19), channel_id=1, source_target_pairs={{0,64},{1,65},{2,66},{3,67},{4,68},{5,69},{6,70},{7,71},{8,72},{9,... | collective-permute-start | bytes 663560 | tf_op jit(solution)/shard_map/ppermute | solution.py:24
  13.5 1.5 %collective-permute-start.7 = (bf16[24,4608]{1,0:T(8,128)(2,1)S(1)}, bf16[24,4608]{1,0:T(8,128)(2,1)S(1)}, u32[]{:S(2)}, u32[]{:S(2)}) collective-permute-start(bf16[24,4608]{1,0:T(8,128)(2,1)S(1)} %get-tuple-element.19), channel_id=1, source_target_pairs={{0,80},{1,81},{2,82},{3,83},{4,84},{5,85},{6,86},{7,87},{8,88},{9,... | collective-permute-start | bytes 663560 | tf_op jit(solution)/shard_map/ppermute | solution.py:24
  15.0 1.5 %collective-permute-start.8 = (bf16[24,4608]{1,0:T(8,128)(2,1)S(1)}, bf16[24,4608]{1,0:T(8,128)(2,1)S(1)}, u32[]{:S(2)}, u32[]{:S(2)}) collective-permute-start(bf16[24,4608]{1,0:T(8,128)(2,1)S(1)} %get-tuple-element.20), channel_id=1, source_target_pairs={{0,16},{1,17},{2,18},{3,19},{4,20},{5,21},{6,22},{7,23},{8,24},{9,... | collective-permute-start | bytes 663560 | tf_op jit(solution)/shard_map/ppermute | solution.py:24
  16.6 2.3 %fusion.10 = bf16[432,1536]{1,0:T(8,128)(2,1)S(1)} fusion(s32[1536]{0:T(1024)S(1)} %fusion.73, bf16[144,1536]{1,0:T(8,128)(2,1)S(1)} %convert_bitcast_fusion.1, bf16[144,1536]{1,0:T(8,128)(2,1)S(1)} %get-tuple-element.26, bf16[144,1536]{1,0:T(8,128)(2,1)S(1)} %get-tuple-element.27), kind=kOutput, calls=%fused_computation.19 | convolution fusion | flops 2045435904 | bytes 2660352 | tf_op jit(solution)/shard_map/dot_general | solution.py:131
  19.2 5.6 %collective-permute-done.8 = bf16[24,4608]{1,0:T(8,128)(2,1)S(1)} collective-permute-done((bf16[24,4608]{1,0:T(8,128)(2,1)S(1)}, bf16[24,4608]{1,0:T(8,128)(2,1)S(1)}, u32[]{:S(2)}, u32[]{:S(2)}) %collective-permute-start.8) | collective-permute-done | bytes 221216 | tf_op jit(solution)/shard_map/ppermute | solution.py:24
  24.9 2.9 %collective-permute-start.9 = (bf16[96,4608]{1,0:T(8,128)(2,1)S(1)}, bf16[96,4608]{1,0:T(8,128)(2,1)S(1)}, u32[]{:S(2)}, u32[]{:S(2)}) collective-permute-start(bf16[96,4608]{1,0:T(8,128)(2,1)S(1)} %constant_dynamic-update-slice_fusion), channel_id=1, source_target_pairs={{0,4},{1,5},{2,6},{3,7},{4,8},{5,9},{6,10},{7,11},{8,12},{9,13},{1... | collective-permute-start | bytes 2654216 | tf_op jit(solution)/shard_map/ppermute | solution.py:24
  27.8 2.2 %collective-permute-start.10 = (bf16[96,4608]{1,0:T(8,128)(2,1)S(1)}, bf16[96,4608]{1,0:T(8,128)(2,1)S(1)}, u32[]{:S(2)}, u32[]{:S(2)}) collective-permute-start(bf16[96,4608]{1,0:T(8,128)(2,1)S(1)} %constant_dynamic-update-slice_fusion), channel_id=1, source_target_pairs={{0,12},{1,13},{2,14},{3,15},{4,0},{5,1},{6,2},{7,3},{8,4},{9,5},{1... | collective-permute-start | bytes 2654216 | tf_op jit(solution)/shard_map/ppermute | solution.py:24
  30.2 1.1 slice.150
  31.4 2.7 %collective-permute-start.4 = (bf16[144,3456]{1,0:T(8,128)(2,1)S(1)}, bf16[144,3456]{1,0:T(8,128)(2,1)S(1)}, u32[]{:S(2)}, u32[]{:S(2)}) collective-permute-start(bf16[144,3456]{1,0:T(8,128)(2,1)S(1)} %pad_maximum_fusion.2), channel_id=1, source_target_pairs={{0,3},{1,0},{2,1},{3,2},{4,7},{5,4},{6,5},{7,6},{8,11},{9,8},{10,9... | collective-permute-start | bytes 2985992 | tf_op jit(solution)/shard_map/ppermute | solution.py:24
  34.2 11.9 %collective-permute-done.9 = bf16[96,4608]{1,0:T(8,128)(2,1)S(1)} collective-permute-done((bf16[96,4608]{1,0:T(8,128)(2,1)S(1)}, bf16[96,4608]{1,0:T(8,128)(2,1)S(1)}, u32[]{:S(2)}, u32[]{:S(2)}) %collective-permute-start.9) | collective-permute-done | bytes 884768 | tf_op jit(solution)/shard_map/ppermute | solution.py:24
  46.2 2.9 %collective-permute-start.12 = (bf16[96,2304]{1,0:T(8,128)(2,1)S(1)}, bf16[96,2304]{1,0:T(8,128)(2,1)S(1)}, u32[]{:S(2)}, u32[]{:S(2)}) collective-permute-start(bf16[96,2304]{1,0:T(8,128)(2,1)S(1)} %slice.192), channel_id=1, source_target_pairs={{0,12},{1,13},{2,14},{3,15},{4,0},{5,1},{6,2},{7,3},{8,4},{9,5},{1... | collective-permute-start | bytes 1327112 | tf_op jit(solution)/shard_map/ppermute | solution.py:24
  49.3 7.7 %collective-permute-done.11 = bf16[96,2304]{1,0:T(8,128)(2,1)S(1)} collective-permute-done((bf16[96,2304]{1,0:T(8,128)(2,1)S(1)}, bf16[96,2304]{1,0:T(8,128)(2,1)S(1)}, u32[]{:S(2)}, u32[]{:S(2)}) %collective-permute-start.11) | collective-permute-done | bytes 442400 | tf_op jit(solution)/shard_map/ppermute | solution.py:24
  57.0 2.0 %collective-permute-done.12 = bf16[96,2304]{1,0:T(8,128)(2,1)S(1)} collective-permute-done((bf16[96,2304]{1,0:T(8,128)(2,1)S(1)}, bf16[96,2304]{1,0:T(8,128)(2,1)S(1)}, u32[]{:S(2)}, u32[]{:S(2)}) %collective-permute-start.12) | collective-permute-done | bytes 442400 | tf_op jit(solution)/shard_map/ppermute | solution.py:24
  59.7 0.6 convolution_convert_fusion.1
  60.5 3.9 %pad_maximum_fusion = bf16[576,4608]{1,0:T(8,128)(2,1)S(1)} fusion(bf16[144,4608]{1,0:T(8,128)(2,1)S(1)} %convert_bitcast_fusion, bf16[144,2304]{1,0:T(8,128)(2,1)S(1)} %slice.190, bf16[144,2304]{1,0:T(8,128)(2,1)S(1)} %slice.189, bf16[144,4608]{1,0:T(8,128)(2,1)} %collective-permute-done.2, bf16[144,4608]{1,0:T(8,128)(2,1)S(1)} %collective-permute-done.1), kind=kLoop, calls=%fused_computation.12 | loop fusion | flops 26542080 | bytes 10616832 | tf_op jit(solution)/shard_map/concatenate | solution.py:65
  64.6 3.4 %fusion.104 = (bf16[576,384]{1,0:T(8,128)(2,1)S(1)}, bf16[576,384]{1,0:T(8,128)(2,1)S(1)}) fusion(f32[576,1152]{1,0:T(8,128)S(1)} %maximum_convert_fusion, bf16[576,4608]{1,0:T(8,128)(2,1)S(1)} %pad_maximum_fusion, bf16[384,4608]{1,0:T(8,128)(2,1)S(1)} %constant_dynamic-update-slice_fusion.4), kind=kOutput, calls=%fused_computation.210 | convolution fusion | flops 2041307136 | bytes 12386304 | tf_op jit(solution)/shard_map/dot_general | solution.py:144
  68.1 0.7 convolution_convert_fusion.3
  68.9 0.7 convolution_convert_fusion.2
  69.7 1.0 collective-permute-start.22
  70.7 3.4 %collective-permute-start.15 = (bf16[96,2304]{1,0:T(8,128)(2,1)S(1)}, bf16[96,2304]{1,0:T(8,128)(2,1)S(1)}, u32[]{:S(2)}, u32[]{:S(2)}) collective-permute-start(bf16[96,2304]{1,0:T(8,128)(2,1)S(1)} %convolution_convert_fusion.2), channel_id=1, source_target_pairs={{0,12},{1,13},{2,14},{3,15},{4,0},{5,1},{6,2},{7,3},{8,4},{9,5},{1... | collective-permute-start | bytes 1327112 | tf_op jit(solution)/shard_map/ppermute | solution.py:24
  74.7 3.5 %collective-permute-done.13 = bf16[96,2304]{1,0:T(8,128)(2,1)S(1)} collective-permute-done((bf16[96,2304]{1,0:T(8,128)(2,1)S(1)}, bf16[96,2304]{1,0:T(8,128)(2,1)S(1)}, u32[]{:S(2)}, u32[]{:S(2)}) %collective-permute-start.13) | collective-permute-done | bytes 442400 | tf_op jit(solution)/shard_map/ppermute | solution.py:24
  78.3 1.2 add_convert_fusion.1
  79.6 2.2 %collective-permute-done.15 = bf16[96,2304]{1,0:T(8,128)(2,1)S(1)} collective-permute-done((bf16[96,2304]{1,0:T(8,128)(2,1)S(1)}, bf16[96,2304]{1,0:T(8,128)(2,1)S(1)}, u32[]{:S(2)}, u32[]{:S(2)}) %collective-permute-start.15) | collective-permute-done | bytes 442400 | tf_op jit(solution)/shard_map/ppermute | solution.py:24
  81.8 1.1 add_convert_fusion
  82.9 3.2 %collective-permute-start.16 = (bf16[96,4608]{1,0:T(8,128)(2,1)S(1)}, bf16[96,4608]{1,0:T(8,128)(2,1)S(1)}, u32[]{:S(2)}, u32[]{:S(2)}) collective-permute-start(bf16[96,4608]{1,0:T(8,128)(2,1)S(1)} %add_convert_fusion), channel_id=1, source_target_pairs={{0,12},{1,13},{2,14},{3,15},{4,0},{5,1},{6,2},{7,3},{8,4},{9,5},{1... | collective-permute-start | bytes 2654216 | tf_op jit(solution)/shard_map/ppermute | solution.py:24
  86.2 1.2 fusion.53
  87.5 1.0 fusion.7
  88.5 3.3 %collective-permute-start.23 = (bf16[144,4608]{1,0:T(8,128)(2,1)S(1)}, bf16[144,4608]{1,0:T(8,128)(2,1)S(1)}, u32[]{:S(2)}, u32[]{:S(2)}) collective-permute-start(bf16[144,4608]{1,0:T(8,128)(2,1)S(1)} %fusion.7), channel_id=1, source_target_pairs={{0,3},{1,0},{2,1},{3,2},{4,7},{5,4},{6,5},{7,6},{8,11},{9,8},{10,9... | collective-permute-start | bytes 3981320 | tf_op jit(solution)/shard_map/ppermute | solution.py:24
  91.9 1.0 fusion.6
  93.0 8.3 %collective-permute-done.14 = bf16[96,4608]{1,0:T(8,128)(2,1)S(1)} collective-permute-done((bf16[96,4608]{1,0:T(8,128)(2,1)S(1)}, bf16[96,4608]{1,0:T(8,128)(2,1)S(1)}, u32[]{:S(2)}, u32[]{:S(2)}) %collective-permute-start.14) | collective-permute-done | bytes 884768 | tf_op jit(solution)/shard_map/ppermute | solution.py:24
  101.7 1.4 %collective-permute-start.17 = (bf16[24,4608]{1,0:T(8,128)(2,1)S(1)}, bf16[24,4608]{1,0:T(8,128)(2,1)S(1)}, u32[]{:S(2)}, u32[]{:S(2)}) collective-permute-start(bf16[24,4608]{1,0:T(8,128)(2,1)S(1)} %get-tuple-element.48), channel_id=1, source_target_pairs={{0,16},{1,17},{2,18},{3,19},{4,20},{5,21},{6,22},{7,23},{8,24},{9,... | collective-permute-start | bytes 663560 | tf_op jit(solution)/shard_map/ppermute | solution.py:24
  103.0 2.2 %collective-permute-start.18 = (bf16[24,4608]{1,0:T(8,128)(2,1)S(1)}, bf16[24,4608]{1,0:T(8,128)(2,1)S(1)}, u32[]{:S(2)}, u32[]{:S(2)}) collective-permute-start(bf16[24,4608]{1,0:T(8,128)(2,1)S(1)} %get-tuple-element.50), channel_id=1, source_target_pairs={{0,80},{1,81},{2,82},{3,83},{4,84},{5,85},{6,86},{7,87},{8,88},{9,... | collective-permute-start | bytes 663560 | tf_op jit(solution)/shard_map/ppermute | solution.py:24
  105.3 3.4 %fusion.28 = (f32[1,1536,144]{1,2,0:T(8,128)}, f32[1,1536,144]{1,2,0:T(8,128)}) fusion(f32[1,1536,144]{1,2,0:T(8,128)S(1)} %copy-done.2, f32[1,1536,144]{1,2,0:T(8,128)S(1)} %copy-done.1, bf16[144,384]{1,0:T(8,128)(2,1)S(1)} %get-tuple-element.54, bf16[144,384]{1,0:T(8,128)(2,1)S(1)} %collective-permute-done.25, bf16[144,384]{1,0:T(8,128)(2,1)S(1)} %slice-done, ...), kind=kOutput, calls=%fused_computation.48 | convolution fusion | flops 684933120 | bytes 3987456 | tf_op jit(solution)/shard_map/dot_general | solution.py:194
  108.7 1.7 %collective-permute-done.18 = bf16[24,4608]{1,0:T(8,128)(2,1)S(1)} collective-permute-done((bf16[24,4608]{1,0:T(8,128)(2,1)S(1)}, bf16[24,4608]{1,0:T(8,128)(2,1)S(1)}, u32[]{:S(2)}, u32[]{:S(2)}) %collective-permute-start.18) | collective-permute-done | bytes 221216 | tf_op jit(solution)/shard_map/ppermute | solution.py:24
  110.4 1.1 collective-permute-done.19
  111.7 2.5 %collective-permute-done.23 = bf16[144,4608]{1,0:T(8,128)(2,1)S(1)} collective-permute-done((bf16[144,4608]{1,0:T(8,128)(2,1)S(1)}, bf16[144,4608]{1,0:T(8,128)(2,1)S(1)}, u32[]{:S(2)}, u32[]{:S(2)}) %collective-permute-start.23) | collective-permute-done | bytes 1327136 | tf_op jit(solution)/shard_map/ppermute | solution.py:24
  114.3 7.5 %collective-permute-start.24 = (bf16[2,12,4608]{2,1,0:T(8,128)(2,1)S(1)}, bf16[2,12,4608]{2,1,0:T(8,128)(2,1)S(1)}, u32[]{:S(2)}, u32[]{:S(2)}) collective-permute-start(bf16[2,12,4608]{2,1,0:T(8,128)(2,1)S(1)} %slice.176), channel_id=1, source_target_pairs={{0,32},{1,33},{2,34},{3,35},{4,36},{5,37},{6,38},{7,39},{8,40},{9,... | collective-permute-start | bytes 663560 | tf_op jit(solution)/shard_map/ppermute | solution.py:24
  121.8 2.9 %fusion.5 = f32[1,144,4608]{2,1,0:T(8,128)} fusion(bf16[384,4608]{1,0:T(8,128)(2,1)S(1)} %constant_dynamic-update-slice_fusion.4, bf16[144,4608]{1,0:T(8,128)(2,1)S(1)} %collective-permute-done.23, bf16[144,4608]{1,0:T(8,128)(2,1)S(1)} %collective-permute-done.21, f32[1,144,4608]{2,1,0:T(8,128)S(1)} %copy-done, s32[]{:T(128)S(6)} %select_n.358), kind=kOutput, calls=%fused_computation.9 | convolution fusion | flops 514252800 | bytes 11698180 | tf_op jit(solution)/shard_map/dot_general | solution.py:175
  125.3 0.9 reshape.349
  (81 shorter events, 4.7 us)
Async XLA Ops:
  3.8 6.6 %collective-permute-start = (bf16[2,12,4608]{2,0,1:T(2,128)(2,1)}, bf16[2,12,4608]{2,0,1:T(2,128)(2,1)S(1)}, u32[]{:S(2)}, u32[]{:S(2)}) collective-permute-start(bf16[2,12,4608]{2,0,1:T(2,128)(2,1)} %bitcast.75), channel_id=1, source_target_pairs={{0,32},{1,33},{2,34},{3,35},{4,36},{5,37},{6,38},{7,39},{8,40},{9,... | collective-permute-start | bytes 663560 | tf_op jit(solution)/shard_map/ppermute | solution.py:24
  7.1 22.9 %collective-permute-start.1 = (bf16[144,4608]{1,0:T(8,128)(2,1)S(1)}, bf16[144,4608]{1,0:T(8,128)(2,1)S(1)}, u32[]{:S(2)}, u32[]{:S(2)}) collective-permute-start(bf16[144,4608]{1,0:T(8,128)(2,1)S(1)} %convert_bitcast_fusion), channel_id=1, source_target_pairs={{0,1},{1,2},{2,3},{3,0},{4,5},{5,6},{6,7},{7,4},{8,9},{9,10},{10,1... | collective-permute-start | bytes 3981320 | tf_op jit(solution)/shard_map/ppermute | solution.py:24
  8.5 21.5 %collective-permute-start.2 = (bf16[144,4608]{1,0:T(8,128)(2,1)S(1)}, bf16[144,4608]{1,0:T(8,128)(2,1)}, u32[]{:S(2)}, u32[]{:S(2)}) collective-permute-start(bf16[144,4608]{1,0:T(8,128)(2,1)S(1)} %convert_bitcast_fusion), channel_id=1, source_target_pairs={{0,3},{1,0},{2,1},{3,2},{4,7},{5,4},{6,5},{7,6},{8,11},{9,8},{10,9... | collective-permute-start | bytes 3981320 | tf_op jit(solution)/shard_map/ppermute | solution.py:24
  10.3 6.2 %copy-start.1 = (f32[1,1536,144]{1,2,0:T(8,128)S(1)}, f32[1,1536,144]{1,2,0:T(8,128)}, u32[]{:S(2)}) copy-start(f32[1,1536,144]{1,2,0:T(8,128)} %param.8) | copy-start | bytes 2654212
  10.4 6.2 %copy-start.2 = (f32[1,1536,144]{1,2,0:T(8,128)S(1)}, f32[1,1536,144]{1,2,0:T(8,128)}, u32[]{:S(2)}) copy-start(f32[1,1536,144]{1,2,0:T(8,128)} %param.9) | copy-start | bytes 2654212
  12.2 6.9 %collective-permute-start.6 = (bf16[24,4608]{1,0:T(8,128)(2,1)S(1)}, bf16[24,4608]{1,0:T(8,128)(2,1)S(1)}, u32[]{:S(2)}, u32[]{:S(2)}) collective-permute-start(bf16[24,4608]{1,0:T(8,128)(2,1)S(1)} %get-tuple-element.19), channel_id=1, source_target_pairs={{0,64},{1,65},{2,66},{3,67},{4,68},{5,69},{6,70},{7,71},{8,72},{9,... | collective-permute-start | bytes 663560 | tf_op jit(solution)/shard_map/ppermute | solution.py:24
  13.5 5.7 %collective-permute-start.7 = (bf16[24,4608]{1,0:T(8,128)(2,1)S(1)}, bf16[24,4608]{1,0:T(8,128)(2,1)S(1)}, u32[]{:S(2)}, u32[]{:S(2)}) collective-permute-start(bf16[24,4608]{1,0:T(8,128)(2,1)S(1)} %get-tuple-element.19), channel_id=1, source_target_pairs={{0,80},{1,81},{2,82},{3,83},{4,84},{5,85},{6,86},{7,87},{8,88},{9,... | collective-permute-start | bytes 663560 | tf_op jit(solution)/shard_map/ppermute | solution.py:24
  15.0 9.9 %collective-permute-start.8 = (bf16[24,4608]{1,0:T(8,128)(2,1)S(1)}, bf16[24,4608]{1,0:T(8,128)(2,1)S(1)}, u32[]{:S(2)}, u32[]{:S(2)}) collective-permute-start(bf16[24,4608]{1,0:T(8,128)(2,1)S(1)} %get-tuple-element.20), channel_id=1, source_target_pairs={{0,16},{1,17},{2,18},{3,19},{4,20},{5,21},{6,22},{7,23},{8,24},{9,... | collective-permute-start | bytes 663560 | tf_op jit(solution)/shard_map/ppermute | solution.py:24
  24.9 21.2 %collective-permute-start.9 = (bf16[96,4608]{1,0:T(8,128)(2,1)S(1)}, bf16[96,4608]{1,0:T(8,128)(2,1)S(1)}, u32[]{:S(2)}, u32[]{:S(2)}) collective-permute-start(bf16[96,4608]{1,0:T(8,128)(2,1)S(1)} %constant_dynamic-update-slice_fusion), channel_id=1, source_target_pairs={{0,4},{1,5},{2,6},{3,7},{4,8},{5,9},{6,10},{7,11},{8,12},{9,13},{1... | collective-permute-start | bytes 2654216 | tf_op jit(solution)/shard_map/ppermute | solution.py:24
  27.8 18.4 %collective-permute-start.10 = (bf16[96,4608]{1,0:T(8,128)(2,1)S(1)}, bf16[96,4608]{1,0:T(8,128)(2,1)S(1)}, u32[]{:S(2)}, u32[]{:S(2)}) collective-permute-start(bf16[96,4608]{1,0:T(8,128)(2,1)S(1)} %constant_dynamic-update-slice_fusion), channel_id=1, source_target_pairs={{0,12},{1,13},{2,14},{3,15},{4,0},{5,1},{6,2},{7,3},{8,4},{9,5},{1... | collective-permute-start | bytes 2654216 | tf_op jit(solution)/shard_map/ppermute | solution.py:24
  30.1 30.2 %collective-permute-start.3 = (bf16[144,3456]{1,0:T(8,128)(2,1)S(1)}, bf16[144,3456]{1,0:T(8,128)(2,1)S(1)}, u32[]{:S(2)}, u32[]{:S(2)}) collective-permute-start(bf16[144,3456]{1,0:T(8,128)(2,1)S(1)} %pad_maximum_fusion.1), channel_id=1, source_target_pairs={{0,1},{1,2},{2,3},{3,0},{4,5},{5,6},{6,7},{7,4},{8,9},{9,10},{10,1... | collective-permute-start | bytes 2985992 | tf_op jit(solution)/shard_map/ppermute | solution.py:24
  31.4 29.0 %collective-permute-start.4 = (bf16[144,3456]{1,0:T(8,128)(2,1)S(1)}, bf16[144,3456]{1,0:T(8,128)(2,1)S(1)}, u32[]{:S(2)}, u32[]{:S(2)}) collective-permute-start(bf16[144,3456]{1,0:T(8,128)(2,1)S(1)} %pad_maximum_fusion.2), channel_id=1, source_target_pairs={{0,3},{1,0},{2,1},{3,2},{4,7},{5,4},{6,5},{7,6},{8,11},{9,8},{10,9... | collective-permute-start | bytes 2985992 | tf_op jit(solution)/shard_map/ppermute | solution.py:24
  34.2 30.3 %collective-permute-start.5 = (bf16[144,1152]{1,0:T(8,128)(2,1)S(1)}, bf16[144,1152]{1,0:T(8,128)(2,1)S(1)}, u32[]{:S(2)}, u32[]{:S(2)}) collective-permute-start(bf16[144,1152]{1,0:T(8,128)(2,1)S(1)} %pad_maximum_fusion.8), channel_id=1, source_target_pairs={{0,2},{1,3},{2,0},{3,1},{4,6},{5,7},{6,4},{7,5},{8,10},{9,11},{10,... | collective-permute-start | bytes 995336 | tf_op jit(solution)/shard_map/ppermute | solution.py:24
  46.1 10.9 %collective-permute-start.11 = (bf16[96,2304]{1,0:T(8,128)(2,1)S(1)}, bf16[96,2304]{1,0:T(8,128)(2,1)S(1)}, u32[]{:S(2)}, u32[]{:S(2)}) collective-permute-start(bf16[96,2304]{1,0:T(8,128)(2,1)S(1)} %slice.191), channel_id=1, source_target_pairs={{0,4},{1,5},{2,6},{3,7},{4,8},{5,9},{6,10},{7,11},{8,12},{9,13},{1... | collective-permute-start | bytes 1327112 | tf_op jit(solution)/shard_map/ppermute | solution.py:24
  46.2 12.7 %collective-permute-start.12 = (bf16[96,2304]{1,0:T(8,128)(2,1)S(1)}, bf16[96,2304]{1,0:T(8,128)(2,1)S(1)}, u32[]{:S(2)}, u32[]{:S(2)}) collective-permute-start(bf16[96,2304]{1,0:T(8,128)(2,1)S(1)} %slice.192), channel_id=1, source_target_pairs={{0,12},{1,13},{2,14},{3,15},{4,0},{5,1},{6,2},{7,3},{8,4},{9,5},{1... | collective-permute-start | bytes 1327112 | tf_op jit(solution)/shard_map/ppermute | solution.py:24
  68.8 9.5 %collective-permute-start.13 = (bf16[96,2304]{1,0:T(8,128)(2,1)S(1)}, bf16[96,2304]{1,0:T(8,128)(2,1)S(1)}, u32[]{:S(2)}, u32[]{:S(2)}) collective-permute-start(bf16[96,2304]{1,0:T(8,128)(2,1)S(1)} %convolution_convert_fusion.3), channel_id=1, source_target_pairs={{0,4},{1,5},{2,6},{3,7},{4,8},{5,9},{6,10},{7,11},{8,12},{9,13},{1... | collective-permute-start | bytes 1327112 | tf_op jit(solution)/shard_map/ppermute | solution.py:24
  69.7 17.8 %collective-permute-start.22 = (bf16[144,2688]{1,0:T(8,128)(2,1)S(1)}, bf16[144,2688]{1,0:T(8,128)(2,1)S(1)}, u32[]{:S(2)}, u32[]{:S(2)}) collective-permute-start(bf16[144,2688]{1,0:T(8,128)(2,1)S(1)} %pad_maximum_fusion.4), channel_id=1, source_target_pairs={{0,3},{1,0},{2,1},{3,2},{4,7},{5,4},{6,5},{7,6},{8,11},{9,8},{10,9... | collective-permute-start | bytes 2322440 | tf_op jit(solution)/shard_map/ppermute | solution.py:24
  70.7 11.1 %collective-permute-start.15 = (bf16[96,2304]{1,0:T(8,128)(2,1)S(1)}, bf16[96,2304]{1,0:T(8,128)(2,1)S(1)}, u32[]{:S(2)}, u32[]{:S(2)}) collective-permute-start(bf16[96,2304]{1,0:T(8,128)(2,1)S(1)} %convolution_convert_fusion.2), channel_id=1, source_target_pairs={{0,12},{1,13},{2,14},{3,15},{4,0},{5,1},{6,2},{7,3},{8,4},{9,5},{1... | collective-permute-start | bytes 1327112 | tf_op jit(solution)/shard_map/ppermute | solution.py:24
  74.2 17.6 %collective-permute-start.20 = (bf16[144,2688]{1,0:T(8,128)(2,1)S(1)}, bf16[144,2688]{1,0:T(8,128)(2,1)S(1)}, u32[]{:S(2)}, u32[]{:S(2)}) collective-permute-start(bf16[144,2688]{1,0:T(8,128)(2,1)S(1)} %pad_maximum_fusion.3), channel_id=1, source_target_pairs={{0,1},{1,2},{2,3},{3,0},{4,5},{5,6},{6,7},{7,4},{8,9},{9,10},{10,1... | collective-permute-start | bytes 2322440 | tf_op jit(solution)/shard_map/ppermute | solution.py:24
  79.5 21.8 %collective-permute-start.14 = (bf16[96,4608]{1,0:T(8,128)(2,1)S(1)}, bf16[96,4608]{1,0:T(8,128)(2,1)S(1)}, u32[]{:S(2)}, u32[]{:S(2)}) collective-permute-start(bf16[96,4608]{1,0:T(8,128)(2,1)S(1)} %add_convert_fusion.1), channel_id=1, source_target_pairs={{0,4},{1,5},{2,6},{3,7},{4,8},{5,9},{6,10},{7,11},{8,12},{9,13},{1... | collective-permute-start | bytes 2654216 | tf_op jit(solution)/shard_map/ppermute | solution.py:24
  82.9 18.4 %collective-permute-start.16 = (bf16[96,4608]{1,0:T(8,128)(2,1)S(1)}, bf16[96,4608]{1,0:T(8,128)(2,1)S(1)}, u32[]{:S(2)}, u32[]{:S(2)}) collective-permute-start(bf16[96,4608]{1,0:T(8,128)(2,1)S(1)} %add_convert_fusion), channel_id=1, source_target_pairs={{0,12},{1,13},{2,14},{3,15},{4,0},{5,1},{6,2},{7,3},{8,4},{9,5},{1... | collective-permute-start | bytes 2654216 | tf_op jit(solution)/shard_map/ppermute | solution.py:24
  87.4 17.9 %collective-permute-start.25 = (bf16[144,384]{1,0:T(8,128)(2,1)S(1)}, bf16[144,384]{1,0:T(8,128)(2,1)S(1)}, u32[]{:S(2)}, u32[]{:S(2)}) collective-permute-start(bf16[144,384]{1,0:T(8,128)(2,1)S(1)} %get-tuple-element.53), channel_id=1, source_target_pairs={{0,2},{1,3},{2,0},{3,1},{4,6},{5,7},{6,4},{7,5},{8,10},{9,11},{10,... | collective-permute-start | bytes 331784 | tf_op jit(solution)/shard_map/ppermute | solution.py:24
  87.5 5.4 %copy-start.3 = (bf16[144,2688]{1,0:T(8,128)(2,1)}, bf16[144,2688]{1,0:T(8,128)(2,1)S(1)}, u32[]{:S(2)}) copy-start(bf16[144,2688]{1,0:T(8,128)(2,1)S(1)} %collective-permute-done.22) | copy-start | bytes 2322436
  88.5 25.7 %collective-permute-start.23 = (bf16[144,4608]{1,0:T(8,128)(2,1)S(1)}, bf16[144,4608]{1,0:T(8,128)(2,1)S(1)}, u32[]{:S(2)}, u32[]{:S(2)}) collective-permute-start(bf16[144,4608]{1,0:T(8,128)(2,1)S(1)} %fusion.7), channel_id=1, source_target_pairs={{0,3},{1,0},{2,1},{3,2},{4,7},{5,4},{6,5},{7,6},{8,11},{9,8},{10,9... | collective-permute-start | bytes 3981320 | tf_op jit(solution)/shard_map/ppermute | solution.py:24
  91.8 1.1 copy-start.4
  92.8 21.4 %collective-permute-start.21 = (bf16[144,4608]{1,0:T(8,128)(2,1)S(1)}, bf16[144,4608]{1,0:T(8,128)(2,1)S(1)}, u32[]{:S(2)}, u32[]{:S(2)}) collective-permute-start(bf16[144,4608]{1,0:T(8,128)(2,1)S(1)} %fusion.6), channel_id=1, source_target_pairs={{0,1},{1,2},{2,3},{3,0},{4,5},{5,6},{6,7},{7,4},{8,9},{9,10},{10,1... | collective-permute-start | bytes 3981320 | tf_op jit(solution)/shard_map/ppermute | solution.py:24
  92.9 12.3 %slice-start = ((bf16[144,2688]{1,0:T(8,128)(2,1)}), bf16[144,384]{1,0:T(8,128)(2,1)S(1)}, s32[]{:S(2)}) async-start(bf16[144,2688]{1,0:T(8,128)(2,1)} %copy-done.3), calls=%async_computation | async-start | bytes 221184 | tf_op jit(solution)/shard_map/slice | solution.py:79
  93.0 12.3 %slice-start.1 = ((bf16[144,2688]{1,0:T(8,128)(2,1)}), bf16[144,384]{1,0:T(8,128)(2,1)S(1)}, s32[]{:S(2)}) async-start(bf16[144,2688]{1,0:T(8,128)(2,1)} %copy-done.4), calls=%async_computation.1 | async-start | bytes 221184 | tf_op jit(solution)/shard_map/slice | solution.py:79
  101.7 7.0 %collective-permute-start.17 = (bf16[24,4608]{1,0:T(8,128)(2,1)S(1)}, bf16[24,4608]{1,0:T(8,128)(2,1)S(1)}, u32[]{:S(2)}, u32[]{:S(2)}) collective-permute-start(bf16[24,4608]{1,0:T(8,128)(2,1)S(1)} %get-tuple-element.48), channel_id=1, source_target_pairs={{0,16},{1,17},{2,18},{3,19},{4,20},{5,21},{6,22},{7,23},{8,24},{9,... | collective-permute-start | bytes 663560 | tf_op jit(solution)/shard_map/ppermute | solution.py:24
  103.0 7.4 %collective-permute-start.18 = (bf16[24,4608]{1,0:T(8,128)(2,1)S(1)}, bf16[24,4608]{1,0:T(8,128)(2,1)S(1)}, u32[]{:S(2)}, u32[]{:S(2)}) collective-permute-start(bf16[24,4608]{1,0:T(8,128)(2,1)S(1)} %get-tuple-element.50), channel_id=1, source_target_pairs={{0,80},{1,81},{2,82},{3,83},{4,84},{5,85},{6,86},{7,87},{8,88},{9,... | collective-permute-start | bytes 663560 | tf_op jit(solution)/shard_map/ppermute | solution.py:24
  105.3 6.3 %collective-permute-start.19 = (bf16[24,4608]{1,0:T(8,128)(2,1)S(1)}, bf16[24,4608]{1,0:T(8,128)(2,1)S(1)}, u32[]{:S(2)}, u32[]{:S(2)}) collective-permute-start(bf16[24,4608]{1,0:T(8,128)(2,1)S(1)} %get-tuple-element.49), channel_id=1, source_target_pairs={{0,64},{1,65},{2,66},{3,67},{4,68},{5,69},{6,70},{7,71},{8,72},{9,... | collective-permute-start | bytes 663560 | tf_op jit(solution)/shard_map/ppermute | solution.py:24
  108.7 13.1 %copy-start = (f32[1,144,4608]{2,1,0:T(8,128)S(1)}, f32[1,144,4608]{2,1,0:T(8,128)}, u32[]{:S(2)}) copy-start(f32[1,144,4608]{2,1,0:T(8,128)} %param.7) | copy-start | bytes 7962628
  114.3 10.4 %collective-permute-start.24 = (bf16[2,12,4608]{2,1,0:T(8,128)(2,1)S(1)}, bf16[2,12,4608]{2,1,0:T(8,128)(2,1)S(1)}, u32[]{:S(2)}, u32[]{:S(2)}) collective-permute-start(bf16[2,12,4608]{2,1,0:T(8,128)(2,1)S(1)} %slice.176), channel_id=1, source_target_pairs={{0,32},{1,33},{2,34},{3,35},{4,36},{5,37},{6,38},{7,39},{8,40},{9,... | collective-permute-start | bytes 663560 | tf_op jit(solution)/shard_map/ppermute | solution.py:24

commit v4 on v3

--- a/solution.py
+++ b/solution.py
@@ -139,7 +139,8 @@
     moved = jnp.concatenate(moved, 0).astype(jnp.float32)
     moved = [moved[:, k * count : (k + 1) * count] for k in range(3)]
 
-    basis = joined(own_basis, near, (top, low))
+    far = lax.optimization_barrier(jnp.concatenate([top, low], 1))
+    basis = jnp.concatenate([*near, far, own_basis], 0)
     grads = joined(line, line_near, ring_far(line_near, shift_row))
     rotated = lax.dot_general(
         basis, grads, (((1,), (1,)), ((), ())), preferred_element_type=jnp.float32

time: 127 us -> 125 us (0.984)
  other arithmetic: 9.82 us -> 8.33 us
    concatenate x1 -> x2, other arithmetic: 3.88 us -> 2.39 us  [the longest x1 2.3 us: body(): basis = jnp.concatenate([*near, far, own_basis], 0)]
  transfers between devices with their start and end apart: 26 -> 26, of which waited for: 10 -> 10; matrix products, arithmetic and copies ran while one was open for 21% -> 20% of each run, Pallas kernels for 0% -> 0%
where the time goes in v4:
time: 125 us
  waiting for transfers between devices  46.6 us (37%)
  starting transfers between devices  42.5 us (34%)
  matrix products  20.2 us (16%)
  other arithmetic  8.33 us (7%)
  local copies, waits for them, and re-layouts  5.83 us (5%)
  between operations  1.27 us (1%)
    ppermute x26, waiting for transfers between devices, route(): return lax.ppermute(value, AXES, pairs)  46.6 us
    ppermute x26, starting transfers between devices, route(): return lax.ppermute(value, AXES, pairs)  42.5 us
    dot_general x5, matrix products, gram_term(): lax.dot_general(columns, grads[:, first:last], (((0,), (0,)), ((), ())),...  6.09 us
    dot_general x5, matrix products, update_term(): lax.dot_general(direction[:, at:at + 8 * rows], basis[:, first:last], (((...  5.04 us
    dot_general x1, matrix products, body(): lax.dot_general(jnp.concatenate(owned, 1), order, (((1,), (1,)), ((), ())...  3.42 us
    dot_general x1, matrix products, body(): lax.dot_general(basis, grads, (((1,), (1,)), ((), ())), preferred_element...  3.36 us
    select_n x3, other arithmetic, pick(): return jnp.where(index == 0, pair[0], pair[1])  2.74 us
  transfers between devices with their start and end apart: 26, of which 10 were waited for; matrix products, arithmetic and copies ran while one was open for 20% of the time, Pallas kernels for 0%

profile of v4, /device:TPU:1, one launch (start us, length us, event | category | flops | bytes accessed | tf_op | source)
XLA Modules:
  0.0 124.8 jit_solution(15392759748689865845)
XLA Ops:
  0.6 1.2 reshape.347
  1.8 1.0 broadcast_select_fusion.1
  2.9 0.9 copy.28
  3.8 1.4 %collective-permute-start = (bf16[2,12,4608]{2,0,1:T(2,128)(2,1)}, bf16[2,12,4608]{2,0,1:T(2,128)(2,1)S(1)}, u32[]{:S(2)}, u32[]{:S(2)}) collective-permute-start(bf16[2,12,4608]{2,0,1:T(2,128)(2,1)} %bitcast.75), channel_id=1, source_target_pairs={{0,32},{1,33},{2,34},{3,35},{4,36},{5,37},{6,38},{7,39},{8,40},{9,... | collective-permute-start | bytes 663560 | tf_op jit(solution)/shard_map/ppermute | solution.py:24
  5.2 1.9 %convert_bitcast_fusion = bf16[144,4608]{1,0:T(8,128)(2,1)S(1)} fusion(f32[1,144,4608]{2,1,0:T(8,128)} %param.6), kind=kLoop, calls=%fused_computation.34 | loop fusion | flops 663552 | bytes 3981312 | tf_op jit(solution)/shard_map/convert_element_type | solution.py:106
  7.1 1.4 %collective-permute-start.1 = (bf16[144,4608]{1,0:T(8,128)(2,1)S(1)}, bf16[144,4608]{1,0:T(8,128)(2,1)S(1)}, u32[]{:S(2)}, u32[]{:S(2)}) collective-permute-start(bf16[144,4608]{1,0:T(8,128)(2,1)S(1)} %convert_bitcast_fusion), channel_id=1, source_target_pairs={{0,1},{1,2},{2,3},{3,0},{4,5},{5,6},{6,7},{7,4},{8,9},{9,10},{10,1... | collective-permute-start | bytes 3981320 | tf_op jit(solution)/shard_map/ppermute | solution.py:24
  8.5 1.5 %collective-permute-start.2 = (bf16[144,4608]{1,0:T(8,128)(2,1)S(1)}, bf16[144,4608]{1,0:T(8,128)(2,1)}, u32[]{:S(2)}, u32[]{:S(2)}) collective-permute-start(bf16[144,4608]{1,0:T(8,128)(2,1)S(1)} %convert_bitcast_fusion), channel_id=1, source_target_pairs={{0,3},{1,0},{2,1},{3,2},{4,7},{5,4},{6,5},{7,6},{8,11},{9,8},{10,9... | collective-permute-start | bytes 3981320 | tf_op jit(solution)/shard_map/ppermute | solution.py:24
  10.4 0.9 broadcast_select_fusion.2
  11.3 0.8 broadcast_select_fusion.3
  12.2 1.3 %collective-permute-start.6 = (bf16[24,4608]{1,0:T(8,128)(2,1)S(1)}, bf16[24,4608]{1,0:T(8,128)(2,1)S(1)}, u32[]{:S(2)}, u32[]{:S(2)}) collective-permute-start(bf16[24,4608]{1,0:T(8,128)(2,1)S(1)} %get-tuple-element.19), channel_id=1, source_target_pairs={{0,64},{1,65},{2,66},{3,67},{4,68},{5,69},{6,70},{7,71},{8,72},{9,... | collective-permute-start | bytes 663560 | tf_op jit(solution)/shard_map/ppermute | solution.py:24
  13.5 1.5 %collective-permute-start.7 = (bf16[24,4608]{1,0:T(8,128)(2,1)S(1)}, bf16[24,4608]{1,0:T(8,128)(2,1)S(1)}, u32[]{:S(2)}, u32[]{:S(2)}) collective-permute-start(bf16[24,4608]{1,0:T(8,128)(2,1)S(1)} %get-tuple-element.19), channel_id=1, source_target_pairs={{0,80},{1,81},{2,82},{3,83},{4,84},{5,85},{6,86},{7,87},{8,88},{9,... | collective-permute-start | bytes 663560 | tf_op jit(solution)/shard_map/ppermute | solution.py:24
  15.0 1.5 %collective-permute-start.8 = (bf16[24,4608]{1,0:T(8,128)(2,1)S(1)}, bf16[24,4608]{1,0:T(8,128)(2,1)S(1)}, u32[]{:S(2)}, u32[]{:S(2)}) collective-permute-start(bf16[24,4608]{1,0:T(8,128)(2,1)S(1)} %get-tuple-element.20), channel_id=1, source_target_pairs={{0,16},{1,17},{2,18},{3,19},{4,20},{5,21},{6,22},{7,23},{8,24},{9,... | collective-permute-start | bytes 663560 | tf_op jit(solution)/shard_map/ppermute | solution.py:24
  16.6 2.3 %fusion.10 = bf16[432,1536]{1,0:T(8,128)(2,1)S(1)} fusion(s32[1536]{0:T(1024)S(1)} %fusion.73, bf16[144,1536]{1,0:T(8,128)(2,1)S(1)} %convert_bitcast_fusion.1, bf16[144,1536]{1,0:T(8,128)(2,1)S(1)} %get-tuple-element.26, bf16[144,1536]{1,0:T(8,128)(2,1)S(1)} %get-tuple-element.27), kind=kOutput, calls=%fused_computation.19 | convolution fusion | flops 2045435904 | bytes 2660352 | tf_op jit(solution)/shard_map/dot_general | solution.py:131
  19.2 5.6 %collective-permute-done.8 = bf16[24,4608]{1,0:T(8,128)(2,1)S(1)} collective-permute-done((bf16[24,4608]{1,0:T(8,128)(2,1)S(1)}, bf16[24,4608]{1,0:T(8,128)(2,1)S(1)}, u32[]{:S(2)}, u32[]{:S(2)}) %collective-permute-start.8) | collective-permute-done | bytes 221216 | tf_op jit(solution)/shard_map/ppermute | solution.py:24
  24.9 2.9 %collective-permute-start.9 = (bf16[96,4608]{1,0:T(8,128)(2,1)S(1)}, bf16[96,4608]{1,0:T(8,128)(2,1)S(1)}, u32[]{:S(2)}, u32[]{:S(2)}) collective-permute-start(bf16[96,4608]{1,0:T(8,128)(2,1)S(1)} %constant_dynamic-update-slice_fusion), channel_id=1, source_target_pairs={{0,4},{1,5},{2,6},{3,7},{4,8},{5,9},{6,10},{7,11},{8,12},{9,13},{1... | collective-permute-start | bytes 2654216 | tf_op jit(solution)/shard_map/ppermute | solution.py:24
  27.8 2.2 %collective-permute-start.10 = (bf16[96,4608]{1,0:T(8,128)(2,1)S(1)}, bf16[96,4608]{1,0:T(8,128)(2,1)S(1)}, u32[]{:S(2)}, u32[]{:S(2)}) collective-permute-start(bf16[96,4608]{1,0:T(8,128)(2,1)S(1)} %constant_dynamic-update-slice_fusion), channel_id=1, source_target_pairs={{0,12},{1,13},{2,14},{3,15},{4,0},{5,1},{6,2},{7,3},{8,4},{9,5},{1... | collective-permute-start | bytes 2654216 | tf_op jit(solution)/shard_map/ppermute | solution.py:24
  30.2 1.1 slice.150
  31.4 2.7 %collective-permute-start.4 = (bf16[144,3456]{1,0:T(8,128)(2,1)S(1)}, bf16[144,3456]{1,0:T(8,128)(2,1)S(1)}, u32[]{:S(2)}, u32[]{:S(2)}) collective-permute-start(bf16[144,3456]{1,0:T(8,128)(2,1)S(1)} %pad_maximum_fusion.3), channel_id=1, source_target_pairs={{0,3},{1,0},{2,1},{3,2},{4,7},{5,4},{6,5},{7,6},{8,11},{9,8},{10,9... | collective-permute-start | bytes 2985992 | tf_op jit(solution)/shard_map/ppermute | solution.py:24
  34.2 11.9 %collective-permute-done.9 = bf16[96,4608]{1,0:T(8,128)(2,1)S(1)} collective-permute-done((bf16[96,4608]{1,0:T(8,128)(2,1)S(1)}, bf16[96,4608]{1,0:T(8,128)(2,1)S(1)}, u32[]{:S(2)}, u32[]{:S(2)}) %collective-permute-start.9) | collective-permute-done | bytes 884768 | tf_op jit(solution)/shard_map/ppermute | solution.py:24
  46.2 2.9 %collective-permute-start.12 = (bf16[96,2304]{1,0:T(8,128)(2,1)S(1)}, bf16[96,2304]{1,0:T(8,128)(2,1)S(1)}, u32[]{:S(2)}, u32[]{:S(2)}) collective-permute-start(bf16[96,2304]{1,0:T(8,128)(2,1)S(1)} %slice.192), channel_id=1, source_target_pairs={{0,12},{1,13},{2,14},{3,15},{4,0},{5,1},{6,2},{7,3},{8,4},{9,5},{1... | collective-permute-start | bytes 1327112 | tf_op jit(solution)/shard_map/ppermute | solution.py:24
  49.3 7.7 %collective-permute-done.11 = bf16[96,2304]{1,0:T(8,128)(2,1)S(1)} collective-permute-done((bf16[96,2304]{1,0:T(8,128)(2,1)S(1)}, bf16[96,2304]{1,0:T(8,128)(2,1)S(1)}, u32[]{:S(2)}, u32[]{:S(2)}) %collective-permute-start.11) | collective-permute-done | bytes 442400 | tf_op jit(solution)/shard_map/ppermute | solution.py:24
  57.0 2.0 %collective-permute-done.12 = bf16[96,2304]{1,0:T(8,128)(2,1)S(1)} collective-permute-done((bf16[96,2304]{1,0:T(8,128)(2,1)S(1)}, bf16[96,2304]{1,0:T(8,128)(2,1)S(1)}, u32[]{:S(2)}, u32[]{:S(2)}) %collective-permute-start.12) | collective-permute-done | bytes 442400 | tf_op jit(solution)/shard_map/ppermute | solution.py:24
  59.7 0.6 convolution_convert_fusion.1
  60.6 2.3 %pad_maximum_fusion = bf16[576,4608]{1,0:T(8,128)(2,1)S(1)} fusion(bf16[144,4608]{1,0:T(8,128)(2,1)S(1)} %convert_bitcast_fusion, bf16[144,4608]{1,0:T(8,128)(2,1)S(1)} %pad_maximum_fusion.1, bf16[144,4608]{1,0:T(8,128)(2,1)} %collective-permute-done.2, bf16[144,4608]{1,0:T(8,128)(2,1)S(1)} %collective-permute-done.1), kind=kLoop, calls=%fused_computation.12 | loop fusion | flops 21233664 | bytes 10616832 | tf_op jit(solution)/shard_map/concatenate | solution.py:143
  63.2 3.4 %fusion.104 = (bf16[576,384]{1,0:T(8,128)(2,1)S(1)}, bf16[576,384]{1,0:T(8,128)(2,1)S(1)}) fusion(f32[576,1152]{1,0:T(8,128)S(1)} %maximum_convert_fusion, bf16[576,4608]{1,0:T(8,128)(2,1)S(1)} %pad_maximum_fusion, bf16[384,4608]{1,0:T(8,128)(2,1)S(1)} %constant_dynamic-update-slice_fusion.4), kind=kOutput, calls=%fused_computation.211 | convolution fusion | flops 2041307136 | bytes 12386304 | tf_op jit(solution)/shard_map/dot_general | solution.py:145
  66.6 0.7 convolution_convert_fusion.3
  67.5 0.7 convolution_convert_fusion.2
  68.2 1.0 collective-permute-start.22
  69.2 3.4 %collective-permute-start.15 = (bf16[96,2304]{1,0:T(8,128)(2,1)S(1)}, bf16[96,2304]{1,0:T(8,128)(2,1)S(1)}, u32[]{:S(2)}, u32[]{:S(2)}) collective-permute-start(bf16[96,2304]{1,0:T(8,128)(2,1)S(1)} %convolution_convert_fusion.2), channel_id=1, source_target_pairs={{0,12},{1,13},{2,14},{3,15},{4,0},{5,1},{6,2},{7,3},{8,4},{9,5},{1... | collective-permute-start | bytes 1327112 | tf_op jit(solution)/shard_map/ppermute | solution.py:24
  73.3 3.5 %collective-permute-done.13 = bf16[96,2304]{1,0:T(8,128)(2,1)S(1)} collective-permute-done((bf16[96,2304]{1,0:T(8,128)(2,1)S(1)}, bf16[96,2304]{1,0:T(8,128)(2,1)S(1)}, u32[]{:S(2)}, u32[]{:S(2)}) %collective-permute-start.13) | collective-permute-done | bytes 442400 | tf_op jit(solution)/shard_map/ppermute | solution.py:24
  76.8 1.2 add_convert_fusion.1
  78.1 2.2 %collective-permute-done.15 = bf16[96,2304]{1,0:T(8,128)(2,1)S(1)} collective-permute-done((bf16[96,2304]{1,0:T(8,128)(2,1)S(1)}, bf16[96,2304]{1,0:T(8,128)(2,1)S(1)}, u32[]{:S(2)}, u32[]{:S(2)}) %collective-permute-start.15) | collective-permute-done | bytes 442400 | tf_op jit(solution)/shard_map/ppermute | solution.py:24
  80.3 1.1 add_convert_fusion
  81.5 3.2 %collective-permute-start.16 = (bf16[96,4608]{1,0:T(8,128)(2,1)S(1)}, bf16[96,4608]{1,0:T(8,128)(2,1)S(1)}, u32[]{:S(2)}, u32[]{:S(2)}) collective-permute-start(bf16[96,4608]{1,0:T(8,128)(2,1)S(1)} %add_convert_fusion), channel_id=1, source_target_pairs={{0,12},{1,13},{2,14},{3,15},{4,0},{5,1},{6,2},{7,3},{8,4},{9,5},{1... | collective-permute-start | bytes 2654216 | tf_op jit(solution)/shard_map/ppermute | solution.py:24
  84.7 1.2 fusion.53
  86.1 1.0 fusion.7
  87.0 3.3 %collective-permute-start.23 = (bf16[144,4608]{1,0:T(8,128)(2,1)S(1)}, bf16[144,4608]{1,0:T(8,128)(2,1)S(1)}, u32[]{:S(2)}, u32[]{:S(2)}) collective-permute-start(bf16[144,4608]{1,0:T(8,128)(2,1)S(1)} %fusion.7), channel_id=1, source_target_pairs={{0,3},{1,0},{2,1},{3,2},{4,7},{5,4},{6,5},{7,6},{8,11},{9,8},{10,9... | collective-permute-start | bytes 3981320 | tf_op jit(solution)/shard_map/ppermute | solution.py:24
  90.4 1.0 fusion.6
  91.5 8.3 %collective-permute-done.14 = bf16[96,4608]{1,0:T(8,128)(2,1)S(1)} collective-permute-done((bf16[96,4608]{1,0:T(8,128)(2,1)S(1)}, bf16[96,4608]{1,0:T(8,128)(2,1)S(1)}, u32[]{:S(2)}, u32[]{:S(2)}) %collective-permute-start.14) | collective-permute-done | bytes 884768 | tf_op jit(solution)/shard_map/ppermute | solution.py:24
  100.2 1.4 %collective-permute-start.17 = (bf16[24,4608]{1,0:T(8,128)(2,1)S(1)}, bf16[24,4608]{1,0:T(8,128)(2,1)S(1)}, u32[]{:S(2)}, u32[]{:S(2)}) collective-permute-start(bf16[24,4608]{1,0:T(8,128)(2,1)S(1)} %get-tuple-element.48), channel_id=1, source_target_pairs={{0,16},{1,17},{2,18},{3,19},{4,20},{5,21},{6,22},{7,23},{8,24},{9,... | collective-permute-start | bytes 663560 | tf_op jit(solution)/shard_map/ppermute | solution.py:24
  101.5 2.2 %collective-permute-start.18 = (bf16[24,4608]{1,0:T(8,128)(2,1)S(1)}, bf16[24,4608]{1,0:T(8,128)(2,1)S(1)}, u32[]{:S(2)}, u32[]{:S(2)}) collective-permute-start(bf16[24,4608]{1,0:T(8,128)(2,1)S(1)} %get-tuple-element.50), channel_id=1, source_target_pairs={{0,80},{1,81},{2,82},{3,83},{4,84},{5,85},{6,86},{7,87},{8,88},{9,... | collective-permute-start | bytes 663560 | tf_op jit(solution)/shard_map/ppermute | solution.py:24
  103.8 3.4 %fusion.28 = (f32[1,1536,144]{1,2,0:T(8,128)}, f32[1,1536,144]{1,2,0:T(8,128)}) fusion(f32[1,1536,144]{1,2,0:T(8,128)S(1)} %copy-done.2, f32[1,1536,144]{1,2,0:T(8,128)S(1)} %copy-done.1, bf16[144,384]{1,0:T(8,128)(2,1)S(1)} %get-tuple-element.54, bf16[144,384]{1,0:T(8,128)(2,1)S(1)} %collective-permute-done.25, bf16[144,384]{1,0:T(8,128)(2,1)S(1)} %slice-done, ...), kind=kOutput, calls=%fused_computation.49 | convolution fusion | flops 684933120 | bytes 3987456 | tf_op jit(solution)/shard_map/dot_general | solution.py:195
  107.2 1.7 %collective-permute-done.18 = bf16[24,4608]{1,0:T(8,128)(2,1)S(1)} collective-permute-done((bf16[24,4608]{1,0:T(8,128)(2,1)S(1)}, bf16[24,4608]{1,0:T(8,128)(2,1)S(1)}, u32[]{:S(2)}, u32[]{:S(2)}) %collective-permute-start.18) | collective-permute-done | bytes 221216 | tf_op jit(solution)/shard_map/ppermute | solution.py:24
  109.0 1.1 collective-permute-done.19
  110.3 2.5 %collective-permute-done.23 = bf16[144,4608]{1,0:T(8,128)(2,1)S(1)} collective-permute-done((bf16[144,4608]{1,0:T(8,128)(2,1)S(1)}, bf16[144,4608]{1,0:T(8,128)(2,1)S(1)}, u32[]{:S(2)}, u32[]{:S(2)}) %collective-permute-start.23) | collective-permute-done | bytes 1327136 | tf_op jit(solution)/shard_map/ppermute | solution.py:24
  112.8 7.5 %collective-permute-start.24 = (bf16[2,12,4608]{2,1,0:T(8,128)(2,1)S(1)}, bf16[2,12,4608]{2,1,0:T(8,128)(2,1)S(1)}, u32[]{:S(2)}, u32[]{:S(2)}) collective-permute-start(bf16[2,12,4608]{2,1,0:T(8,128)(2,1)S(1)} %slice.176), channel_id=1, source_target_pairs={{0,32},{1,33},{2,34},{3,35},{4,36},{5,37},{6,38},{7,39},{8,40},{9,... | collective-permute-start | bytes 663560 | tf_op jit(solution)/shard_map/ppermute | solution.py:24
  120.3 2.9 %fusion.5 = f32[1,144,4608]{2,1,0:T(8,128)} fusion(bf16[384,4608]{1,0:T(8,128)(2,1)S(1)} %constant_dynamic-update-slice_fusion.4, bf16[144,4608]{1,0:T(8,128)(2,1)S(1)} %collective-permute-done.23, bf16[144,4608]{1,0:T(8,128)(2,1)S(1)} %collective-permute-done.21, f32[1,144,4608]{2,1,0:T(8,128)S(1)} %copy-done, s32[]{:T(128)S(6)} %select_n.358), kind=kOutput, calls=%fused_computation.9 | convolution fusion | flops 514252800 | bytes 11698180 | tf_op jit(solution)/shard_map/dot_general | solution.py:176
  123.9 0.9 reshape.349
  (82 shorter events, 4.8 us)
Async XLA Ops:
  3.8 6.6 %collective-permute-start = (bf16[2,12,4608]{2,0,1:T(2,128)(2,1)}, bf16[2,12,4608]{2,0,1:T(2,128)(2,1)S(1)}, u32[]{:S(2)}, u32[]{:S(2)}) collective-permute-start(bf16[2,12,4608]{2,0,1:T(2,128)(2,1)} %bitcast.75), channel_id=1, source_target_pairs={{0,32},{1,33},{2,34},{3,35},{4,36},{5,37},{6,38},{7,39},{8,40},{9,... | collective-permute-start | bytes 663560 | tf_op jit(solution)/shard_map/ppermute | solution.py:24
  7.1 22.9 %collective-permute-start.1 = (bf16[144,4608]{1,0:T(8,128)(2,1)S(1)}, bf16[144,4608]{1,0:T(8,128)(2,1)S(1)}, u32[]{:S(2)}, u32[]{:S(2)}) collective-permute-start(bf16[144,4608]{1,0:T(8,128)(2,1)S(1)} %convert_bitcast_fusion), channel_id=1, source_target_pairs={{0,1},{1,2},{2,3},{3,0},{4,5},{5,6},{6,7},{7,4},{8,9},{9,10},{10,1... | collective-permute-start | bytes 3981320 | tf_op jit(solution)/shard_map/ppermute | solution.py:24
  8.5 21.5 %collective-permute-start.2 = (bf16[144,4608]{1,0:T(8,128)(2,1)S(1)}, bf16[144,4608]{1,0:T(8,128)(2,1)}, u32[]{:S(2)}, u32[]{:S(2)}) collective-permute-start(bf16[144,4608]{1,0:T(8,128)(2,1)S(1)} %convert_bitcast_fusion), channel_id=1, source_target_pairs={{0,3},{1,0},{2,1},{3,2},{4,7},{5,4},{6,5},{7,6},{8,11},{9,8},{10,9... | collective-permute-start | bytes 3981320 | tf_op jit(solution)/shard_map/ppermute | solution.py:24
  10.3 6.2 %copy-start.1 = (f32[1,1536,144]{1,2,0:T(8,128)S(1)}, f32[1,1536,144]{1,2,0:T(8,128)}, u32[]{:S(2)}) copy-start(f32[1,1536,144]{1,2,0:T(8,128)} %param.8) | copy-start | bytes 2654212
  10.4 6.2 %copy-start.2 = (f32[1,1536,144]{1,2,0:T(8,128)S(1)}, f32[1,1536,144]{1,2,0:T(8,128)}, u32[]{:S(2)}) copy-start(f32[1,1536,144]{1,2,0:T(8,128)} %param.9) | copy-start | bytes 2654212
  12.2 6.9 %collective-permute-start.6 = (bf16[24,4608]{1,0:T(8,128)(2,1)S(1)}, bf16[24,4608]{1,0:T(8,128)(2,1)S(1)}, u32[]{:S(2)}, u32[]{:S(2)}) collective-permute-start(bf16[24,4608]{1,0:T(8,128)(2,1)S(1)} %get-tuple-element.19), channel_id=1, source_target_pairs={{0,64},{1,65},{2,66},{3,67},{4,68},{5,69},{6,70},{7,71},{8,72},{9,... | collective-permute-start | bytes 663560 | tf_op jit(solution)/shard_map/ppermute | solution.py:24
  13.5 5.7 %collective-permute-start.7 = (bf16[24,4608]{1,0:T(8,128)(2,1)S(1)}, bf16[24,4608]{1,0:T(8,128)(2,1)S(1)}, u32[]{:S(2)}, u32[]{:S(2)}) collective-permute-start(bf16[24,4608]{1,0:T(8,128)(2,1)S(1)} %get-tuple-element.19), channel_id=1, source_target_pairs={{0,80},{1,81},{2,82},{3,83},{4,84},{5,85},{6,86},{7,87},{8,88},{9,... | collective-permute-start | bytes 663560 | tf_op jit(solution)/shard_map/ppermute | solution.py:24
  15.0 9.9 %collective-permute-start.8 = (bf16[24,4608]{1,0:T(8,128)(2,1)S(1)}, bf16[24,4608]{1,0:T(8,128)(2,1)S(1)}, u32[]{:S(2)}, u32[]{:S(2)}) collective-permute-start(bf16[24,4608]{1,0:T(8,128)(2,1)S(1)} %get-tuple-element.20), channel_id=1, source_target_pairs={{0,16},{1,17},{2,18},{3,19},{4,20},{5,21},{6,22},{7,23},{8,24},{9,... | collective-permute-start | bytes 663560 | tf_op jit(solution)/shard_map/ppermute | solution.py:24
  24.9 21.2 %collective-permute-start.9 = (bf16[96,4608]{1,0:T(8,128)(2,1)S(1)}, bf16[96,4608]{1,0:T(8,128)(2,1)S(1)}, u32[]{:S(2)}, u32[]{:S(2)}) collective-permute-start(bf16[96,4608]{1,0:T(8,128)(2,1)S(1)} %constant_dynamic-update-slice_fusion), channel_id=1, source_target_pairs={{0,4},{1,5},{2,6},{3,7},{4,8},{5,9},{6,10},{7,11},{8,12},{9,13},{1... | collective-permute-start | bytes 2654216 | tf_op jit(solution)/shard_map/ppermute | solution.py:24
  27.8 18.4 %collective-permute-start.10 = (bf16[96,4608]{1,0:T(8,128)(2,1)S(1)}, bf16[96,4608]{1,0:T(8,128)(2,1)S(1)}, u32[]{:S(2)}, u32[]{:S(2)}) collective-permute-start(bf16[96,4608]{1,0:T(8,128)(2,1)S(1)} %constant_dynamic-update-slice_fusion), channel_id=1, source_target_pairs={{0,12},{1,13},{2,14},{3,15},{4,0},{5,1},{6,2},{7,3},{8,4},{9,5},{1... | collective-permute-start | bytes 2654216 | tf_op jit(solution)/shard_map/ppermute | solution.py:24
  30.1 30.2 %collective-permute-start.3 = (bf16[144,3456]{1,0:T(8,128)(2,1)S(1)}, bf16[144,3456]{1,0:T(8,128)(2,1)S(1)}, u32[]{:S(2)}, u32[]{:S(2)}) collective-permute-start(bf16[144,3456]{1,0:T(8,128)(2,1)S(1)} %pad_maximum_fusion.2), channel_id=1, source_target_pairs={{0,1},{1,2},{2,3},{3,0},{4,5},{5,6},{6,7},{7,4},{8,9},{9,10},{10,1... | collective-permute-start | bytes 2985992 | tf_op jit(solution)/shard_map/ppermute | solution.py:24
  31.4 29.0 %collective-permute-start.4 = (bf16[144,3456]{1,0:T(8,128)(2,1)S(1)}, bf16[144,3456]{1,0:T(8,128)(2,1)S(1)}, u32[]{:S(2)}, u32[]{:S(2)}) collective-permute-start(bf16[144,3456]{1,0:T(8,128)(2,1)S(1)} %pad_maximum_fusion.3), channel_id=1, source_target_pairs={{0,3},{1,0},{2,1},{3,2},{4,7},{5,4},{6,5},{7,6},{8,11},{9,8},{10,9... | collective-permute-start | bytes 2985992 | tf_op jit(solution)/shard_map/ppermute | solution.py:24
  34.2 28.8 %collective-permute-start.5 = (bf16[144,1152]{1,0:T(8,128)(2,1)S(1)}, bf16[144,1152]{1,0:T(8,128)(2,1)S(1)}, u32[]{:S(2)}, u32[]{:S(2)}) collective-permute-start(bf16[144,1152]{1,0:T(8,128)(2,1)S(1)} %pad_maximum_fusion.9), channel_id=1, source_target_pairs={{0,2},{1,3},{2,0},{3,1},{4,6},{5,7},{6,4},{7,5},{8,10},{9,11},{10,... | collective-permute-start | bytes 995336 | tf_op jit(solution)/shard_map/ppermute | solution.py:24
  46.1 10.9 %collective-permute-start.11 = (bf16[96,2304]{1,0:T(8,128)(2,1)S(1)}, bf16[96,2304]{1,0:T(8,128)(2,1)S(1)}, u32[]{:S(2)}, u32[]{:S(2)}) collective-permute-start(bf16[96,2304]{1,0:T(8,128)(2,1)S(1)} %slice.191), channel_id=1, source_target_pairs={{0,4},{1,5},{2,6},{3,7},{4,8},{5,9},{6,10},{7,11},{8,12},{9,13},{1... | collective-permute-start | bytes 1327112 | tf_op jit(solution)/shard_map/ppermute | solution.py:24
  46.2 12.7 %collective-permute-start.12 = (bf16[96,2304]{1,0:T(8,128)(2,1)S(1)}, bf16[96,2304]{1,0:T(8,128)(2,1)S(1)}, u32[]{:S(2)}, u32[]{:S(2)}) collective-permute-start(bf16[96,2304]{1,0:T(8,128)(2,1)S(1)} %slice.192), channel_id=1, source_target_pairs={{0,12},{1,13},{2,14},{3,15},{4,0},{5,1},{6,2},{7,3},{8,4},{9,5},{1... | collective-permute-start | bytes 1327112 | tf_op jit(solution)/shard_map/ppermute | solution.py:24
  67.3 9.5 %collective-permute-start.13 = (bf16[96,2304]{1,0:T(8,128)(2,1)S(1)}, bf16[96,2304]{1,0:T(8,128)(2,1)S(1)}, u32[]{:S(2)}, u32[]{:S(2)}) collective-permute-start(bf16[96,2304]{1,0:T(8,128)(2,1)S(1)} %convolution_convert_fusion.3), channel_id=1, source_target_pairs={{0,4},{1,5},{2,6},{3,7},{4,8},{5,9},{6,10},{7,11},{8,12},{9,13},{1... | collective-permute-start | bytes 1327112 | tf_op jit(solution)/shard_map/ppermute | solution.py:24
  68.2 17.8 %collective-permute-start.22 = (bf16[144,2688]{1,0:T(8,128)(2,1)S(1)}, bf16[144,2688]{1,0:T(8,128)(2,1)S(1)}, u32[]{:S(2)}, u32[]{:S(2)}) collective-permute-start(bf16[144,2688]{1,0:T(8,128)(2,1)S(1)} %pad_maximum_fusion.5), channel_id=1, source_target_pairs={{0,3},{1,0},{2,1},{3,2},{4,7},{5,4},{6,5},{7,6},{8,11},{9,8},{10,9... | collective-permute-start | bytes 2322440 | tf_op jit(solution)/shard_map/ppermute | solution.py:24
  69.2 11.1 %collective-permute-start.15 = (bf16[96,2304]{1,0:T(8,128)(2,1)S(1)}, bf16[96,2304]{1,0:T(8,128)(2,1)S(1)}, u32[]{:S(2)}, u32[]{:S(2)}) collective-permute-start(bf16[96,2304]{1,0:T(8,128)(2,1)S(1)} %convolution_convert_fusion.2), channel_id=1, source_target_pairs={{0,12},{1,13},{2,14},{3,15},{4,0},{5,1},{6,2},{7,3},{8,4},{9,5},{1... | collective-permute-start | bytes 1327112 | tf_op jit(solution)/shard_map/ppermute | solution.py:24
  72.7 17.6 %collective-permute-start.20 = (bf16[144,2688]{1,0:T(8,128)(2,1)S(1)}, bf16[144,2688]{1,0:T(8,128)(2,1)S(1)}, u32[]{:S(2)}, u32[]{:S(2)}) collective-permute-start(bf16[144,2688]{1,0:T(8,128)(2,1)S(1)} %pad_maximum_fusion.4), channel_id=1, source_target_pairs={{0,1},{1,2},{2,3},{3,0},{4,5},{5,6},{6,7},{7,4},{8,9},{9,10},{10,1... | collective-permute-start | bytes 2322440 | tf_op jit(solution)/shard_map/ppermute | solution.py:24
  78.0 21.8 %collective-permute-start.14 = (bf16[96,4608]{1,0:T(8,128)(2,1)S(1)}, bf16[96,4608]{1,0:T(8,128)(2,1)S(1)}, u32[]{:S(2)}, u32[]{:S(2)}) collective-permute-start(bf16[96,4608]{1,0:T(8,128)(2,1)S(1)} %add_convert_fusion.1), channel_id=1, source_target_pairs={{0,4},{1,5},{2,6},{3,7},{4,8},{5,9},{6,10},{7,11},{8,12},{9,13},{1... | collective-permute-start | bytes 2654216 | tf_op jit(solution)/shard_map/ppermute | solution.py:24
  81.5 18.4 %collective-permute-start.16 = (bf16[96,4608]{1,0:T(8,128)(2,1)S(1)}, bf16[96,4608]{1,0:T(8,128)(2,1)S(1)}, u32[]{:S(2)}, u32[]{:S(2)}) collective-permute-start(bf16[96,4608]{1,0:T(8,128)(2,1)S(1)} %add_convert_fusion), channel_id=1, source_target_pairs={{0,12},{1,13},{2,14},{3,15},{4,0},{5,1},{6,2},{7,3},{8,4},{9,5},{1... | collective-permute-start | bytes 2654216 | tf_op jit(solution)/shard_map/ppermute | solution.py:24
  85.9 17.9 %collective-permute-start.25 = (bf16[144,384]{1,0:T(8,128)(2,1)S(1)}, bf16[144,384]{1,0:T(8,128)(2,1)S(1)}, u32[]{:S(2)}, u32[]{:S(2)}) collective-permute-start(bf16[144,384]{1,0:T(8,128)(2,1)S(1)} %get-tuple-element.53), channel_id=1, source_target_pairs={{0,2},{1,3},{2,0},{3,1},{4,6},{5,7},{6,4},{7,5},{8,10},{9,11},{10,... | collective-permute-start | bytes 331784 | tf_op jit(solution)/shard_map/ppermute | solution.py:24
  86.0 5.5 %copy-start.3 = (bf16[144,2688]{1,0:T(8,128)(2,1)}, bf16[144,2688]{1,0:T(8,128)(2,1)S(1)}, u32[]{:S(2)}) copy-start(bf16[144,2688]{1,0:T(8,128)(2,1)S(1)} %collective-permute-done.22) | copy-start | bytes 2322436
  87.0 25.7 %collective-permute-start.23 = (bf16[144,4608]{1,0:T(8,128)(2,1)S(1)}, bf16[144,4608]{1,0:T(8,128)(2,1)S(1)}, u32[]{:S(2)}, u32[]{:S(2)}) collective-permute-start(bf16[144,4608]{1,0:T(8,128)(2,1)S(1)} %fusion.7), channel_id=1, source_target_pairs={{0,3},{1,0},{2,1},{3,2},{4,7},{5,4},{6,5},{7,6},{8,11},{9,8},{10,9... | collective-permute-start | bytes 3981320 | tf_op jit(solution)/shard_map/ppermute | solution.py:24
  90.3 1.1 copy-start.4
  91.4 21.4 %collective-permute-start.21 = (bf16[144,4608]{1,0:T(8,128)(2,1)S(1)}, bf16[144,4608]{1,0:T(8,128)(2,1)S(1)}, u32[]{:S(2)}, u32[]{:S(2)}) collective-permute-start(bf16[144,4608]{1,0:T(8,128)(2,1)S(1)} %fusion.6), channel_id=1, source_target_pairs={{0,1},{1,2},{2,3},{3,0},{4,5},{5,6},{6,7},{7,4},{8,9},{9,10},{10,1... | collective-permute-start | bytes 3981320 | tf_op jit(solution)/shard_map/ppermute | solution.py:24
  91.5 12.3 %slice-start = ((bf16[144,2688]{1,0:T(8,128)(2,1)}), bf16[144,384]{1,0:T(8,128)(2,1)S(1)}, s32[]{:S(2)}) async-start(bf16[144,2688]{1,0:T(8,128)(2,1)} %copy-done.3), calls=%async_computation | async-start | bytes 221184 | tf_op jit(solution)/shard_map/slice | solution.py:79
  91.5 12.3 %slice-start.1 = ((bf16[144,2688]{1,0:T(8,128)(2,1)}), bf16[144,384]{1,0:T(8,128)(2,1)S(1)}, s32[]{:S(2)}) async-start(bf16[144,2688]{1,0:T(8,128)(2,1)} %copy-done.4), calls=%async_computation.1 | async-start | bytes 221184 | tf_op jit(solution)/shard_map/slice | solution.py:79
  100.2 7.1 %collective-permute-start.17 = (bf16[24,4608]{1,0:T(8,128)(2,1)S(1)}, bf16[24,4608]{1,0:T(8,128)(2,1)S(1)}, u32[]{:S(2)}, u32[]{:S(2)}) collective-permute-start(bf16[24,4608]{1,0:T(8,128)(2,1)S(1)} %get-tuple-element.48), channel_id=1, source_target_pairs={{0,16},{1,17},{2,18},{3,19},{4,20},{5,21},{6,22},{7,23},{8,24},{9,... | collective-permute-start | bytes 663560 | tf_op jit(solution)/shard_map/ppermute | solution.py:24
  101.5 7.4 %collective-permute-start.18 = (bf16[24,4608]{1,0:T(8,128)(2,1)S(1)}, bf16[24,4608]{1,0:T(8,128)(2,1)S(1)}, u32[]{:S(2)}, u32[]{:S(2)}) collective-permute-start(bf16[24,4608]{1,0:T(8,128)(2,1)S(1)} %get-tuple-element.50), channel_id=1, source_target_pairs={{0,80},{1,81},{2,82},{3,83},{4,84},{5,85},{6,86},{7,87},{8,88},{9,... | collective-permute-start | bytes 663560 | tf_op jit(solution)/shard_map/ppermute | solution.py:24
  103.8 6.3 %collective-permute-start.19 = (bf16[24,4608]{1,0:T(8,128)(2,1)S(1)}, bf16[24,4608]{1,0:T(8,128)(2,1)S(1)}, u32[]{:S(2)}, u32[]{:S(2)}) collective-permute-start(bf16[24,4608]{1,0:T(8,128)(2,1)S(1)} %get-tuple-element.49), channel_id=1, source_target_pairs={{0,64},{1,65},{2,66},{3,67},{4,68},{5,69},{6,70},{7,71},{8,72},{9,... | collective-permute-start | bytes 663560 | tf_op jit(solution)/shard_map/ppermute | solution.py:24
  107.2 13.1 %copy-start = (f32[1,144,4608]{2,1,0:T(8,128)S(1)}, f32[1,144,4608]{2,1,0:T(8,128)}, u32[]{:S(2)}) copy-start(f32[1,144,4608]{2,1,0:T(8,128)} %param.7) | copy-start | bytes 7962628
  112.8 10.4 %collective-permute-start.24 = (bf16[2,12,4608]{2,1,0:T(8,128)(2,1)S(1)}, bf16[2,12,4608]{2,1,0:T(8,128)(2,1)S(1)}, u32[]{:S(2)}, u32[]{:S(2)}) collective-permute-start(bf16[2,12,4608]{2,1,0:T(8,128)(2,1)S(1)} %slice.176), channel_id=1, source_target_pairs={{0,32},{1,33},{2,34},{3,35},{4,36},{5,37},{6,38},{7,39},{8,40},{9,... | collective-permute-start | bytes 663560 | tf_op jit(solution)/shard_map/ppermute | solution.py:24

commit v5 on v4

--- a/solution.py
+++ b/solution.py
@@ -65,18 +65,20 @@
     return jnp.concatenate([*near, jnp.concatenate(far, 1), own], 0)
 
 
-def ring_sum(term, width, shift, riders=None):
+def ring_sum(term, width, shift, riders=None, wait=None):
     cut = width // 2
     up, down = term(2, 0, cut).astype(half), term(2, cut, width).astype(half)
     if riders is not None:
         up = jnp.concatenate([up, riders[1]], 1)
         down = jnp.concatenate([down, riders[0]], 1)
     top, low = shift(up, 1), shift(down, -1)
+    if wait is not None:
+        top, low, wait = lax.optimization_barrier((top, low, wait))
     up = term(1, 0, width) + jnp.pad(top[:, :cut].astype(jnp.float32), ((0, 0), (0, cut)))
     down = term(0, 0, width) + jnp.pad(low[:, :cut].astype(jnp.float32), ((0, 0), (cut, 0)))
     up = shift(up.astype(half), 1)
     down = shift(down.astype(half), -1)
-    return up, down, (top[:, cut:], low[:, cut:])
+    return up, down, (top[:, cut:], low[:, cut:]), wait
 
 
 def body(gradient, eigenbasis, gram_sum, first_moment, second_moment):
@@ -158,7 +160,7 @@
             preferred_element_type=jnp.float32,
         )
 
-    up, down, _ = ring_sum(update_term, width, shift_row)
+    up, down, *_ = ring_sum(update_term, width, shift_row)
     summed = update_term(3, 0, width) + up.astype(jnp.float32) + down.astype(jnp.float32)
     summed = summed.reshape(4, 2 * rows, width)
     sent = summed.astype(half)
@@ -181,8 +183,10 @@
         )
 
     blocks = rotated.astype(half).reshape(4, span, count)
-    up, down, (from_before, from_after) = ring_sum(gram_term, width, shift_own, blocks[:2])
-    owned = [from_before, from_after, shift_own(blocks[2], 2), blocks[3]]
+    up, down, (from_before, from_after), farthest = ring_sum(
+        gram_term, width, shift_own, blocks[:2], blocks[2]
+    )
+    owned = [from_before, from_after, shift_own(farthest, 2), blocks[3]]
     update, up, down = lax.optimization_barrier((update, up, down))
     product = gram_term(3, 0, width) + up.astype(jnp.float32) + down.astype(jnp.float32)
     new_gram = 0.95 * gram_sum[0] + 0.05 * product

time: 125 us -> 125 us (level)
    ppermute x26, starting transfers between devices: 42.5 us -> 41.3 us  [route(): return lax.ppermute(value, AXES, pairs)]
  transfers between devices with their start and end apart: 26 -> 26, of which waited for: 10 -> 11; matrix products, arithmetic and copies ran while one was open for 20% -> 20% of each run, Pallas kernels for 0% -> 0%
where the time goes in v5:
time: 125 us
  waiting for transfers between devices  47.6 us (38%)
  starting transfers between devices  41.3 us (33%)
  matrix products  20.2 us (16%)
  other arithmetic  8.33 us (7%)
  local copies, waits for them, and re-layouts  5.83 us (5%)
  between operations  1.26 us (1%)
    ppermute x26, waiting for transfers between devices, route(): return lax.ppermute(value, AXES, pairs)  47.6 us
    ppermute x26, starting transfers between devices, route(): return lax.ppermute(value, AXES, pairs)  41.3 us
    dot_general x5, matrix products, gram_term(): lax.dot_general(columns, grads[:, first:last], (((0,), (0,)), ((), ())),...  6.07 us
    dot_general x5, matrix products, update_term(): lax.dot_general(direction[:, at:at + 8 * rows], basis[:, first:last], (((...  5.04 us
    dot_general x1, matrix products, body(): lax.dot_general(jnp.concatenate(owned, 1), order, (((1,), (1,)), ((), ())...  3.42 us
    dot_general x1, matrix products, body(): lax.dot_general(basis, grads, (((1,), (1,)), ((), ())), preferred_element...  3.36 us
    select_n x3, other arithmetic, pick(): return jnp.where(index == 0, pair[0], pair[1])  2.74 us
  transfers between devices with their start and end apart: 26, of which 11 were waited for; matrix products, arithmetic and copies ran while one was open for 20% of the time, Pallas kernels for 0%

profile of v5, /device:TPU:1, one launch (start us, length us, event | category | flops | bytes accessed | tf_op | source)
XLA Modules:
  0.0 124.5 jit_solution(6705972161500291587)
XLA Ops:
  0.6 1.2 reshape.347
  1.8 1.0 broadcast_select_fusion.1
  2.9 0.9 copy.28
  3.8 1.4 %collective-permute-start = (bf16[2,12,4608]{2,0,1:T(2,128)(2,1)}, bf16[2,12,4608]{2,0,1:T(2,128)(2,1)S(1)}, u32[]{:S(2)}, u32[]{:S(2)}) collective-permute-start(bf16[2,12,4608]{2,0,1:T(2,128)(2,1)} %bitcast.75), channel_id=1, source_target_pairs={{0,32},{1,33},{2,34},{3,35},{4,36},{5,37},{6,38},{7,39},{8,40},{9,... | collective-permute-start | bytes 663560 | tf_op jit(solution)/shard_map/ppermute | solution.py:24
  5.2 1.9 %convert_bitcast_fusion = bf16[144,4608]{1,0:T(8,128)(2,1)S(1)} fusion(f32[1,144,4608]{2,1,0:T(8,128)} %param.6), kind=kLoop, calls=%fused_computation.34 | loop fusion | flops 663552 | bytes 3981312 | tf_op jit(solution)/shard_map/convert_element_type | solution.py:108
  7.1 1.4 %collective-permute-start.1 = (bf16[144,4608]{1,0:T(8,128)(2,1)S(1)}, bf16[144,4608]{1,0:T(8,128)(2,1)S(1)}, u32[]{:S(2)}, u32[]{:S(2)}) collective-permute-start(bf16[144,4608]{1,0:T(8,128)(2,1)S(1)} %convert_bitcast_fusion), channel_id=1, source_target_pairs={{0,1},{1,2},{2,3},{3,0},{4,5},{5,6},{6,7},{7,4},{8,9},{9,10},{10,1... | collective-permute-start | bytes 3981320 | tf_op jit(solution)/shard_map/ppermute | solution.py:24
  8.5 1.5 %collective-permute-start.2 = (bf16[144,4608]{1,0:T(8,128)(2,1)S(1)}, bf16[144,4608]{1,0:T(8,128)(2,1)}, u32[]{:S(2)}, u32[]{:S(2)}) collective-permute-start(bf16[144,4608]{1,0:T(8,128)(2,1)S(1)} %convert_bitcast_fusion), channel_id=1, source_target_pairs={{0,3},{1,0},{2,1},{3,2},{4,7},{5,4},{6,5},{7,6},{8,11},{9,8},{10,9... | collective-permute-start | bytes 3981320 | tf_op jit(solution)/shard_map/ppermute | solution.py:24
  10.4 0.9 broadcast_select_fusion.2
  11.3 0.8 broadcast_select_fusion.3
  12.2 1.3 %collective-permute-start.6 = (bf16[24,4608]{1,0:T(8,128)(2,1)S(1)}, bf16[24,4608]{1,0:T(8,128)(2,1)S(1)}, u32[]{:S(2)}, u32[]{:S(2)}) collective-permute-start(bf16[24,4608]{1,0:T(8,128)(2,1)S(1)} %get-tuple-element.22), channel_id=1, source_target_pairs={{0,64},{1,65},{2,66},{3,67},{4,68},{5,69},{6,70},{7,71},{8,72},{9,... | collective-permute-start | bytes 663560 | tf_op jit(solution)/shard_map/ppermute | solution.py:24
  13.5 1.5 %collective-permute-start.7 = (bf16[24,4608]{1,0:T(8,128)(2,1)S(1)}, bf16[24,4608]{1,0:T(8,128)(2,1)S(1)}, u32[]{:S(2)}, u32[]{:S(2)}) collective-permute-start(bf16[24,4608]{1,0:T(8,128)(2,1)S(1)} %get-tuple-element.22), channel_id=1, source_target_pairs={{0,80},{1,81},{2,82},{3,83},{4,84},{5,85},{6,86},{7,87},{8,88},{9,... | collective-permute-start | bytes 663560 | tf_op jit(solution)/shard_map/ppermute | solution.py:24
  15.0 1.5 %collective-permute-start.8 = (bf16[24,4608]{1,0:T(8,128)(2,1)S(1)}, bf16[24,4608]{1,0:T(8,128)(2,1)S(1)}, u32[]{:S(2)}, u32[]{:S(2)}) collective-permute-start(bf16[24,4608]{1,0:T(8,128)(2,1)S(1)} %get-tuple-element.23), channel_id=1, source_target_pairs={{0,16},{1,17},{2,18},{3,19},{4,20},{5,21},{6,22},{7,23},{8,24},{9,... | collective-permute-start | bytes 663560 | tf_op jit(solution)/shard_map/ppermute | solution.py:24
  16.6 2.3 %fusion.10 = bf16[432,1536]{1,0:T(8,128)(2,1)S(1)} fusion(s32[1536]{0:T(1024)S(1)} %fusion.73, bf16[144,1536]{1,0:T(8,128)(2,1)S(1)} %convert_bitcast_fusion.1, bf16[144,1536]{1,0:T(8,128)(2,1)S(1)} %get-tuple-element.32, bf16[144,1536]{1,0:T(8,128)(2,1)S(1)} %get-tuple-element.33), kind=kOutput, calls=%fused_computation.19 | convolution fusion | flops 2045435904 | bytes 2660352 | tf_op jit(solution)/shard_map/dot_general | solution.py:133
  19.2 5.6 %collective-permute-done.8 = bf16[24,4608]{1,0:T(8,128)(2,1)S(1)} collective-permute-done((bf16[24,4608]{1,0:T(8,128)(2,1)S(1)}, bf16[24,4608]{1,0:T(8,128)(2,1)S(1)}, u32[]{:S(2)}, u32[]{:S(2)}) %collective-permute-start.8) | collective-permute-done | bytes 221216 | tf_op jit(solution)/shard_map/ppermute | solution.py:24
  24.9 2.9 %collective-permute-start.9 = (bf16[96,4608]{1,0:T(8,128)(2,1)S(1)}, bf16[96,4608]{1,0:T(8,128)(2,1)S(1)}, u32[]{:S(2)}, u32[]{:S(2)}) collective-permute-start(bf16[96,4608]{1,0:T(8,128)(2,1)S(1)} %constant_dynamic-update-slice_fusion), channel_id=1, source_target_pairs={{0,4},{1,5},{2,6},{3,7},{4,8},{5,9},{6,10},{7,11},{8,12},{9,13},{1... | collective-permute-start | bytes 2654216 | tf_op jit(solution)/shard_map/ppermute | solution.py:24
  27.8 2.2 %collective-permute-start.10 = (bf16[96,4608]{1,0:T(8,128)(2,1)S(1)}, bf16[96,4608]{1,0:T(8,128)(2,1)S(1)}, u32[]{:S(2)}, u32[]{:S(2)}) collective-permute-start(bf16[96,4608]{1,0:T(8,128)(2,1)S(1)} %constant_dynamic-update-slice_fusion), channel_id=1, source_target_pairs={{0,12},{1,13},{2,14},{3,15},{4,0},{5,1},{6,2},{7,3},{8,4},{9,5},{1... | collective-permute-start | bytes 2654216 | tf_op jit(solution)/shard_map/ppermute | solution.py:24
  30.2 1.1 slice.150
  31.4 2.7 %collective-permute-start.4 = (bf16[144,3456]{1,0:T(8,128)(2,1)S(1)}, bf16[144,3456]{1,0:T(8,128)(2,1)S(1)}, u32[]{:S(2)}, u32[]{:S(2)}) collective-permute-start(bf16[144,3456]{1,0:T(8,128)(2,1)S(1)} %pad_maximum_fusion.3), channel_id=1, source_target_pairs={{0,3},{1,0},{2,1},{3,2},{4,7},{5,4},{6,5},{7,6},{8,11},{9,8},{10,9... | collective-permute-start | bytes 2985992 | tf_op jit(solution)/shard_map/ppermute | solution.py:24
  34.2 11.9 %collective-permute-done.9 = bf16[96,4608]{1,0:T(8,128)(2,1)S(1)} collective-permute-done((bf16[96,4608]{1,0:T(8,128)(2,1)S(1)}, bf16[96,4608]{1,0:T(8,128)(2,1)S(1)}, u32[]{:S(2)}, u32[]{:S(2)}) %collective-permute-start.9) | collective-permute-done | bytes 884768 | tf_op jit(solution)/shard_map/ppermute | solution.py:24
  46.2 2.9 %collective-permute-start.12 = (bf16[96,2304]{1,0:T(8,128)(2,1)S(1)}, bf16[96,2304]{1,0:T(8,128)(2,1)S(1)}, u32[]{:S(2)}, u32[]{:S(2)}) collective-permute-start(bf16[96,2304]{1,0:T(8,128)(2,1)S(1)} %slice.192), channel_id=1, source_target_pairs={{0,12},{1,13},{2,14},{3,15},{4,0},{5,1},{6,2},{7,3},{8,4},{9,5},{1... | collective-permute-start | bytes 1327112 | tf_op jit(solution)/shard_map/ppermute | solution.py:24
  49.3 7.7 %collective-permute-done.11 = bf16[96,2304]{1,0:T(8,128)(2,1)S(1)} collective-permute-done((bf16[96,2304]{1,0:T(8,128)(2,1)S(1)}, bf16[96,2304]{1,0:T(8,128)(2,1)S(1)}, u32[]{:S(2)}, u32[]{:S(2)}) %collective-permute-start.11) | collective-permute-done | bytes 442400 | tf_op jit(solution)/shard_map/ppermute | solution.py:24
  57.0 2.0 %collective-permute-done.12 = bf16[96,2304]{1,0:T(8,128)(2,1)S(1)} collective-permute-done((bf16[96,2304]{1,0:T(8,128)(2,1)S(1)}, bf16[96,2304]{1,0:T(8,128)(2,1)S(1)}, u32[]{:S(2)}, u32[]{:S(2)}) %collective-permute-start.12) | collective-permute-done | bytes 442400 | tf_op jit(solution)/shard_map/ppermute | solution.py:24
  60.6 2.3 %pad_maximum_fusion = bf16[576,4608]{1,0:T(8,128)(2,1)S(1)} fusion(bf16[144,4608]{1,0:T(8,128)(2,1)S(1)} %convert_bitcast_fusion, bf16[144,4608]{1,0:T(8,128)(2,1)S(1)} %pad_maximum_fusion.1, bf16[144,4608]{1,0:T(8,128)(2,1)} %collective-permute-done.2, bf16[144,4608]{1,0:T(8,128)(2,1)S(1)} %collective-permute-done.1), kind=kLoop, calls=%fused_computation.12 | loop fusion | flops 21233664 | bytes 10616832 | tf_op jit(solution)/shard_map/concatenate | solution.py:145
  63.2 3.4 %fusion.104 = (bf16[576,384]{1,0:T(8,128)(2,1)S(1)}, bf16[576,384]{1,0:T(8,128)(2,1)S(1)}) fusion(f32[576,1152]{1,0:T(8,128)S(1)} %maximum_convert_fusion, bf16[576,4608]{1,0:T(8,128)(2,1)S(1)} %pad_maximum_fusion, bf16[384,4608]{1,0:T(8,128)(2,1)S(1)} %constant_dynamic-update-slice_fusion.4), kind=kOutput, calls=%fused_computation.211 | convolution fusion | flops 2041307136 | bytes 12386304 | tf_op jit(solution)/shard_map/dot_general | solution.py:147
  66.6 0.7 convolution_convert_fusion.3
  67.5 0.7 convolution_convert_fusion.2
  68.2 1.0 collective-permute-start.21
  69.2 3.4 %collective-permute-start.15 = (bf16[96,2304]{1,0:T(8,128)(2,1)S(1)}, bf16[96,2304]{1,0:T(8,128)(2,1)S(1)}, u32[]{:S(2)}, u32[]{:S(2)}) collective-permute-start(bf16[96,2304]{1,0:T(8,128)(2,1)S(1)} %convolution_convert_fusion.2), channel_id=1, source_target_pairs={{0,12},{1,13},{2,14},{3,15},{4,0},{5,1},{6,2},{7,3},{8,4},{9,5},{1... | collective-permute-start | bytes 1327112 | tf_op jit(solution)/shard_map/ppermute | solution.py:24
  73.3 3.5 %collective-permute-done.13 = bf16[96,2304]{1,0:T(8,128)(2,1)S(1)} collective-permute-done((bf16[96,2304]{1,0:T(8,128)(2,1)S(1)}, bf16[96,2304]{1,0:T(8,128)(2,1)S(1)}, u32[]{:S(2)}, u32[]{:S(2)}) %collective-permute-start.13) | collective-permute-done | bytes 442400 | tf_op jit(solution)/shard_map/ppermute | solution.py:24
  76.8 1.2 add_convert_fusion.1
  78.1 2.2 %collective-permute-done.15 = bf16[96,2304]{1,0:T(8,128)(2,1)S(1)} collective-permute-done((bf16[96,2304]{1,0:T(8,128)(2,1)S(1)}, bf16[96,2304]{1,0:T(8,128)(2,1)S(1)}, u32[]{:S(2)}, u32[]{:S(2)}) %collective-permute-start.15) | collective-permute-done | bytes 442400 | tf_op jit(solution)/shard_map/ppermute | solution.py:24
  80.3 1.1 add_convert_fusion
  81.5 3.2 %collective-permute-start.16 = (bf16[96,4608]{1,0:T(8,128)(2,1)S(1)}, bf16[96,4608]{1,0:T(8,128)(2,1)S(1)}, u32[]{:S(2)}, u32[]{:S(2)}) collective-permute-start(bf16[96,4608]{1,0:T(8,128)(2,1)S(1)} %add_convert_fusion), channel_id=1, source_target_pairs={{0,12},{1,13},{2,14},{3,15},{4,0},{5,1},{6,2},{7,3},{8,4},{9,5},{1... | collective-permute-start | bytes 2654216 | tf_op jit(solution)/shard_map/ppermute | solution.py:24
  84.7 1.2 fusion.53
  85.9 0.6 collective-permute-done.20
  87.2 1.0 fusion.7
  88.1 3.1 %collective-permute-start.23 = (bf16[144,4608]{1,0:T(8,128)(2,1)S(1)}, bf16[144,4608]{1,0:T(8,128)(2,1)S(1)}, u32[]{:S(2)}, u32[]{:S(2)}) collective-permute-start(bf16[144,4608]{1,0:T(8,128)(2,1)S(1)} %fusion.7), channel_id=1, source_target_pairs={{0,3},{1,0},{2,1},{3,2},{4,7},{5,4},{6,5},{7,6},{8,11},{9,8},{10,9... | collective-permute-start | bytes 3981320 | tf_op jit(solution)/shard_map/ppermute | solution.py:24
  91.2 1.0 fusion.6
  92.3 6.6 %collective-permute-done.14 = bf16[96,4608]{1,0:T(8,128)(2,1)S(1)} collective-permute-done((bf16[96,4608]{1,0:T(8,128)(2,1)S(1)}, bf16[96,4608]{1,0:T(8,128)(2,1)S(1)}, u32[]{:S(2)}, u32[]{:S(2)}) %collective-permute-start.14) | collective-permute-done | bytes 884768 | tf_op jit(solution)/shard_map/ppermute | solution.py:24
  99.2 1.1 collective-permute-start.17
  100.4 2.2 %collective-permute-start.18 = (bf16[24,4608]{1,0:T(8,128)(2,1)S(1)}, bf16[24,4608]{1,0:T(8,128)(2,1)S(1)}, u32[]{:S(2)}, u32[]{:S(2)}) collective-permute-start(bf16[24,4608]{1,0:T(8,128)(2,1)S(1)} %get-tuple-element.56), channel_id=1, source_target_pairs={{0,80},{1,81},{2,82},{3,83},{4,84},{5,85},{6,86},{7,87},{8,88},{9,... | collective-permute-start | bytes 663560 | tf_op jit(solution)/shard_map/ppermute | solution.py:24
  102.6 3.4 %fusion.28 = (f32[1,1536,144]{1,2,0:T(8,128)}, f32[1,1536,144]{1,2,0:T(8,128)}) fusion(f32[1,1536,144]{1,2,0:T(8,128)S(1)} %copy-done.2, f32[1,1536,144]{1,2,0:T(8,128)S(1)} %copy-done.1, bf16[144,384]{1,0:T(8,128)(2,1)S(1)} %get-tuple-element.59, bf16[144,384]{1,0:T(8,128)(2,1)S(1)} %collective-permute-done.25, bf16[144,384]{1,0:T(8,128)(2,1)S(1)} %slice-done, ...), kind=kOutput, calls=%fused_computation.49 | convolution fusion | flops 684933120 | bytes 3987456 | tf_op jit(solution)/shard_map/dot_general | solution.py:199
  106.1 1.9 %collective-permute-done.18 = bf16[24,4608]{1,0:T(8,128)(2,1)S(1)} collective-permute-done((bf16[24,4608]{1,0:T(8,128)(2,1)S(1)}, bf16[24,4608]{1,0:T(8,128)(2,1)S(1)}, u32[]{:S(2)}, u32[]{:S(2)}) %collective-permute-start.18) | collective-permute-done | bytes 221216 | tf_op jit(solution)/shard_map/ppermute | solution.py:24
  107.9 1.0 collective-permute-done.19
  109.1 4.6 %collective-permute-done.23 = bf16[144,4608]{1,0:T(8,128)(2,1)S(1)} collective-permute-done((bf16[144,4608]{1,0:T(8,128)(2,1)S(1)}, bf16[144,4608]{1,0:T(8,128)(2,1)S(1)}, u32[]{:S(2)}, u32[]{:S(2)}) %collective-permute-start.23) | collective-permute-done | bytes 1327136 | tf_op jit(solution)/shard_map/ppermute | solution.py:24
  113.8 6.3 %collective-permute-start.24 = (bf16[2,12,4608]{2,1,0:T(8,128)(2,1)S(1)}, bf16[2,12,4608]{2,1,0:T(8,128)(2,1)S(1)}, u32[]{:S(2)}, u32[]{:S(2)}) collective-permute-start(bf16[2,12,4608]{2,1,0:T(8,128)(2,1)S(1)} %slice.177), channel_id=1, source_target_pairs={{0,32},{1,33},{2,34},{3,35},{4,36},{5,37},{6,38},{7,39},{8,40},{9,... | collective-permute-start | bytes 663560 | tf_op jit(solution)/shard_map/ppermute | solution.py:24
  120.1 2.9 %fusion.5 = f32[1,144,4608]{2,1,0:T(8,128)} fusion(bf16[384,4608]{1,0:T(8,128)(2,1)S(1)} %constant_dynamic-update-slice_fusion.4, bf16[144,4608]{1,0:T(8,128)(2,1)S(1)} %collective-permute-done.23, bf16[144,4608]{1,0:T(8,128)(2,1)S(1)} %collective-permute-done.22, f32[1,144,4608]{2,1,0:T(8,128)S(1)} %copy-done, s32[]{:T(128)S(6)} %select_n.358), kind=kOutput, calls=%fused_computation.9 | convolution fusion | flops 514252800 | bytes 11698180 | tf_op jit(solution)/shard_map/dot_general | solution.py:178
  123.6 0.9 reshape.349
  (82 shorter events, 5.8 us)
Async XLA Ops:
  3.8 6.6 %collective-permute-start = (bf16[2,12,4608]{2,0,1:T(2,128)(2,1)}, bf16[2,12,4608]{2,0,1:T(2,128)(2,1)S(1)}, u32[]{:S(2)}, u32[]{:S(2)}) collective-permute-start(bf16[2,12,4608]{2,0,1:T(2,128)(2,1)} %bitcast.75), channel_id=1, source_target_pairs={{0,32},{1,33},{2,34},{3,35},{4,36},{5,37},{6,38},{7,39},{8,40},{9,... | collective-permute-start | bytes 663560 | tf_op jit(solution)/shard_map/ppermute | solution.py:24
  7.1 22.9 %collective-permute-start.1 = (bf16[144,4608]{1,0:T(8,128)(2,1)S(1)}, bf16[144,4608]{1,0:T(8,128)(2,1)S(1)}, u32[]{:S(2)}, u32[]{:S(2)}) collective-permute-start(bf16[144,4608]{1,0:T(8,128)(2,1)S(1)} %convert_bitcast_fusion), channel_id=1, source_target_pairs={{0,1},{1,2},{2,3},{3,0},{4,5},{5,6},{6,7},{7,4},{8,9},{9,10},{10,1... | collective-permute-start | bytes 3981320 | tf_op jit(solution)/shard_map/ppermute | solution.py:24
  8.5 21.5 %collective-permute-start.2 = (bf16[144,4608]{1,0:T(8,128)(2,1)S(1)}, bf16[144,4608]{1,0:T(8,128)(2,1)}, u32[]{:S(2)}, u32[]{:S(2)}) collective-permute-start(bf16[144,4608]{1,0:T(8,128)(2,1)S(1)} %convert_bitcast_fusion), channel_id=1, source_target_pairs={{0,3},{1,0},{2,1},{3,2},{4,7},{5,4},{6,5},{7,6},{8,11},{9,8},{10,9... | collective-permute-start | bytes 3981320 | tf_op jit(solution)/shard_map/ppermute | solution.py:24
  10.3 6.2 %copy-start.1 = (f32[1,1536,144]{1,2,0:T(8,128)S(1)}, f32[1,1536,144]{1,2,0:T(8,128)}, u32[]{:S(2)}) copy-start(f32[1,1536,144]{1,2,0:T(8,128)} %param.8) | copy-start | bytes 2654212
  10.4 6.2 %copy-start.2 = (f32[1,1536,144]{1,2,0:T(8,128)S(1)}, f32[1,1536,144]{1,2,0:T(8,128)}, u32[]{:S(2)}) copy-start(f32[1,1536,144]{1,2,0:T(8,128)} %param.9) | copy-start | bytes 2654212
  12.2 6.9 %collective-permute-start.6 = (bf16[24,4608]{1,0:T(8,128)(2,1)S(1)}, bf16[24,4608]{1,0:T(8,128)(2,1)S(1)}, u32[]{:S(2)}, u32[]{:S(2)}) collective-permute-start(bf16[24,4608]{1,0:T(8,128)(2,1)S(1)} %get-tuple-element.22), channel_id=1, source_target_pairs={{0,64},{1,65},{2,66},{3,67},{4,68},{5,69},{6,70},{7,71},{8,72},{9,... | collective-permute-start | bytes 663560 | tf_op jit(solution)/shard_map/ppermute | solution.py:24
  13.5 5.7 %collective-permute-start.7 = (bf16[24,4608]{1,0:T(8,128)(2,1)S(1)}, bf16[24,4608]{1,0:T(8,128)(2,1)S(1)}, u32[]{:S(2)}, u32[]{:S(2)}) collective-permute-start(bf16[24,4608]{1,0:T(8,128)(2,1)S(1)} %get-tuple-element.22), channel_id=1, source_target_pairs={{0,80},{1,81},{2,82},{3,83},{4,84},{5,85},{6,86},{7,87},{8,88},{9,... | collective-permute-start | bytes 663560 | tf_op jit(solution)/shard_map/ppermute | solution.py:24
  15.0 9.9 %collective-permute-start.8 = (bf16[24,4608]{1,0:T(8,128)(2,1)S(1)}, bf16[24,4608]{1,0:T(8,128)(2,1)S(1)}, u32[]{:S(2)}, u32[]{:S(2)}) collective-permute-start(bf16[24,4608]{1,0:T(8,128)(2,1)S(1)} %get-tuple-element.23), channel_id=1, source_target_pairs={{0,16},{1,17},{2,18},{3,19},{4,20},{5,21},{6,22},{7,23},{8,24},{9,... | collective-permute-start | bytes 663560 | tf_op jit(solution)/shard_map/ppermute | solution.py:24
  24.9 21.2 %collective-permute-start.9 = (bf16[96,4608]{1,0:T(8,128)(2,1)S(1)}, bf16[96,4608]{1,0:T(8,128)(2,1)S(1)}, u32[]{:S(2)}, u32[]{:S(2)}) collective-permute-start(bf16[96,4608]{1,0:T(8,128)(2,1)S(1)} %constant_dynamic-update-slice_fusion), channel_id=1, source_target_pairs={{0,4},{1,5},{2,6},{3,7},{4,8},{5,9},{6,10},{7,11},{8,12},{9,13},{1... | collective-permute-start | bytes 2654216 | tf_op jit(solution)/shard_map/ppermute | solution.py:24
  27.8 18.4 %collective-permute-start.10 = (bf16[96,4608]{1,0:T(8,128)(2,1)S(1)}, bf16[96,4608]{1,0:T(8,128)(2,1)S(1)}, u32[]{:S(2)}, u32[]{:S(2)}) collective-permute-start(bf16[96,4608]{1,0:T(8,128)(2,1)S(1)} %constant_dynamic-update-slice_fusion), channel_id=1, source_target_pairs={{0,12},{1,13},{2,14},{3,15},{4,0},{5,1},{6,2},{7,3},{8,4},{9,5},{1... | collective-permute-start | bytes 2654216 | tf_op jit(solution)/shard_map/ppermute | solution.py:24
  30.1 30.2 %collective-permute-start.3 = (bf16[144,3456]{1,0:T(8,128)(2,1)S(1)}, bf16[144,3456]{1,0:T(8,128)(2,1)S(1)}, u32[]{:S(2)}, u32[]{:S(2)}) collective-permute-start(bf16[144,3456]{1,0:T(8,128)(2,1)S(1)} %pad_maximum_fusion.2), channel_id=1, source_target_pairs={{0,1},{1,2},{2,3},{3,0},{4,5},{5,6},{6,7},{7,4},{8,9},{9,10},{10,1... | collective-permute-start | bytes 2985992 | tf_op jit(solution)/shard_map/ppermute | solution.py:24
  31.4 29.0 %collective-permute-start.4 = (bf16[144,3456]{1,0:T(8,128)(2,1)S(1)}, bf16[144,3456]{1,0:T(8,128)(2,1)S(1)}, u32[]{:S(2)}, u32[]{:S(2)}) collective-permute-start(bf16[144,3456]{1,0:T(8,128)(2,1)S(1)} %pad_maximum_fusion.3), channel_id=1, source_target_pairs={{0,3},{1,0},{2,1},{3,2},{4,7},{5,4},{6,5},{7,6},{8,11},{9,8},{10,9... | collective-permute-start | bytes 2985992 | tf_op jit(solution)/shard_map/ppermute | solution.py:24
  34.2 28.8 %collective-permute-start.5 = (bf16[144,1152]{1,0:T(8,128)(2,1)S(1)}, bf16[144,1152]{1,0:T(8,128)(2,1)S(1)}, u32[]{:S(2)}, u32[]{:S(2)}) collective-permute-start(bf16[144,1152]{1,0:T(8,128)(2,1)S(1)} %pad_maximum_fusion.9), channel_id=1, source_target_pairs={{0,2},{1,3},{2,0},{3,1},{4,6},{5,7},{6,4},{7,5},{8,10},{9,11},{10,... | collective-permute-start | bytes 995336 | tf_op jit(solution)/shard_map/ppermute | solution.py:24
  46.1 10.9 %collective-permute-start.11 = (bf16[96,2304]{1,0:T(8,128)(2,1)S(1)}, bf16[96,2304]{1,0:T(8,128)(2,1)S(1)}, u32[]{:S(2)}, u32[]{:S(2)}) collective-permute-start(bf16[96,2304]{1,0:T(8,128)(2,1)S(1)} %slice.191), channel_id=1, source_target_pairs={{0,4},{1,5},{2,6},{3,7},{4,8},{5,9},{6,10},{7,11},{8,12},{9,13},{1... | collective-permute-start | bytes 1327112 | tf_op jit(solution)/shard_map/ppermute | solution.py:24
  46.2 12.7 %collective-permute-start.12 = (bf16[96,2304]{1,0:T(8,128)(2,1)S(1)}, bf16[96,2304]{1,0:T(8,128)(2,1)S(1)}, u32[]{:S(2)}, u32[]{:S(2)}) collective-permute-start(bf16[96,2304]{1,0:T(8,128)(2,1)S(1)} %slice.192), channel_id=1, source_target_pairs={{0,12},{1,13},{2,14},{3,15},{4,0},{5,1},{6,2},{7,3},{8,4},{9,5},{1... | collective-permute-start | bytes 1327112 | tf_op jit(solution)/shard_map/ppermute | solution.py:24
  67.3 9.5 %collective-permute-start.13 = (bf16[96,2304]{1,0:T(8,128)(2,1)S(1)}, bf16[96,2304]{1,0:T(8,128)(2,1)S(1)}, u32[]{:S(2)}, u32[]{:S(2)}) collective-permute-start(bf16[96,2304]{1,0:T(8,128)(2,1)S(1)} %convolution_convert_fusion.3), channel_id=1, source_target_pairs={{0,4},{1,5},{2,6},{3,7},{4,8},{5,9},{6,10},{7,11},{8,12},{9,13},{1... | collective-permute-start | bytes 1327112 | tf_op jit(solution)/shard_map/ppermute | solution.py:24
  68.2 17.7 %collective-permute-start.21 = (bf16[144,2688]{1,0:T(8,128)(2,1)S(1)}, bf16[144,2688]{1,0:T(8,128)(2,1)S(1)}, u32[]{:S(2)}, u32[]{:S(2)}) collective-permute-start(bf16[144,2688]{1,0:T(8,128)(2,1)S(1)} %pad_maximum_fusion.5), channel_id=1, source_target_pairs={{0,3},{1,0},{2,1},{3,2},{4,7},{5,4},{6,5},{7,6},{8,11},{9,8},{10,9... | collective-permute-start | bytes 2322440 | tf_op jit(solution)/shard_map/ppermute | solution.py:24
  69.2 11.1 %collective-permute-start.15 = (bf16[96,2304]{1,0:T(8,128)(2,1)S(1)}, bf16[96,2304]{1,0:T(8,128)(2,1)S(1)}, u32[]{:S(2)}, u32[]{:S(2)}) collective-permute-start(bf16[96,2304]{1,0:T(8,128)(2,1)S(1)} %convolution_convert_fusion.2), channel_id=1, source_target_pairs={{0,12},{1,13},{2,14},{3,15},{4,0},{5,1},{6,2},{7,3},{8,4},{9,5},{1... | collective-permute-start | bytes 1327112 | tf_op jit(solution)/shard_map/ppermute | solution.py:24
  72.7 13.8 %collective-permute-start.20 = (bf16[144,2688]{1,0:T(8,128)(2,1)S(1)}, bf16[144,2688]{1,0:T(8,128)(2,1)S(1)}, u32[]{:S(2)}, u32[]{:S(2)}) collective-permute-start(bf16[144,2688]{1,0:T(8,128)(2,1)S(1)} %pad_maximum_fusion.4), channel_id=1, source_target_pairs={{0,1},{1,2},{2,3},{3,0},{4,5},{5,6},{6,7},{7,4},{8,9},{9,10},{10,1... | collective-permute-start | bytes 2322440 | tf_op jit(solution)/shard_map/ppermute | solution.py:24
  78.0 20.9 %collective-permute-start.14 = (bf16[96,4608]{1,0:T(8,128)(2,1)S(1)}, bf16[96,4608]{1,0:T(8,128)(2,1)S(1)}, u32[]{:S(2)}, u32[]{:S(2)}) collective-permute-start(bf16[96,4608]{1,0:T(8,128)(2,1)S(1)} %add_convert_fusion.1), channel_id=1, source_target_pairs={{0,4},{1,5},{2,6},{3,7},{4,8},{5,9},{6,10},{7,11},{8,12},{9,13},{1... | collective-permute-start | bytes 2654216 | tf_op jit(solution)/shard_map/ppermute | solution.py:24
  81.5 17.4 %collective-permute-start.16 = (bf16[96,4608]{1,0:T(8,128)(2,1)S(1)}, bf16[96,4608]{1,0:T(8,128)(2,1)S(1)}, u32[]{:S(2)}, u32[]{:S(2)}) collective-permute-start(bf16[96,4608]{1,0:T(8,128)(2,1)S(1)} %add_convert_fusion), channel_id=1, source_target_pairs={{0,12},{1,13},{2,14},{3,15},{4,0},{5,1},{6,2},{7,3},{8,4},{9,5},{1... | collective-permute-start | bytes 2654216 | tf_op jit(solution)/shard_map/ppermute | solution.py:24
  85.9 2.2 %copy-start.3 = (bf16[144,2688]{1,0:T(8,128)(2,1)}, bf16[144,2688]{1,0:T(8,128)(2,1)S(1)}, u32[]{:S(2)}) copy-start(bf16[144,2688]{1,0:T(8,128)(2,1)S(1)} %collective-permute-done.21) | copy-start | bytes 2322436
  86.6 1.6 %copy-start.4 = (bf16[144,2688]{1,0:T(8,128)(2,1)}, bf16[144,2688]{1,0:T(8,128)(2,1)S(1)}, u32[]{:S(2)}) copy-start(bf16[144,2688]{1,0:T(8,128)(2,1)S(1)} %collective-permute-done.20) | copy-start | bytes 2322436
  86.7 15.9 %collective-permute-start.25 = (bf16[144,384]{1,0:T(8,128)(2,1)S(1)}, bf16[144,384]{1,0:T(8,128)(2,1)S(1)}, u32[]{:S(2)}, u32[]{:S(2)}) collective-permute-start(bf16[144,384]{1,0:T(8,128)(2,1)S(1)} %get-tuple-element.29), channel_id=1, source_target_pairs={{0,2},{1,3},{2,0},{3,1},{4,6},{5,7},{6,4},{7,5},{8,10},{9,11},{10,... | collective-permute-start | bytes 331784 | tf_op jit(solution)/shard_map/ppermute | solution.py:24
  88.1 25.5 %collective-permute-start.23 = (bf16[144,4608]{1,0:T(8,128)(2,1)S(1)}, bf16[144,4608]{1,0:T(8,128)(2,1)S(1)}, u32[]{:S(2)}, u32[]{:S(2)}) collective-permute-start(bf16[144,4608]{1,0:T(8,128)(2,1)S(1)} %fusion.7), channel_id=1, source_target_pairs={{0,3},{1,0},{2,1},{3,2},{4,7},{5,4},{6,5},{7,6},{8,11},{9,8},{10,9... | collective-permute-start | bytes 3981320 | tf_op jit(solution)/shard_map/ppermute | solution.py:24
  92.2 10.4 %slice-start = ((bf16[144,2688]{1,0:T(8,128)(2,1)}), bf16[144,384]{1,0:T(8,128)(2,1)S(1)}, s32[]{:S(2)}) async-start(bf16[144,2688]{1,0:T(8,128)(2,1)} %copy-done.3), calls=%async_computation | async-start | bytes 221184 | tf_op jit(solution)/shard_map/slice | solution.py:81
  92.2 10.4 %slice-start.1 = ((bf16[144,2688]{1,0:T(8,128)(2,1)}), bf16[144,384]{1,0:T(8,128)(2,1)S(1)}, s32[]{:S(2)}) async-start(bf16[144,2688]{1,0:T(8,128)(2,1)} %copy-done.4), calls=%async_computation.1 | async-start | bytes 221184 | tf_op jit(solution)/shard_map/slice | solution.py:81
  92.2 21.5 %collective-permute-start.22 = (bf16[144,4608]{1,0:T(8,128)(2,1)S(1)}, bf16[144,4608]{1,0:T(8,128)(2,1)S(1)}, u32[]{:S(2)}, u32[]{:S(2)}) collective-permute-start(bf16[144,4608]{1,0:T(8,128)(2,1)S(1)} %fusion.6), channel_id=1, source_target_pairs={{0,1},{1,2},{2,3},{3,0},{4,5},{5,6},{6,7},{7,4},{8,9},{9,10},{10,1... | collective-permute-start | bytes 3981320 | tf_op jit(solution)/shard_map/ppermute | solution.py:24
  99.2 6.8 %collective-permute-start.17 = (bf16[24,4608]{1,0:T(8,128)(2,1)S(1)}, bf16[24,4608]{1,0:T(8,128)(2,1)S(1)}, u32[]{:S(2)}, u32[]{:S(2)}) collective-permute-start(bf16[24,4608]{1,0:T(8,128)(2,1)S(1)} %get-tuple-element.54), channel_id=1, source_target_pairs={{0,16},{1,17},{2,18},{3,19},{4,20},{5,21},{6,22},{7,23},{8,24},{9,... | collective-permute-start | bytes 663560 | tf_op jit(solution)/shard_map/ppermute | solution.py:24
  100.4 7.6 %collective-permute-start.18 = (bf16[24,4608]{1,0:T(8,128)(2,1)S(1)}, bf16[24,4608]{1,0:T(8,128)(2,1)S(1)}, u32[]{:S(2)}, u32[]{:S(2)}) collective-permute-start(bf16[24,4608]{1,0:T(8,128)(2,1)S(1)} %get-tuple-element.56), channel_id=1, source_target_pairs={{0,80},{1,81},{2,82},{3,83},{4,84},{5,85},{6,86},{7,87},{8,88},{9,... | collective-permute-start | bytes 663560 | tf_op jit(solution)/shard_map/ppermute | solution.py:24
  102.6 6.3 %collective-permute-start.19 = (bf16[24,4608]{1,0:T(8,128)(2,1)S(1)}, bf16[24,4608]{1,0:T(8,128)(2,1)S(1)}, u32[]{:S(2)}, u32[]{:S(2)}) collective-permute-start(bf16[24,4608]{1,0:T(8,128)(2,1)S(1)} %get-tuple-element.55), channel_id=1, source_target_pairs={{0,64},{1,65},{2,66},{3,67},{4,68},{5,69},{6,70},{7,71},{8,72},{9,... | collective-permute-start | bytes 663560 | tf_op jit(solution)/shard_map/ppermute | solution.py:24
  106.0 14.1 %copy-start = (f32[1,144,4608]{2,1,0:T(8,128)S(1)}, f32[1,144,4608]{2,1,0:T(8,128)}, u32[]{:S(2)}) copy-start(f32[1,144,4608]{2,1,0:T(8,128)} %param.7) | copy-start | bytes 7962628
  113.8 9.3 %collective-permute-start.24 = (bf16[2,12,4608]{2,1,0:T(8,128)(2,1)S(1)}, bf16[2,12,4608]{2,1,0:T(8,128)(2,1)S(1)}, u32[]{:S(2)}, u32[]{:S(2)}) collective-permute-start(bf16[2,12,4608]{2,1,0:T(8,128)(2,1)S(1)} %slice.177), channel_id=1, source_target_pairs={{0,32},{1,33},{2,34},{3,35},{4,36},{5,37},{6,38},{7,39},{8,40},{9,... | collective-permute-start | bytes 663560 | tf_op jit(solution)/shard_map/ppermute | solution.py:24
